TPU v7x, 32 devices: a whole 2x2x4 slice. The times are simulated.
32 devices in a mesh: dp: 16 (over z, y, core), strip: 2 (over x).
Axes of the slice: x: 2, y: 2, z: 4, core: 2. Of those that a mesh axis runs over, the one named last changes fastest.
Arguments:
- low_tokens: bfloat16 [64, 576, 1024], P('dp', 'strip'), may hold values from -6 to 6
- high_map: bfloat16 [64, 32, 32, 1536], P('dp', 'strip'), may hold values from -6 to 6
- counts: int32 [16], P('dp'), may hold values from 1 to 4, as said below
- row_edges: int32 [25], replicated, may hold values from 0 to 32, as said below
- col_edges: int32 [25], replicated, may hold values from 0 to 32, as said below
- w_qkv: bfloat16 [1024, 3072], replicated, may hold values from -0.1875 to 0.1875
- w_attn_out: bfloat16 [1024, 1024], replicated, may hold values from -1.5 to 1.5
- w_fc1: bfloat16 [1024, 4096], replicated, may hold values from -0.1875 to 0.1875
- w_fc2: bfloat16 [4096, 1024], replicated, may hold values from -0.09375 to 0.09375
- vit_gains: float32 [2, 1024], replicated, may hold values from 0.5 to 1.5
- vit_shifts: float32 [2, 1024], replicated, may hold values from -3 to 3
- w_pw1: bfloat16 [1536, 6144], replicated, may hold values from -0.15625 to 0.15625
- w_pw2: bfloat16 [6144, 1536], replicated, may hold values from -0.078125 to 0.078125
- w_pool: bfloat16 [1536, 1024], replicated, may hold values from -0.15625 to 0.15625
- dw_kernel: float32 [49, 1536], replicated, may hold values from -0.875 to 0.875
- conv_gains: float32 [2, 1536], replicated, may hold values from 0.5 to 1.5
- conv_shifts: float32 [2, 1536], replicated, may hold values from -3 to 3
- w_gate: float32 [1536], replicated, may hold values from -0.15625 to 0.15625
- d_merged: bfloat16 [64, 576, 1024], P('dp', 'strip'), may hold values from -6 to 6
- d_conv: bfloat16 [64, 32, 32, 1536], P('dp', 'strip'), may hold values from -6 to 6
Outputs:
- merged: bfloat16 [64, 576, 1024], P('dp', 'strip')
- conv_out: bfloat16 [64, 32, 32, 1536], P('dp', 'strip')
- grad_tokens: bfloat16 [64, 576, 1024], P('dp', 'strip')
- grad_map: bfloat16 [64, 32, 32, 1536], P('dp', 'strip')
- vit_grads: float32 [12587008], P(('dp', 'strip'))
- conv_grads: float32 [20530176], P(('dp', 'strip'))
Inputs may be any that keep to these rules, and one draw needn't show every extreme that they name: `counts`: some sample has 4 live images and some has 1; most have 1 or 2. `row_edges`: starts at 0, ends at 32, consecutive entries differ by 1 or 2; where the row strips of the strip axis meet, the entry of the first bin of a strip's token rows differs by exactly one from the first map row of that strip, with the same sign at every such boundary. `col_edges`: starts at 0, ends at 32, consecutive entries differ by 1 or 2.
All inputs are finite; a program needn't handle non-finite values.
Results may differ from a plain program's by a relative error of at most 0.013.
Values may be sent and summed in bfloat16 or wider, within the bound.
No kernel may reach another device: no remote copies, remote signals or barrier semaphores. Data moves between devices by JAX's collectives and lax.ppermute only.
A program may use at most 640 MiB of HBM per device.

v0:
```python
import math

import jax
import jax.numpy as jnp
from jax import lax
from jax.sharding import PartitionSpec as P

HEADS = 16
KS = 7


exact_mode = lax.Precision.HIGHEST
EPSILON = 1e-05


def extended(cells, sides, width):
    for axis, dim in sides:
        count = lax.axis_size(axis)
        ends = count - 1
        head = lax.slice_in_dim(cells, 0, width, axis=dim)
        tail = lax.slice_in_dim(cells, cells.shape[dim] - width, cells.shape[dim], axis=dim)
        cells = jnp.concatenate(
            [
                lax.ppermute(tail, axis, [(i, (i + 1) % count) for i in range(ends)]),
                cells,
                lax.ppermute(head, axis, [((i + 1) % count, i) for i in range(ends)]),
            ],
            axis=dim,
        )
    return cells


def normed(values, gain, shift):
    center = values - jnp.mean(values, axis=-1, keepdims=True)
    spread = jnp.mean(center * center, axis=-1, keepdims=True)
    return center * lax.rsqrt(spread + EPSILON) * gain + shift


def bin_weights(edges, cell_count):
    cells = jnp.arange(cell_count, dtype=jnp.int32)
    inside = (cells[None, :] >= edges[:-1, None]) & (cells[None, :] < edges[1:, None])
    widths = (edges[1:] - edges[:-1]).astype(jnp.float32)
    return inside.astype(jnp.float32) / widths[:, None]


def strip_bins(edges, first_bin, bin_count, first_cell, cell_count):
    padded = jnp.concatenate([edges[:1], edges, edges[-1:]])
    window = lax.dynamic_slice_in_dim(padded, first_bin + 1, bin_count + 1)
    cells = first_cell + jnp.arange(cell_count, dtype=jnp.int32)
    inside = (cells[None, :] >= window[:-1, None]) & (cells[None, :] < window[1:, None])
    widths = jnp.maximum(window[1:] - window[:-1], 1).astype(jnp.float32)
    return inside.astype(jnp.float32) / widths[:, None]


def depthwise(framed, kernel, row_count, col_count, flipped):
    total = jnp.zeros(framed.shape[:1] + (row_count, col_count) + framed.shape[3:], jnp.float32)
    for tap_row in range(KS):
        for tap_col in range(KS):
            top = KS - 1 - tap_row if flipped else tap_row
            left = KS - 1 - tap_col if flipped else tap_col
            total = (
                total
                + kernel[tap_row * KS + tap_col]
                * framed[:, top : top + row_count, left : left + col_count, :]
            )
    return total


def per_device(
    low_tokens,
    high_map,
    counts,
    row_edges,
    col_edges,
    w_qkv,
    w_attn_out,
    w_fc1,
    w_fc2,
    vit_gains,
    vit_shifts,
    w_pw1,
    w_pw2,
    w_pool,
    dw_kernel,
    conv_gains,
    conv_shifts,
    w_gate,
    d_merged,
    d_conv,
):
    slot_count, tok_rows, model_width = low_tokens.shape
    row_count, col_count, channels = (high_map.shape[1], high_map.shape[2], high_map.shape[3])
    per_sample = slot_count // counts.shape[0]
    head_size = model_width // HEADS
    score_scale = 1.0 / math.sqrt(head_size)
    kernel_reach = KS // 2
    strip_index = lax.axis_index("strip")
    live_mask = (
        (jnp.arange(per_sample, dtype=jnp.int32)[None, :] < counts[:, None])
        .astype(jnp.float32)
        .reshape(slot_count)
    )
    token_mask = live_mask[:, None, None]
    map_mask = live_mask[:, None, None, None]
    tokens = low_tokens.astype(jnp.float32)
    normed_in, first_back = jax.vjp(normed, tokens, vit_gains[0], vit_shifts[0])
    normed_low = normed_in.astype(jnp.bfloat16)
    qkv_low = jnp.einsum(
        "itd,de->ite", normed_low, w_qkv, preferred_element_type=jnp.float32
    ).astype(jnp.bfloat16)
    query = qkv_low[..., :model_width].reshape(slot_count, tok_rows, HEADS, head_size)
    all_kv = lax.all_gather(qkv_low[..., model_width:], "strip", axis=1, tiled=True)
    key_heads = all_kv[..., :model_width].reshape(slot_count, -1, HEADS, head_size)
    value_heads = all_kv[..., model_width:].reshape(slot_count, -1, HEADS, head_size)
    scores = (
        jnp.einsum("ithe,iuhe->ihtu", query, key_heads, preferred_element_type=jnp.float32)
        * score_scale
    )
    probs = jax.nn.softmax(scores, axis=-1)
    probs_low = probs.astype(jnp.bfloat16)
    mixed_low = (
        jnp.einsum("ihtu,iuhe->ithe", probs_low, value_heads, preferred_element_type=jnp.float32)
        .reshape(slot_count, tok_rows, model_width)
        .astype(jnp.bfloat16)
    )
    residual = tokens + jnp.einsum(
        "itd,de->ite", mixed_low, w_attn_out, preferred_element_type=jnp.float32
    )
    inner, inner_back = jax.vjp(normed, residual, vit_gains[1], vit_shifts[1])
    inner_low = inner.astype(jnp.bfloat16)
    mlp_pre = jnp.einsum("itd,df->itf", inner_low, w_fc1, preferred_element_type=jnp.float32)
    mlp_act, mlp_back = jax.vjp(jax.nn.gelu, mlp_pre)
    mlp_low = mlp_act.astype(jnp.bfloat16)
    low_out = residual + jnp.einsum(
        "itf,fd->itd", mlp_low, w_fc2, preferred_element_type=jnp.float32
    )
    high_in = high_map.astype(jnp.float32)
    framed = extended(high_map, (("strip", 1),), kernel_reach).astype(jnp.float32)
    framed = jnp.pad(framed, ((0, 0), (0, 0), (kernel_reach, kernel_reach), (0, 0)))
    conv_mid = conv_shifts[0] + depthwise(framed, dw_kernel, row_count, col_count, False)
    spatial, spatial_back = jax.vjp(normed, conv_mid, conv_gains[0], conv_shifts[1])
    spatial_low = spatial.astype(jnp.bfloat16)
    expand_pre = jnp.einsum("iyxc,cf->iyxf", spatial_low, w_pw1, preferred_element_type=jnp.float32)
    expand_act, expand_back = jax.vjp(jax.nn.gelu, expand_pre)
    expand_low = expand_act.astype(jnp.bfloat16)
    branch = jnp.einsum("iyxf,fc->iyxc", expand_low, w_pw2, preferred_element_type=jnp.float32)
    high_out = high_in + conv_gains[1] * branch
    col_bins = bin_weights(col_edges, col_count)
    grid_side = col_bins.shape[0]
    own_bins = tok_rows // grid_side
    first_own = strip_index * own_bins
    near_bins = strip_bins(
        row_edges, first_own - 1, own_bins + 2, strip_index * row_count, row_count
    )
    partial_value = jnp.einsum(
        "by,iyxc,ax->ibac", near_bins, high_out, col_bins, precision=exact_mode
    )
    framed_bins = extended(partial_value.astype(jnp.bfloat16), (("strip", 1),), 1).astype(
        partial_value.dtype
    )
    pooled_rows = framed_bins[:, 2 : own_bins + 2]
    pooled_rows = pooled_rows.at[:, 0].add(framed_bins[:, 0])
    pooled_rows = pooled_rows.at[:, own_bins - 1].add(framed_bins[:, own_bins + 3])
    pooled = pooled_rows.reshape(slot_count, tok_rows, channels)
    pooled_low = pooled.astype(jnp.bfloat16)
    pooled_wide = pooled_low.astype(jnp.float32)
    lifted = jnp.einsum("itc,cd->itd", pooled_low, w_pool, preferred_element_type=jnp.float32)
    gate_value = jax.nn.sigmoid(jnp.sum(pooled_wide * w_gate, axis=-1, keepdims=True))
    merged = token_mask * (low_out + gate_value * lifted)
    conv_out = map_mask * high_out
    d_top = d_merged.astype(jnp.float32) * token_mask
    d_high = d_conv.astype(jnp.float32) * map_mask
    d_logit = jnp.sum(d_top * lifted, axis=-1, keepdims=True) * gate_value * (1.0 - gate_value)
    d_lifted = (gate_value * d_top).astype(jnp.bfloat16)
    grad_gate = jnp.sum(d_logit * pooled_wide, axis=(0, 1))
    grad_pool = jnp.einsum("itc,itd->cd", pooled_low, d_lifted, preferred_element_type=jnp.float32)
    d_pooled = (
        jnp.einsum("itd,cd->itc", d_lifted, w_pool, preferred_element_type=jnp.float32)
        + d_logit * w_gate
    ).astype(jnp.bfloat16)
    pooled_near = extended(
        d_pooled.reshape(slot_count, own_bins, grid_side, channels), (("strip", 1),), 1
    )
    d_post = d_high + jnp.einsum(
        "by,ibac,ax->iyxc",
        near_bins.astype(jnp.bfloat16),
        pooled_near,
        col_bins.astype(jnp.bfloat16),
        preferred_element_type=jnp.float32,
    )
    grad_scale = jnp.sum(d_post * branch, axis=(0, 1, 2))
    d_branch = (conv_gains[1] * d_post).astype(jnp.bfloat16)
    grad_pw2 = jnp.einsum("iyxf,iyxc->fc", expand_low, d_branch, preferred_element_type=jnp.float32)
    d_expand = expand_back(
        jnp.einsum("iyxc,fc->iyxf", d_branch, w_pw2, preferred_element_type=jnp.float32)
    )[0].astype(jnp.bfloat16)
    grad_pw1 = jnp.einsum(
        "iyxc,iyxf->cf", spatial_low, d_expand, preferred_element_type=jnp.float32
    )
    d_spatial = jnp.einsum("iyxf,cf->iyxc", d_expand, w_pw1, preferred_element_type=jnp.float32)
    d_conv_in, grad_conv_gain, grad_conv_shift = spatial_back(d_spatial)
    grad_bias = jnp.sum(d_conv_in, axis=(0, 1, 2))
    kernel_rows = []
    for tap_row in range(KS):
        for tap_col in range(KS):
            kernel_rows.append(
                jnp.sum(
                    framed[:, tap_row : tap_row + row_count, tap_col : tap_col + col_count, :]
                    * d_conv_in,
                    axis=(0, 1, 2),
                )
            )
    grad_kernel = jnp.stack(kernel_rows)
    d_rim = extended(d_conv_in.astype(jnp.bfloat16), (("strip", 1),), kernel_reach).astype(
        d_conv_in.dtype
    )
    d_rim = jnp.pad(d_rim, ((0, 0), (0, 0), (kernel_reach, kernel_reach), (0, 0)))
    grad_map = (d_post + depthwise(d_rim, dw_kernel, row_count, col_count, True)).astype(
        jnp.bfloat16
    )
    d_mlp = d_top.astype(jnp.bfloat16)
    grad_fc2 = jnp.einsum("itf,itd->fd", mlp_low, d_mlp, preferred_element_type=jnp.float32)
    d_fc = mlp_back(jnp.einsum("itd,fd->itf", d_mlp, w_fc2, preferred_element_type=jnp.float32))[
        0
    ].astype(jnp.bfloat16)
    grad_fc1 = jnp.einsum("itd,itf->df", inner_low, d_fc, preferred_element_type=jnp.float32)
    d_inner = jnp.einsum("itf,df->itd", d_fc, w_fc1, preferred_element_type=jnp.float32)
    d_res_norm, grad_gain_b, grad_shift_b = inner_back(d_inner)
    d_residual = d_top + d_res_norm
    d_attn = d_residual.astype(jnp.bfloat16)
    grad_out = jnp.einsum("itd,ite->de", mixed_low, d_attn, preferred_element_type=jnp.float32)
    d_mixed = jnp.einsum(
        "ite,de->itd", d_attn, w_attn_out, preferred_element_type=jnp.float32
    ).astype(jnp.bfloat16)
    d_heads = d_mixed.reshape(slot_count, tok_rows, HEADS, head_size)
    d_probs = jnp.einsum(
        "ithe,iuhe->ihtu", d_heads, value_heads, preferred_element_type=jnp.float32
    )
    d_scores = (probs * (d_probs - jnp.sum(d_probs * probs, axis=-1, keepdims=True))).astype(
        jnp.bfloat16
    )
    d_query = (
        jnp.einsum("ihtu,iuhe->ithe", d_scores, key_heads, preferred_element_type=jnp.float32)
        * score_scale
    )
    d_keys = (
        jnp.einsum("ihtu,ithe->iuhe", d_scores, query, preferred_element_type=jnp.float32)
        * score_scale
    )
    d_values = jnp.einsum("ihtu,ithe->iuhe", probs_low, d_heads, preferred_element_type=jnp.float32)
    d_kv = jnp.concatenate(
        [
            d_keys.reshape(slot_count, -1, model_width),
            d_values.reshape(slot_count, -1, model_width),
        ],
        axis=-1,
    )
    d_kv = lax.psum_scatter(
        d_kv.astype(jnp.bfloat16), "strip", scatter_dimension=1, tiled=True
    ).astype(jnp.float32)
    d_qkv = jnp.concatenate(
        [d_query.reshape(slot_count, tok_rows, model_width), d_kv], axis=-1
    ).astype(jnp.bfloat16)
    grad_qkv = jnp.einsum("itd,ite->de", normed_low, d_qkv, preferred_element_type=jnp.float32)
    d_normed = jnp.einsum("ite,de->itd", d_qkv, w_qkv, preferred_element_type=jnp.float32)
    d_tok_norm, grad_gain_a, grad_shift_a = first_back(d_normed)
    grad_tokens = (d_residual + d_tok_norm).astype(jnp.bfloat16)
    vit_flat = jnp.concatenate(
        [
            grad_qkv.reshape(-1),
            grad_out.reshape(-1),
            grad_fc1.reshape(-1),
            grad_fc2.reshape(-1),
            jnp.stack([grad_gain_a, grad_gain_b]).reshape(-1),
            jnp.stack([grad_shift_a, grad_shift_b]).reshape(-1),
        ]
    )
    conv_flat = jnp.concatenate(
        [
            grad_pw1.reshape(-1),
            grad_pw2.reshape(-1),
            grad_pool.reshape(-1),
            grad_kernel.reshape(-1),
            jnp.stack([grad_conv_gain, grad_scale]).reshape(-1),
            jnp.stack([grad_bias, grad_conv_shift]).reshape(-1),
            grad_gate,
        ]
    )
    data_count = lax.axis_size("dp")
    strip_count = lax.axis_size("strip")
    vit_blocks = vit_flat.reshape(data_count, strip_count, -1)
    conv_blocks = conv_flat.reshape(data_count, strip_count, -1)
    vit_recv, conv_recv = (
        lax.all_to_all(
            vit_blocks.astype(jnp.bfloat16), "dp", split_axis=0, concat_axis=0, tiled=True
        ).astype(vit_blocks.dtype),
        lax.all_to_all(
            conv_blocks.astype(jnp.bfloat16), "dp", split_axis=0, concat_axis=0, tiled=True
        ).astype(conv_blocks.dtype),
    )
    vit_part = jnp.sum(vit_recv, axis=0)
    conv_part = jnp.sum(conv_recv, axis=0)
    vit_sum, conv_sum = (
        lax.psum_scatter(
            vit_part.astype(jnp.bfloat16), "strip", scatter_dimension=0, tiled=True
        ).astype(jnp.float32),
        lax.psum_scatter(
            conv_part.astype(jnp.bfloat16), "strip", scatter_dimension=0, tiled=True
        ).astype(jnp.float32),
    )
    return (
        merged.astype(jnp.bfloat16),
        conv_out.astype(jnp.bfloat16),
        grad_tokens,
        grad_map,
        vit_sum.reshape(-1),
        conv_sum.reshape(-1),
    )


def solution(mesh):
    in_specs = (
        P("dp", "strip", None),
        P("dp", "strip", None, None),
        P("dp"),
        P(),
        P(),
        P(),
        P(),
        P(),
        P(),
        P(),
        P(),
        P(),
        P(),
        P(),
        P(),
        P(),
        P(),
        P(),
        P("dp", "strip", None),
        P("dp", "strip", None, None),
    )
    out_specs = (
        P("dp", "strip", None),
        P("dp", "strip", None, None),
        P("dp", "strip", None),
        P("dp", "strip", None, None),
        P(("dp", "strip")),
        P(("dp", "strip")),
    )
    return jax.shard_map(
        per_device, mesh=mesh, in_specs=in_specs, out_specs=out_specs, check_vma=False
    )
```

profile of v0, /device:TPU:13, one launch (start us, length us, event | category | flops | bytes accessed | tf_op | source)
XLA Modules:
  0.0 3073.1 jit_solution(3139895337916146759)
XLA Ops:
  23.5 11.2 fusion.153
  56.7 9.9 maximum_convert_fusion
  67.0 297.4 %fusion.240 = (f32[4,16,32]{2,1,0:T(8,128)S(1)}, f32[4,16,32,1536]{3,2,1,0:T(8,128)}) fusion(f32[1536]{0:T(1024)S(1)} %get-tuple-element.194, f32[1536]{0:T(1024)S(1)} %get-tuple-element.193, f32[1536]{0:T(1024)S(1)} %get-tuple-element.92, f32[4,22,32,1536]{3,2,1,0:T(8,128)} %maximum_convert_fusion, f32[1536]{0:T(1024)S(1)} %get-tuple-element.93, ...), kind=kLoop, calls=%fused_computation.503 | loop fusion | flops 311425024 | bytes 118302720 | tf_op jit(solution)/shard_map/jvp()/reduce_sum | solution.py:34
  371.6 50.1 %fusion.23 = f32[4,16,32,6144]{3,2,1,0:T(8,128)} fusion(bf16[1536,6144]{1,0:T(8,128)(2,1)} %param.35, f32[4,16,32,1536]{3,2,1,0:T(8,128)} %get-tuple-element.152, f32[1536]{0:T(1024)} %get-tuple-element.142, f32[1536]{0:T(1024)S(1)} %get-tuple-element.141, f32[4,16,32]{2,1,0:T(8,128)S(1)} %fusion.206, f32[4,16,32]{2,1,0:T(8,128)S(1)} %broadcast_multiply_fusion), kind=kOutput, calls=%fused_computation.117 | convolution fusion | flops 38670434304 | bytes 81817600 | tf_op jit(solution)/shard_map/iyxc,cf->iyxf/dot_general | solution.py:143
  445.7 22.7 fusion.251
  468.5 20.5 fusion.185
  496.2 16.4 fusion.138
  512.6 27.4 fusion.20
  540.0 18.6 multiply_reduce_fusion.55
  575.0 19.4 fusion.177
  594.4 32.2 %multiply_reduce_fusion = (f32[4,16,288]{2,1,0:T(8,128)S(1)}, f32[4,16,288,576]{3,2,1,0:T(8,128)}) fusion(f32[4,16,288,576]{3,2,1,0:T(8,128)} %get-tuple-element.183, f32[4,16,288]{2,1,0:T(8,128)S(1)} %get-tuple-element.182, bf16[4,288,16,64]{1,3,2,0:T(8,128)(2,1)} %bitcast.216, bf16[4,576,16,64]{1,3,2,0:T(8,128)(2,1)} %bitcast.209), kind=kOutput, calls=%fused_computation.96 | convolution fusion | flops 1390786560 | bytes 92160000 | tf_op jit(solution)/shard_map/ithe,iuhe->ihtu/dot_general | solution.py:236
  634.4 37.8 %multiply_convert_fusion.1 = bf16[4,16,288,576]{3,2,1,0:T(8,128)(2,1)} fusion(f32[4,16,288,576]{3,2,1,0:T(8,128)} %get-tuple-element.188, f32[4,16,288]{2,1,0:T(8,128)S(1)} %get-tuple-element.187, f32[4,16,288,576]{3,2,1,0:T(8,128)} %get-tuple-element.183, f32[4,16,288]{2,1,0:T(8,128)S(1)} %get-tuple-element.182), kind=kLoop, calls=%fused_computation.95 | loop fusion | flops 42467328 | bytes 106315776 | tf_op jit(solution)/shard_map/convert_element_type | solution.py:239
  672.2 15.7 multiply_convert_fusion.5
  695.9 9.2 pad_maximum_fusion
  705.2 54.1 %fusion.26 = f32[4,16,32,1536]{3,2,1,0:T(8,128)} fusion(bf16[6144,1536]{1,0:T(8,128)(2,1)} %param.36, f32[4,16,32,6144]{3,2,1,0:T(8,128)} %fusion.23), kind=kOutput, calls=%fused_computation.120 | convolution fusion | flops 38767951872 | bytes 81788928 | tf_op jit(solution)/shard_map/iyxf,fc->iyxc/dot_general | solution.py:146
  759.3 12.6 fusion.141
  771.9 14.7 convert_bitcast_fusion
  795.2 11.4 collective-permute-done.3
  819.9 9.5 scatter-add.6
  834.2 9.4 scatter-add.9
  856.6 21.7 fusion.156
  887.2 18.5 fusion.157
  905.7 9.6 copy.183
  922.0 15.7 multiply_convert_fusion.6
  942.3 12.5 fusion.238
  957.3 9.2 multiply_reduce_fusion.56
  984.4 12.0 fusion.181
  1016.6 27.8 convert_element_type.206
  1077.1 17.4 multiply_reduce_fusion.2
  1094.4 58.7 %bitcast_convert_fusion = bf16[6144,1536]{1,0:T(8,128)(2,1)} fusion(f32[4,16,32,1536]{3,2,1,0:T(8,128)} %get-tuple-element.191, f32[1536]{0:T(1024)S(1)} %copy-done.29, f32[4,16,32,6144]{3,2,1,0:T(8,128)} %fusion.23), kind=kOutput, calls=%fused_computation.100 | convolution fusion | flops 38783680512 | bytes 81795072 | tf_op jit(solution)/shard_map/iyxf,iyxc->fc/dot_general | solution.py:193
  1153.1 85.2 %fusion.7 = bf16[4,16,32,6144]{3,2,1,0:T(8,128)(2,1)} fusion(f32[4,16,32,6144]{3,2,1,0:T(8,128)} %fusion.23, bf16[6144,1536]{1,0:T(8,128)(2,1)} %param.36, f32[4,16,32,1536]{3,2,1,0:T(8,128)} %get-tuple-element.191, f32[1536]{0:T(1024)S(1)} %copy-done.29), kind=kOutput, calls=%fused_computation.93 | convolution fusion | flops 38912655360 | bytes 106960896 | tf_op jit(solution)/shard_map/iyxc,fc->iyxf/dot_general | solution.py:195
  1238.4 35.2 %reshape.410 = bf16[9437184]{0:T(1024)(128)(2,1)} reshape(bf16[6144,1536]{1,0:T(8,128)(2,1)} %bitcast_convert_fusion) | data formatting | bytes 37748736 | tf_op jit(solution)/shard_map/reshape | solution.py:281
  1273.7 54.0 %fusion.140 = bf16[192,48,8,128]{3,2,1,0:T(8,128)(2,1)} fusion(bf16[4,16,32,6144]{3,2,1,0:T(8,128)(2,1)} %fusion.7, f32[4,16,32,1536]{3,2,1,0:T(8,128)} %get-tuple-element.152, f32[1536]{0:T(1024)} %get-tuple-element.142, f32[1536]{0:T(1024)S(1)} %copy-done.32, f32[4,16,32]{2,1,0:T(8,128)S(1)} %copy-done.25, f32[4,16,32]{2,1,0:T(8,128)S(1)} %copy-done.23), kind=kOutput, calls=%fused_computation.308 | convolution fusion | flops 38679871488 | bytes 56651776 | tf_op jit(solution)/shard_map/iyxc,iyxf->cf/dot_general | solution.py:197
  1327.7 11.0 copy.187
  1338.7 9.3 constant_dynamic-update-slice_fusion.1
  1358.8 57.7 %fusion.237 = (bf16[1536]{0:T(1024)(128)(2,1)S(1)}, f32[4,16,32]{2,1,0:T(8,128)S(1)}, f32[4,16,32,1536]{3,2,1,0:T(8,128)}) fusion(f32[1536]{0:T(1024)S(1)} %copy-done.32, f32[4,16,32,1536]{3,2,1,0:T(8,128)} %get-tuple-element.152, f32[4,16,32]{2,1,0:T(8,128)S(1)} %copy-done.23, bf16[4,16,32,6144]{3,2,1,0:T(8,128)(2,1)} %fusion.7, bf16[1536,6144]{1,0:T(8,128)(2,1)} %param.35), kind=kOutput, calls=%fused_computation.500 | convolution fusion | flops 38670434304 | bytes 69231616 | tf_op jit(solution)/shard_map/iyxf,cf->iyxc/dot_general | solution.py:200
  1416.5 10.4 multiply_reduce_fusion.3
  1427.1 106.6 %multiply_reduce_fusion.4 = (bf16[1536]{0:T(1024)(128)(2,1)S(1)}, bf16[1536]{0:T(1024)(128)(2,1)S(1)}, bf16[1536]{0:T(1024)(128)(2,1)S(1)}, bf16[1536]{0:T(1024)...) fusion(f32[4,22,32,1536]{3,2,1,0:T(8,128)} %maximum_convert_fus, ...), kind=kLoop, calls=%fused_computation.228 | loop fusion | flops 135238656 | bytes 92893184 | tf_op jit(solution)/shard_map/reduce_sum | solution.py:207
  1533.9 66.1 %multiply_reduce_fusion.40 = (bf16[1536]{0:T(1024)(128)(2,1)S(1)}, bf16[1536]{0:T(1024)(128)(2,1)S(1)}, bf16[1536]{0:T(1024)(128)(2,1)S(1)}, bf16[1536]{0:T(1024...) fusion(f32[4,16,32,1536]{3,2,1,0:T(8,128)} %get-tuple-element.1, ...), kind=kLoop, calls=%fused_computation.264 | loop fusion | flops 84913152 | bytes 55093248 | tf_op jit(solution)/shard_map/reduce_sum | solution.py:207
  1600.0 97.1 %multiply_reduce_fusion.22 = (bf16[1536]{0:T(1024)(128)(2,1)S(1)}, bf16[1536]{0:T(1024)(128)(2,1)S(1)}, bf16[1536]{0:T(1024)(128)(2,1)S(1)}, bf16[1536]{0:T(1024...) fusion(f32[4,16,32,1536]{3,2,1,0:T(8,128)} %get-tuple-element.1, ...), kind=kLoop, calls=%fused_computation.246 | loop fusion | flops 116364288 | bytes 61396992 | tf_op jit(solution)/shard_map/reduce_sum | solution.py:207
  1724.6 70.2 %convert_element_type.207 = bf16[16,2,641568]{2,1,0:T(2,128)(2,1)} reshape(bf16[20530176]{0:T(1024)(128)(2,1)} %dynamic-update-slice.12) | data formatting | bytes 82120704 | tf_op jit(solution)/shard_map/convert_element_type | solution.py:298
  1807.5 21.3 multiply_convert_fusion.8
  1844.0 114.7 %reduce_sum.760 = bf16[2,393344]{1,0:T(2,128)(2,1)} reduce(bf16[16,2,393344]{2,1,0:T(2,128)(2,1)} %all-to-all-done, bf16[]{:T(256)} %constant.126.clone.1), dimensions={0}, to_apply=%region_22.23 | reduce | flops 11800320 | bytes 26747394 | tf_op jit(solution)/shard_map/reduce_sum | solution.py:301
  1959.1 726.0 %all-to-all-done.1 = bf16[16,2,641568]{2,1,0:T(2,128)(2,1)} async-done(((bf16[16,2,641568]{2,1,0:T(2,128)(2,1)}), bf16[16,2,641568]{2,1,0:T(2,128)(2,1)}, u32[]{:S(2)}, u32[]{:S(2)}) %all-to-all-start.1) | async-done | bytes 41060384 | tf_op jit(solution)/shard_map/all_to_all | solution.py:297
  2685.0 60.3 %reduce_sum.816 = bf16[2,641568]{1,0:T(2,128)(2,1)} reduce(bf16[16,2,641568]{2,1,0:T(2,128)(2,1)} %all-to-all-done.1, bf16[]{:T(256)} %constant.126.clone.1), dimensions={0}, to_apply=%region_78.79 | reduce | flops 19247040 | bytes 43626624 | tf_op jit(solution)/shard_map/reduce_sum | solution.py:302
  2745.7 273.3 %fusion.116 = bf16[4,16,32,1536]{3,2,1,0:T(8,128)(2,1)} fusion(f32[4,16,32,1536]{3,2,1,0:T(8,128)} %get-tuple-element.191, f32[4,22,32,1536]{3,2,1,0:T(8,128)} %maximum_convert_fusion.1, f32[1536]{0:T(1024)S(1)} %copy-done.36, f32[1536]{0:T(1024)S(1)} %copy-done.34, f32[1536]{0:T(1024)S(1)} %copy-done.96, f32[1536]{0:T(1024)S(1)} %copy-done.98, ...), kind=kLoop, calls=%fused_computation.213 | loop fusion | flops 311427072 | bytes 124579840 | tf_op jit(solution)/shard_map/convert_element_type | solution.py:218
  3019.1 17.4 fusion.201
  3036.5 29.8 fusion.182
  (529 shorter events, 306.9 us)
Async XLA Ops:
  7.2 950.1 %copy-start = (bf16[1536,1024]{1,0:T(8,128)(2,1)S(1)}, bf16[1536,1024]{1,0:T(8,128)(2,1)}, u32[]{:S(2)}) copy-start(bf16[1536,1024]{1,0:T(8,128)(2,1)} %param.37) | copy-start | bytes 9437188
  7.2 414.6 %all-gather.2.cloned.1.call-start = ((), (), s32[]{:S(2)}) async-start(), calls=%async_computation.3 | async-start | bytes 14155776 | tf_op jit(solution)/shard_map/all_gather | solution.py:112
  10.6 46.1 %collective-permute-start = (bf16[4,3,32,1536]{3,2,1,0:T(8,128)(2,1)}, bf16[4,3,32,1536]{3,2,1,0:T(8,128)(2,1)}, u32[]{:S(2)}, u32[]{:S(2)}) collective-permute-start(bf16[4,3,32,1536]{3,2,1,0:T(8,128)(2,1)} %get-tuple-element.160), channel_id=1, source_target_pairs={{0,1},{2,3},{4,5},{6,7},{8,9},{10,11},{12,13},{14,15},{16,17},{18,... | collective-permute-start | bytes 3538952 | tf_op jit(solution)/shard_map/ppermute | solution.py:24
  14.9 41.9 %collective-permute-start.1 = (bf16[4,3,32,1536]{3,2,1,0:T(8,128)(2,1)}, bf16[4,3,32,1536]{3,2,1,0:T(8,128)(2,1)}, u32[]{:S(2)}, u32[]{:S(2)}) collective-permute-start(bf16[4,3,32,1536]{3,2,1,0:T(8,128)(2,1)} %get-tuple-element.161), channel_id=1, source_target_pairs={{1,0},{3,2},{5,4},{7,6},{9,8},{11,10},{13,12},{15,14},{17,16},{19,... | collective-permute-start | bytes 3538952 | tf_op jit(solution)/shard_map/ppermute | solution.py:26
  40.3 901.9 %reduce-scatter.2.cloned.1.call-start = ((), (), s32[]{:S(2)}) async-start(), calls=%async_computation.4 | async-start | bytes 14155776 | tf_op jit(solution)/shard_map/reduce_scatter | solution.py:258
  787.7 18.8 collective-permute-start.3
  789.2 18.5 collective-permute-start.2
  1044.4 750.4 %all-to-all-start = ((bf16[16,2,393344]{2,1,0:T(2,128)(2,1)}), bf16[16,2,393344]{2,1,0:T(2,128)(2,1)}, u32[]{:S(2)}, u32[]{:S(2)}) async-start(bf16[16,2,393344]{2,1,0:T(2,128)(2,1)} %convert_element_type.206), calls=%async_computation.1 | async-start | bytes 50348032 | tf_op jit(solution)/shard_map/all_to_all | solution.py:294
  1055.3 10.4 collective-permute-start.4
  1059.4 9.9 collective-permute-start.5
  1794.8 890.2 %all-to-all-start.1 = ((bf16[16,2,641568]{2,1,0:T(2,128)(2,1)}), bf16[16,2,641568]{2,1,0:T(2,128)(2,1)}, u32[]{:S(2)}, u32[]{:S(2)}) async-start(bf16[16,2,641568]{2,1,0:T(2,128)(2,1)} %convert_element_type.207), calls=%async_computation.2 | async-start | bytes 82132992 | tf_op jit(solution)/shard_map/all_to_all | solution.py:297
  1802.4 1216.7 %all-reduce.7.cloned.1.call-start = ((), (), s32[]{:S(2)}) async-start(), calls=%async_computation.5 | async-start | bytes 8280064
  1804.9 26.4 collective-permute-start.6
  1806.2 29.0 collective-permute-start.7
  1958.7 786.6 %copy-start.42 = (f32[1536]{0:T(1024)S(1)}, f32[1536]{0:T(1024)}, u32[]{:S(2)}) copy-start(f32[1536]{0:T(1024)} %copy-done.41) | copy-start | bytes 18436
  1958.7 786.6 %copy-start.44 = (f32[1536]{0:T(1024)S(1)}, f32[1536]{0:T(1024)}, u32[]{:S(2)}) copy-start(f32[1536]{0:T(1024)} %copy-done.43) | copy-start | bytes 18436
  1958.7 786.6 %copy-start.46 = (f32[1536]{0:T(1024)S(1)}, f32[1536]{0:T(1024)}, u32[]{:S(2)}) copy-start(f32[1536]{0:T(1024)} %copy-done.45) | copy-start | bytes 18436
  1958.8 786.6 %copy-start.48 = (f32[1536]{0:T(1024)S(1)}, f32[1536]{0:T(1024)}, u32[]{:S(2)}) copy-start(f32[1536]{0:T(1024)} %copy-done.47) | copy-start | bytes 18436
  1958.8 786.6 %copy-start.50 = (f32[1536]{0:T(1024)S(1)}, f32[1536]{0:T(1024)}, u32[]{:S(2)}) copy-start(f32[1536]{0:T(1024)} %copy-done.49) | copy-start | bytes 18436
  1958.8 786.6 %copy-start.52 = (f32[1536]{0:T(1024)S(1)}, f32[1536]{0:T(1024)}, u32[]{:S(2)}) copy-start(f32[1536]{0:T(1024)} %copy-done.51) | copy-start | bytes 18436
  1958.8 786.6 %copy-start.54 = (f32[1536]{0:T(1024)S(1)}, f32[1536]{0:T(1024)}, u32[]{:S(2)}) copy-start(f32[1536]{0:T(1024)} %copy-done.53) | copy-start | bytes 18436
  1958.8 786.6 %copy-start.56 = (f32[1536]{0:T(1024)S(1)}, f32[1536]{0:T(1024)}, u32[]{:S(2)}) copy-start(f32[1536]{0:T(1024)} %copy-done.55) | copy-start | bytes 18436
  1958.8 786.6 %copy-start.58 = (f32[1536]{0:T(1024)S(1)}, f32[1536]{0:T(1024)}, u32[]{:S(2)}) copy-start(f32[1536]{0:T(1024)} %copy-done.57) | copy-start | bytes 18436
  1958.8 786.6 %copy-start.60 = (f32[1536]{0:T(1024)S(1)}, f32[1536]{0:T(1024)}, u32[]{:S(2)}) copy-start(f32[1536]{0:T(1024)} %copy-done.59) | copy-start | bytes 18436
  1958.8 786.6 %copy-start.62 = (f32[1536]{0:T(1024)S(1)}, f32[1536]{0:T(1024)}, u32[]{:S(2)}) copy-start(f32[1536]{0:T(1024)} %copy-done.61) | copy-start | bytes 18436
  1958.8 786.6 %copy-start.64 = (f32[1536]{0:T(1024)S(1)}, f32[1536]{0:T(1024)}, u32[]{:S(2)}) copy-start(f32[1536]{0:T(1024)} %copy-done.63) | copy-start | bytes 18436
  1958.8 786.6 %copy-start.66 = (f32[1536]{0:T(1024)S(1)}, f32[1536]{0:T(1024)}, u32[]{:S(2)}) copy-start(f32[1536]{0:T(1024)} %copy-done.65) | copy-start | bytes 18436
  1958.9 786.6 %copy-start.68 = (f32[1536]{0:T(1024)S(1)}, f32[1536]{0:T(1024)}, u32[]{:S(2)}) copy-start(f32[1536]{0:T(1024)} %copy-done.67) | copy-start | bytes 18436
  1958.9 786.6 %copy-start.70 = (f32[1536]{0:T(1024)S(1)}, f32[1536]{0:T(1024)}, u32[]{:S(2)}) copy-start(f32[1536]{0:T(1024)} %copy-done.69) | copy-start | bytes 18436
  1958.9 786.6 %copy-start.72 = (f32[1536]{0:T(1024)S(1)}, f32[1536]{0:T(1024)}, u32[]{:S(2)}) copy-start(f32[1536]{0:T(1024)} %copy-done.71) | copy-start | bytes 18436
  1958.9 786.6 %copy-start.74 = (f32[1536]{0:T(1024)S(1)}, f32[1536]{0:T(1024)}, u32[]{:S(2)}) copy-start(f32[1536]{0:T(1024)} %copy-done.73) | copy-start | bytes 18436
  1958.9 786.6 %copy-start.76 = (f32[1536]{0:T(1024)S(1)}, f32[1536]{0:T(1024)}, u32[]{:S(2)}) copy-start(f32[1536]{0:T(1024)} %copy-done.75) | copy-start | bytes 18436
  1958.9 786.6 %copy-start.78 = (f32[1536]{0:T(1024)S(1)}, f32[1536]{0:T(1024)}, u32[]{:S(2)}) copy-start(f32[1536]{0:T(1024)} %copy-done.77) | copy-start | bytes 18436
  1958.9 786.6 %copy-start.80 = (f32[1536]{0:T(1024)S(1)}, f32[1536]{0:T(1024)}, u32[]{:S(2)}) copy-start(f32[1536]{0:T(1024)} %copy-done.79) | copy-start | bytes 18436
  1958.9 786.6 %copy-start.82 = (f32[1536]{0:T(1024)S(1)}, f32[1536]{0:T(1024)}, u32[]{:S(2)}) copy-start(f32[1536]{0:T(1024)} %copy-done.81) | copy-start | bytes 18436
  1958.9 786.6 %copy-start.84 = (f32[1536]{0:T(1024)S(1)}, f32[1536]{0:T(1024)}, u32[]{:S(2)}) copy-start(f32[1536]{0:T(1024)} %copy-done.83) | copy-start | bytes 18436
  1958.9 786.6 %copy-start.86 = (f32[1536]{0:T(1024)S(1)}, f32[1536]{0:T(1024)}, u32[]{:S(2)}) copy-start(f32[1536]{0:T(1024)} %copy-done.85) | copy-start | bytes 18436
  1959.0 786.6 %copy-start.88 = (f32[1536]{0:T(1024)S(1)}, f32[1536]{0:T(1024)}, u32[]{:S(2)}) copy-start(f32[1536]{0:T(1024)} %copy-done.87) | copy-start | bytes 18436
  1959.0 786.6 %copy-start.90 = (f32[1536]{0:T(1024)S(1)}, f32[1536]{0:T(1024)}, u32[]{:S(2)}) copy-start(f32[1536]{0:T(1024)} %copy-done.89) | copy-start | bytes 18436
  1959.0 786.6 %copy-start.92 = (f32[1536]{0:T(1024)S(1)}, f32[1536]{0:T(1024)}, u32[]{:S(2)}) copy-start(f32[1536]{0:T(1024)} %copy-done.91) | copy-start | bytes 18436
  1959.0 786.6 %copy-start.94 = (f32[1536]{0:T(1024)S(1)}, f32[1536]{0:T(1024)}, u32[]{:S(2)}) copy-start(f32[1536]{0:T(1024)} %copy-done.93) | copy-start | bytes 18436
  1959.0 786.6 %copy-start.96 = (f32[1536]{0:T(1024)S(1)}, f32[1536]{0:T(1024)}, u32[]{:S(2)}) copy-start(f32[1536]{0:T(1024)} %copy-done.95) | copy-start | bytes 18436
  1959.0 786.6 %copy-start.98 = (f32[1536]{0:T(1024)S(1)}, f32[1536]{0:T(1024)}, u32[]{:S(2)}) copy-start(f32[1536]{0:T(1024)} %copy-done.97) | copy-start | bytes 18436
  1959.0 786.6 %copy-start.100 = (f32[1536]{0:T(1024)S(1)}, f32[1536]{0:T(1024)}, u32[]{:S(2)}) copy-start(f32[1536]{0:T(1024)} %copy-done.99) | copy-start | bytes 18436
  1959.0 786.6 %copy-start.102 = (f32[1536]{0:T(1024)S(1)}, f32[1536]{0:T(1024)}, u32[]{:S(2)}) copy-start(f32[1536]{0:T(1024)} %copy-done.101) | copy-start | bytes 18436
  1959.0 786.6 %copy-start.104 = (f32[1536]{0:T(1024)S(1)}, f32[1536]{0:T(1024)}, u32[]{:S(2)}) copy-start(f32[1536]{0:T(1024)} %copy-done.103) | copy-start | bytes 18436
  1959.0 786.6 %copy-start.106 = (f32[1536]{0:T(1024)S(1)}, f32[1536]{0:T(1024)}, u32[]{:S(2)}) copy-start(f32[1536]{0:T(1024)} %copy-done.105) | copy-start | bytes 18436
  1959.1 786.6 %copy-start.108 = (f32[1536]{0:T(1024)S(1)}, f32[1536]{0:T(1024)}, u32[]{:S(2)}) copy-start(f32[1536]{0:T(1024)} %copy-done.107) | copy-start | bytes 18436
  (136 other events, 6041.9 us)
Sparse Core Ops, SparseCore 0:
  40.4 120.7 all-gather.1
  705.3 120.5 reduce-scatter.1
  2745.4 105.5 all-reduce.6
where the time goes:
time: 3080 us; the launch traced here: 3070 us
  other arithmetic  1180 us (38%)
  waiting for transfers between devices  748 us (24%)
  matrix products  734 us (24%)
  local copies, waits for them, and re-layouts  354 us (11%)
  starting transfers between devices  37.4 us (1%)
    all_to_all x1, waiting for transfers between devices, per_device(): lax.all_to_all(conv_blocks.astype(jnp.bfloat16), 'dp', split_axis=0, conc...  726 us
    reduce_sum x3, other arithmetic, normed(): center = values - jnp.mean(values, axis=-1, keepdims=True)  303 us
    convert_element_type x1, other arithmetic, per_device(): (d_post + depthwise(d_rim, dw_kernel, row_count, col_count, True)).astype...  273 us
    reduce_sum x3, other arithmetic, per_device(): jnp.sum(framed[:, tap_row:tap_row + row_count, tap_col:tap_col + col_coun...  270 us
    reduce_sum x1, other arithmetic, per_device(): vit_part = jnp.sum(vit_recv, axis=0)  115 us
    unnamed x360, local copies, waits for them, and re-layouts  91.8 us
    dot_general x1, matrix products, per_device(): jnp.einsum('iyxc,fc->iyxf', d_branch, w_pw2, preferred_element_type=jnp.f...  85.2 us
    convert_element_type x1, local copies, waits for them, and re-layouts, per_device(): conv_blocks.astype(jnp.bfloat16)  70.2 us
  transfers between devices with their start and end apart: 13, of which 7 were waited for; matrix products, arithmetic and copies ran while one was open for 57% of the time, Pallas kernels for 0%

commit v1 on v0

v1 whole, which is shorter than its diff:
```python
import math

import jax
import jax.numpy as jnp
from jax import lax
from jax.experimental import pallas as pl
from jax.experimental.pallas import tpu as pltpu
from jax.sharding import PartitionSpec as P

HEADS = 16
KS = 7
REACH = KS // 2
EPSILON = 1e-05
LANES = 128
EDGE = 8
F32 = jnp.float32
BF16 = jnp.bfloat16
VMEM_BYTES = 60 * 1024 * 1024


def dot_nn(a, b):
    return jnp.dot(a, b, preferred_element_type=F32)


def dot_nt(a, b):
    return lax.dot_general(a, b, (((1,), (1,)), ((), ())), preferred_element_type=F32)


def dot_tn(a, b):
    return lax.dot_general(a, b, (((0,), (0,)), ((), ())), preferred_element_type=F32)


def flip(value):
    return value.astype(F32).T.astype(BF16)


def row_step(rows):
    for step in (128, 96, 64, 48, 32, 16):
        if rows % step == 0:
            return step
    return rows


def over_rows(rows, body):
    step = row_step(rows)

    def one(at, carry):
        body(pl.ds(pl.multiple_of(at * step, step), step))
        return carry

    if step == rows:
        body(pl.ds(0, rows))
    else:
        lax.fori_loop(0, rows // step, one, 0)


def lane_tile(at):
    return pl.ds(pl.multiple_of(at * LANES, LANES), LANES)


def unit(values):
    center = values - jnp.mean(values, axis=-1, keepdims=True)
    inverse = lax.rsqrt(jnp.mean(center * center, axis=-1, keepdims=True) + EPSILON)
    return center * inverse, inverse


def unit_back(unit_values, inverse, grad):
    return (
        grad
        - jnp.mean(grad, axis=-1, keepdims=True)
        - unit_values * jnp.mean(grad * unit_values, axis=-1, keepdims=True)
    ) * inverse


def gelu_pair(x):
    scale = math.sqrt(2.0 / math.pi)
    square = x * x
    bend = jnp.tanh(x * (scale + (scale * 0.044715) * square))
    half = 0.5 + 0.5 * bend
    slope = half + (0.5 * x) * (1.0 - bend * bend) * (scale + (3.0 * scale * 0.044715) * square)
    return x * half, slope


def col_sum(values):
    return jnp.sum(values, axis=0, keepdims=True)


def held(at, live):
    return jnp.maximum(jnp.minimum(at, live[0] - 1), 0)


def slot(*shape):
    return pl.BlockSpec(
        (1,) + shape, lambda *g: (held(g[0], g[-1]),) + (0,) * len(shape)
    )


def every_slot(*shape):
    return pl.BlockSpec((1,) + shape, lambda *g: (g[0],) + (0,) * len(shape))


def whole(*shape):
    return pl.BlockSpec(shape, lambda *g: (0,) * len(shape), pipeline_mode=pl.Buffered(1))


def result(*shape):
    return pl.BlockSpec(shape, lambda *g: (0,) * len(shape))


def run(name, body, grid, live, args, in_specs, outs, scratch=(), flops=0):
    out_shape = [jax.ShapeDtypeStruct(shape, dtype) for shape, dtype, _ in outs]
    moved = sum(a.size * a.dtype.itemsize for a in args)
    moved += sum(math.prod(s) * jnp.dtype(d).itemsize for s, d, _ in outs)
    return pl.pallas_call(
        body,
        grid_spec=pltpu.PrefetchScalarGridSpec(
            num_scalar_prefetch=1,
            grid=grid,
            in_specs=in_specs,
            out_specs=[spec for _, _, spec in outs],
            scratch_shapes=list(scratch),
        ),
        out_shape=out_shape,
        compiler_params=pltpu.CompilerParams(
            dimension_semantics=("arbitrary",) * len(grid), vmem_limit_bytes=VMEM_BYTES
        ),
        cost_estimate=pl.CostEstimate(
            flops=int(flops), bytes_accessed=int(moved), transcendentals=0
        ),
        name=name,
    )(live, *args)


def vit_front(live, tok_all, w_qkv, w_out, gains, shifts, tok_rows):
    slots, key_rows, width = tok_all.shape
    head = width // HEADS
    pairs = width // LANES
    per_tile = LANES // head

    def body(
        n, x_ref, wq_ref, wo_ref, g_ref, b_ref,
        normed_ref, q_ref, kv_ref, probs_ref, mixed_ref, res_ref, inner_ref, flip_ref,
    ):
        @pl.when(pl.program_id(0) < n[0])
        def _():
            def first_norm(rows):
                value, _ = unit(x_ref[0, rows, :].astype(F32))
                normed_ref[0, rows, :] = (value * g_ref[0:1, :] + b_ref[0:1, :]).astype(BF16)

            over_rows(key_rows, first_norm)
            q_ref[0] = dot_nn(normed_ref[0, 0:tok_rows, :], wq_ref[:, 0:width]).astype(BF16)
            for part in range(4):
                cols = slice(part * width // 2, (part + 1) * width // 2)
                w_cols = slice(width + cols.start, width + cols.stop)
                kv_ref[0, :, cols] = dot_nn(normed_ref[0], wq_ref[:, w_cols]).astype(BF16)

            lane = lax.broadcasted_iota(jnp.int32, (1, LANES), 1) // head

            def heads(pair, carry):
                q = q_ref[0, :, lane_tile(pair)] * jnp.asarray(1.0 / math.sqrt(head), BF16)
                k = kv_ref[0, :, lane_tile(pair)].astype(F32)
                v_flip = flip(kv_ref[0, :, lane_tile(pairs + pair)])
                mixed = []
                for h in range(per_tile):
                    scores = dot_nt(jnp.where(lane == h, k, 0.0).astype(BF16), q)
                    top = jnp.max(scores, axis=0, keepdims=True)
                    raised = jnp.exp(scores - top)
                    probs = (raised * (1.0 / col_sum(raised))).astype(BF16)
                    probs_ref[0, pair * per_tile + h] = probs
                    mixed.append(dot_nn(v_flip[h * head : (h + 1) * head, :], probs))
                mixed_ref[0, :, lane_tile(pair)] = jnp.concatenate(mixed, axis=0).T.astype(BF16)
                return carry

            lax.fori_loop(0, pairs, heads, 0)
            res_ref[0] = dot_nn(mixed_ref[0], wo_ref[...])

            def second_norm(rows):
                res = res_ref[0, rows, :] + x_ref[0, rows, :].astype(F32)
                res_ref[0, rows, :] = res
                value, _ = unit(res)
                inner_ref[0, rows, :] = (value * g_ref[1:2, :] + b_ref[1:2, :]).astype(BF16)

            over_rows(tok_rows, second_norm)
            flip_ref[0] = flip(inner_ref[0])

    macs = slots * (key_rows * width * 2 * width + tok_rows * width * 2 * width)
    macs += slots * 2 * HEADS * tok_rows * key_rows * LANES
    return run(
        "vit_front",
        body,
        (slots,),
        live,
        (tok_all, w_qkv, w_out, gains, shifts),
        [slot(key_rows, width), whole(*w_qkv.shape), whole(*w_out.shape)]
        + [whole(*gains.shape), whole(*shifts.shape)],
        [
            ((slots, key_rows, width), BF16, slot(key_rows, width)),
            ((slots, tok_rows, width), BF16, slot(tok_rows, width)),
            ((slots, key_rows, 2 * width), BF16, slot(key_rows, 2 * width)),
            ((slots, HEADS, key_rows, tok_rows), BF16, slot(HEADS, key_rows, tok_rows)),
            ((slots, tok_rows, width), BF16, slot(tok_rows, width)),
            ((slots, tok_rows, width), F32, slot(tok_rows, width)),
            ((slots, tok_rows, width), BF16, slot(tok_rows, width)),
            ((slots, width, tok_rows), BF16, slot(width, tok_rows)),
        ],
        flops=2 * macs,
    )


def vit_mlp(live, inner, inner_flip, d_mlp, residual, w_fc1, w_fc2):
    slots, tok_rows, width = inner.shape
    hidden = w_fc1.shape[1]
    block = 512
    steps = hidden // block

    def body(
        n, x_ref, xt_ref, dm_ref, res_ref, w1_ref, w2_ref, low_ref, din_ref, g1_ref, g2_ref, a1, a2
    ):
        @pl.when(pl.program_id(0) == 0)
        def _():
            low_ref[...] = res_ref[...]
            din_ref[...] = jnp.zeros(din_ref.shape, F32)

        a1[...] = jnp.zeros(a1.shape, F32)
        a2[...] = jnp.zeros(a2.shape, F32)

        def one(at, carry):
            act, slope = gelu_pair(dot_nn(x_ref[at], w1_ref[...]))
            act = act.astype(BF16)
            low_ref[at] += dot_nn(act, w2_ref[...])
            d_fc = (slope * dot_nt(dm_ref[at], w2_ref[...])).astype(BF16)
            a1[...] += dot_nn(xt_ref[at], d_fc)
            a2[...] += dot_tn(act, dm_ref[at])
            din_ref[at] += dot_nt(d_fc, w1_ref[...])
            return carry

        lax.fori_loop(0, n[0], one, 0)
        g1_ref[...] = a1[...].astype(BF16)
        g2_ref[...] = a2[...].astype(BF16)

    wide = (slots, tok_rows, width)
    by_col = pl.BlockSpec((width, block), lambda j, n: (0, j))
    by_row = pl.BlockSpec((block, width), lambda j, n: (j, 0))
    return run(
        "vit_mlp",
        body,
        (steps,),
        live,
        (inner, inner_flip, d_mlp, residual, w_fc1, w_fc2),
        [whole(*wide), whole(*inner_flip.shape), whole(*wide), whole(*wide), by_col, by_row],
        [
            (wide, F32, result(*wide)),
            (wide, F32, result(*wide)),
            (w_fc1.shape, BF16, by_col),
            (w_fc2.shape, BF16, by_row),
        ],
        [pltpu.VMEM((width, block), F32), pltpu.VMEM((block, width), F32)],
        flops=12 * slots * tok_rows * width * hidden,
    )


def vit_back(live, residual, d_inner, d_merged, mixed, w_out, gains):
    slots, tok_rows, width = residual.shape

    def body(
        n, res_ref, din_ref, dm_ref, mix_ref, wo_ref, g_ref,
        dres_ref, dmix_ref, gout_ref, sums_ref, low, acc,
    ):
        at = pl.program_id(0)

        @pl.when(at == 0)
        def _():
            acc[...] = jnp.zeros(acc.shape, F32)
            sums_ref[...] = jnp.zeros(sums_ref.shape, F32)

        @pl.when(at < n[0])
        def _():
            def back(rows):
                value, inverse = unit(res_ref[0, rows, :])
                e = din_ref[0, rows, :]
                sums_ref[0:1, :] += col_sum(e * value)
                sums_ref[1:2, :] += col_sum(e)
                d_res = dm_ref[0, rows, :].astype(F32) + unit_back(value, inverse, e * g_ref[1:2, :])
                dres_ref[0, rows, :] = d_res
                low[rows, :] = d_res.astype(BF16)

            over_rows(tok_rows, back)
            dmix_ref[0] = dot_nt(low[...], wo_ref[...]).astype(BF16)
            acc[...] += dot_tn(mix_ref[0], low[...])

        @pl.when(at == slots - 1)
        def _():
            gout_ref[...] = acc[...].astype(BF16)

    wide = (slots, tok_rows, width)
    one = slot(tok_rows, width)
    return run(
        "vit_back",
        body,
        (slots,),
        live,
        (residual, d_inner, d_merged, mixed, w_out, gains),
        [one, one, one, one, whole(*w_out.shape), whole(*gains.shape)],
        [
            (wide, F32, one),
            (wide, BF16, one),
            (w_out.shape, BF16, result(*w_out.shape)),
            ((8, width), F32, result(8, width)),
        ],
        [pltpu.VMEM((tok_rows, width), BF16), pltpu.VMEM(w_out.shape, F32)],
        flops=4 * slots * tok_rows * width * width,
    )


def attention_back(live, probs, q, kv, d_mixed):
    slots, _, key_rows, tok_rows = probs.shape
    width = q.shape[2]
    head = width // HEADS
    pairs = width // LANES
    per_tile = LANES // head
    scale = 1.0 / math.sqrt(head)

    def body(n, p_ref, q_ref, k_ref, v_ref, dm_ref, dq_ref, dk_ref, dv_ref):
        @pl.when(pl.program_id(0) < n[0])
        def _():
            lane = lax.broadcasted_iota(jnp.int32, (1, LANES), 1) // head
            q = q_ref[0].astype(F32) * scale
            v = v_ref[0].astype(F32)
            dm = dm_ref[0].astype(F32)
            dm_low = dm_ref[0]
            k_flip = flip(k_ref[0].astype(F32) * scale)
            d_keys = jnp.zeros((key_rows, LANES), F32)
            d_values = jnp.zeros((key_rows, LANES), F32)
            d_query = []
            for h in range(per_tile):
                own = lane == h
                probs_low = p_ref[0, h]
                d_probs = dot_nt(jnp.where(own, v, 0.0).astype(BF16), dm_low)
                d_values += dot_nn(probs_low, jnp.where(own, dm, 0.0).astype(BF16))
                wide = probs_low.astype(F32)
                d_scores = (wide * (d_probs - col_sum(wide * d_probs))).astype(BF16)
                d_keys += dot_nn(d_scores, jnp.where(own, q, 0.0).astype(BF16))
                d_query.append(dot_nn(k_flip[h * head : (h + 1) * head, :], d_scores))
            dq_ref[0] = jnp.concatenate(d_query, axis=0).T.astype(BF16)
            dk_ref[0] = d_keys.astype(BF16)
            dv_ref[0] = d_values.astype(BF16)

    def held_pair(i, p, n):
        return jnp.where(i < n[0], p, pairs - 1)

    def at_pair(rows, shift=0):
        return pl.BlockSpec(
            (1, rows, LANES), lambda i, p, n: (held(i, n), 0, held_pair(i, p, n) + shift)
        )

    own = at_pair(tok_rows)
    keys = at_pair(key_rows)
    return run(
        "attention_back",
        body,
        (slots, pairs),
        live,
        (probs, q, kv, kv, d_mixed),
        [
            pl.BlockSpec(
                (1, per_tile, key_rows, tok_rows),
                lambda i, p, n: (held(i, n), held_pair(i, p, n), 0, 0),
            ),
            own,
            keys,
            at_pair(key_rows, pairs),
            own,
        ],
        [
            (q.shape, BF16, own),
            ((slots, key_rows, width), BF16, keys),
            ((slots, key_rows, width), BF16, keys),
        ],
        flops=8 * slots * HEADS * tok_rows * key_rows * LANES,
    )


def qkv_back(live, normed, d_q, d_k, d_v, w_qkv):
    slots, key_rows, width = normed.shape
    tok_rows = d_q.shape[1]

    def body(n, x_ref, dq_ref, dk_ref, dv_ref, w_ref, dn_ref, gw_ref, x_flip, acc):
        at = pl.program_id(0)

        @pl.when(at == 0)
        def _():
            acc[...] = jnp.zeros(acc.shape, F32)

        @pl.when(at < n[0])
        def _():
            x_flip[...] = flip(x_ref[0])
            dn_ref[0] = dot_nt(dk_ref[0], w_ref[:, width : 2 * width])
            dn_ref[0] += dot_nt(dv_ref[0], w_ref[:, 2 * width :])
            dn_ref[0, 0:tok_rows, :] += dot_nt(dq_ref[0], w_ref[:, 0:width])
            acc[:, 0:width] += dot_nn(x_flip[:, 0:tok_rows], dq_ref[0])
            acc[:, width : 2 * width] += dot_nn(x_flip[...], dk_ref[0])
            acc[:, 2 * width :] += dot_nn(x_flip[...], dv_ref[0])

        @pl.when(at == slots - 1)
        def _():
            gw_ref[...] = acc[...].astype(BF16)

    keys = slot(key_rows, width)
    return run(
        "qkv_back",
        body,
        (slots,),
        live,
        (normed, d_q, d_k, d_v, w_qkv),
        [keys, slot(tok_rows, width), keys, keys, whole(*w_qkv.shape)],
        [(normed.shape, F32, keys), (w_qkv.shape, BF16, result(*w_qkv.shape))],
        [pltpu.VMEM((width, key_rows), BF16), pltpu.VMEM(w_qkv.shape, F32)],
        flops=4 * slots * width * width * (2 * key_rows + tok_rows),
    )


def tokens_back(live, tokens, d_norm, arrived, d_residual, gains):
    slots, tok_rows, width = tokens.shape

    def body(n, x_ref, dn_ref, more_ref, dres_ref, g_ref, out_ref, sums_ref):
        at = pl.program_id(0)

        @pl.when(at == 0)
        def _():
            sums_ref[...] = jnp.zeros(sums_ref.shape, F32)

        @pl.when(at < n[0])
        def _():
            def back(rows):
                value, inverse = unit(x_ref[0, rows, :].astype(F32))
                e = dn_ref[0, rows, :] + more_ref[0, rows, :].astype(F32)
                sums_ref[0:1, :] += col_sum(e * value)
                sums_ref[1:2, :] += col_sum(e)
                grad = dres_ref[0, rows, :] + unit_back(value, inverse, e * g_ref[0:1, :])
                out_ref[0, rows, :] = grad.astype(BF16)

            over_rows(tok_rows, back)

        @pl.when(at >= n[0])
        def _():
            out_ref[...] = jnp.zeros(out_ref.shape, BF16)

    one = slot(tok_rows, width)
    return run(
        "tokens_back",
        body,
        (slots,),
        live,
        (tokens, d_norm, arrived, d_residual, gains),
        [one, one, one, one, whole(*gains.shape)],
        [
            (tokens.shape, BF16, every_slot(tok_rows, width)),
            ((8, width), F32, result(8, width)),
        ],
    )


def stage_rows(frame, top_ref, mid_ref, bottom_ref, lanes):
    rows, cols = mid_ref.shape[1], mid_ref.shape[2]
    inside = slice(EDGE, EDGE + cols)
    frame[0:REACH, inside, :] = top_ref[0, :, :, lanes].astype(F32)
    frame[REACH : REACH + rows, inside, :] = mid_ref[0, :, :, lanes].astype(F32)
    frame[REACH + rows :, inside, :] = bottom_ref[0, :, :, lanes].astype(F32)


def depthwise_rows(frame, rows, cols, tap, flipped, emit):
    totals = {}
    for y in range(rows + 2 * REACH):
        for left in range(KS):
            shifted = frame[y, EDGE - REACH + left : EDGE - REACH + left + cols, :]
            for top in range(KS):
                out = y - top
                if 0 <= out < rows:
                    at = (KS - 1 - top) * KS + KS - 1 - left if flipped else top * KS + left
                    term = shifted * tap(at)
                    totals[out] = totals[out] + term if out in totals else term
        if y >= 2 * REACH:
            emit(y - 2 * REACH, totals.pop(y - 2 * REACH))


def conv_front(live, top, high, bottom, kernel, gains, shifts):
    slots, rows, cols, channels = high.shape
    cells = rows * cols

    def body(
        n, top_ref, mid_ref, bottom_ref, k_ref, g_ref, b_ref,
        spatial_ref, flip_ref, unit_ref, inv_ref, frame, middle,
    ):
        @pl.when(pl.program_id(0) < n[0])
        def _():
            frame[...] = jnp.zeros(frame.shape, F32)

            def tile(at, carry):
                lanes = lane_tile(at)
                stage_rows(frame, top_ref, mid_ref, bottom_ref, lanes)
                bias = b_ref[0:1, lanes]

                def emit(y, total):
                    middle[y * cols : (y + 1) * cols, lanes] = total + bias

                depthwise_rows(frame, rows, cols, lambda t: k_ref[t : t + 1, lanes], False, emit)
                return carry

            lax.fori_loop(0, channels // LANES, tile, 0)

            def norm(part):
                value, inverse = unit(middle[part, :])
                inv_ref[0, part, :] = inverse
                unit_ref[0, part, :] = value.astype(BF16)
                spatial_ref[0, part, :] = (value * g_ref[0:1, :] + b_ref[1:2, :]).astype(BF16)

            over_rows(cells, norm)
            flip_ref[0] = flip(spatial_ref[0])

    halo = slot(REACH, cols, channels)
    return run(
        "conv_front",
        body,
        (slots,),
        live,
        (top, high, bottom, kernel, gains, shifts),
        [halo, slot(rows, cols, channels), halo, whole(*kernel.shape)]
        + [whole(*gains.shape), whole(*shifts.shape)],
        [
            ((slots, cells, channels), BF16, slot(cells, channels)),
            ((slots, channels, cells), BF16, slot(channels, cells)),
            ((slots, cells, channels), BF16, slot(cells, channels)),
            ((slots, cells, 1), F32, slot(cells, 1)),
        ],
        [
            pltpu.VMEM((rows + 2 * REACH, cols + 2 * EDGE, LANES), F32),
            pltpu.VMEM((cells, channels), F32),
        ],
        flops=2 * slots * cells * channels * KS * KS * 40,
    )


def conv_mlp(live, spatial, high, w_pw1, w_pw2, gains):
    slots, cells, channels = spatial.shape
    hidden = w_pw1.shape[1]
    block = 512
    steps = hidden // block

    def body(
        n, x_ref, high_ref, w1_ref, w2_ref, g_ref, act_ref, slope_ref, branch_ref, out_ref, acc
    ):
        at, step = pl.program_id(0), pl.program_id(1)

        @pl.when(at < n[0])
        def _():
            act, slope = gelu_pair(dot_nn(x_ref[0], w1_ref[...]))
            act = act.astype(BF16)
            act_ref[0] = act
            slope_ref[0] = slope.astype(BF16)
            part = dot_nn(act, w2_ref[...])

            @pl.when(step == 0)
            def _():
                acc[...] = part

            @pl.when(step > 0)
            def _():
                acc[...] += part

            @pl.when(step == steps - 1)
            def _():
                def close(rows):
                    branch = acc[rows, :]
                    branch_ref[0, rows, :] = branch.astype(BF16)
                    out_ref[0, rows, :] = (
                        high_ref[0, rows, :].astype(F32) + g_ref[1:2, :] * branch
                    ).astype(BF16)

                over_rows(cells, close)

        @pl.when((at >= n[0]) & (step == 0))
        def _():
            out_ref[...] = jnp.zeros(out_ref.shape, BF16)

    def held_step(i, j, n):
        return jnp.where(i < n[0], j, steps - 1)

    one = slot(cells, channels)
    hidden_block = pl.BlockSpec(
        (1, cells, block), lambda i, j, n: (held(i, n), 0, held_step(i, j, n))
    )
    return run(
        "conv_mlp",
        body,
        (slots, steps),
        live,
        (spatial, high, w_pw1, w_pw2, gains),
        [
            one,
            one,
            pl.BlockSpec((channels, block), lambda i, j, n: (0, held_step(i, j, n))),
            pl.BlockSpec((block, channels), lambda i, j, n: (held_step(i, j, n), 0)),
            whole(*gains.shape),
        ],
        [
            ((slots, cells, hidden), BF16, hidden_block),
            ((slots, cells, hidden), BF16, hidden_block),
            (spatial.shape, BF16, one),
            (spatial.shape, BF16, every_slot(cells, channels)),
        ],
        [pltpu.VMEM((cells, channels), F32)],
        flops=4 * slots * cells * channels * hidden,
    )


def pool(live, high_out, bins, side):
    slots, cells, channels = high_out.shape
    tok_rows = bins.shape[0] - 2 * side

    def body(n, x_ref, p_ref, own_ref, before_ref, after_ref):
        @pl.when(pl.program_id(0) < n[0])
        def _():
            part = dot_nn(p_ref[...], x_ref[0])
            before_ref[0] = part[0:side].astype(BF16)
            own_ref[0] = part[side : side + tok_rows]
            after_ref[0] = part[side + tok_rows :].astype(BF16)

    return run(
        "pool",
        body,
        (slots,),
        live,
        (high_out, bins),
        [slot(cells, channels), whole(*bins.shape)],
        [
            ((slots, tok_rows, channels), F32, slot(tok_rows, channels)),
            ((slots, side, channels), BF16, slot(side, channels)),
            ((slots, side, channels), BF16, slot(side, channels)),
        ],
        flops=2 * slots * cells * channels * bins.shape[0],
    )


def adapter(live, own, first, last, low_out, d_merged, w_pool, w_gate):
    slots, tok_rows, channels = own.shape
    side = first.shape[1]
    width = w_pool.shape[1]

    def body(
        n, own_ref, first_ref, last_ref, low_ref, dm_ref, w_ref, gate_ref,
        merged_ref, dpool_ref, gw_ref, ggate_ref, acc,
    ):
        at = pl.program_id(0)

        @pl.when(at == 0)
        def _():
            acc[...] = jnp.zeros(acc.shape, F32)
            ggate_ref[...] = jnp.zeros(ggate_ref.shape, F32)

        @pl.when(at < n[0])
        def _():
            pooled_low = jnp.concatenate(
                [
                    own_ref[0, 0:side] + first_ref[0].astype(F32),
                    own_ref[0, side : tok_rows - side],
                    own_ref[0, tok_rows - side :] + last_ref[0].astype(F32),
                ],
                axis=0,
            ).astype(BF16)
            pooled = pooled_low.astype(F32)
            lifted = dot_nn(pooled_low, w_ref[...])
            logit = jnp.sum(pooled * gate_ref[...], axis=-1, keepdims=True)
            gate = 1.0 / (1.0 + jnp.exp(-logit))
            merged_ref[0] = (low_ref[0] + gate * lifted).astype(BF16)
            d_top = dm_ref[0].astype(F32)
            d_logit = jnp.sum(d_top * lifted, axis=-1, keepdims=True) * gate * (1.0 - gate)
            d_lifted = (gate * d_top).astype(BF16)
            acc[...] += dot_tn(pooled_low, d_lifted)
            ggate_ref[0:1, :] += col_sum(d_logit * pooled)
            dpool_ref[0] = (dot_nt(d_lifted, w_ref[...]) + d_logit * gate_ref[...]).astype(BF16)

        @pl.when(at >= n[0])
        def _():
            merged_ref[...] = jnp.zeros(merged_ref.shape, BF16)

        @pl.when(at == slots - 1)
        def _():
            gw_ref[...] = acc[...].astype(BF16)

    edge = slot(side, channels)
    return run(
        "adapter",
        body,
        (slots,),
        live,
        (own, first, last, low_out, d_merged, w_pool, w_gate),
        [slot(tok_rows, channels), edge, edge, slot(tok_rows, width), slot(tok_rows, width)]
        + [whole(*w_pool.shape), whole(*w_gate.shape)],
        [
            ((slots, tok_rows, width), BF16, every_slot(tok_rows, width)),
            (own.shape, BF16, slot(tok_rows, channels)),
            (w_pool.shape, BF16, result(*w_pool.shape)),
            ((8, channels), F32, result(8, channels)),
        ],
        [pltpu.VMEM(w_pool.shape, F32)],
        flops=6 * slots * tok_rows * channels * width,
    )


def unpool(live, near, spread, d_conv, branch, gains):
    slots, near_rows, channels = near.shape
    cells = d_conv.shape[1]

    def body(n, near_ref, s_ref, dc_ref, branch_ref, g_ref, dpost_ref, dbranch_ref, sums_ref):
        at = pl.program_id(0)

        @pl.when(at == 0)
        def _():
            sums_ref[...] = jnp.zeros(sums_ref.shape, F32)

        @pl.when(at < n[0])
        def _():
            def part(rows):
                d_post = dc_ref[0, rows, :].astype(F32) + dot_nn(s_ref[rows, :], near_ref[0])
                sums_ref[0:1, :] += col_sum(d_post * branch_ref[0, rows, :].astype(F32))
                dpost_ref[0, rows, :] = d_post.astype(BF16)
                dbranch_ref[0, rows, :] = (g_ref[1:2, :] * d_post).astype(BF16)

            over_rows(cells, part)

    one = slot(cells, channels)
    return run(
        "unpool",
        body,
        (slots,),
        live,
        (near, spread, d_conv, branch, gains),
        [slot(near_rows, channels), whole(*spread.shape), one, one, whole(*gains.shape)],
        [
            (d_conv.shape, BF16, one),
            (d_conv.shape, BF16, one),
            ((8, channels), F32, result(8, channels)),
        ],
        flops=2 * slots * cells * channels * near_rows,
    )


def conv_mlp_back(live, spatial_flip, act, slope, d_branch, w_pw1, w_pw2):
    slots, channels, cells = spatial_flip.shape
    hidden = w_pw1.shape[1]
    block = 256
    steps = hidden // block

    def body(
        n, xt_ref, act_ref, slope_ref, db_ref, w1_ref, w2_ref, g1_ref, g2_ref, dsp_ref,
        a1, a2, dsp, sem,
    ):
        step = pl.program_id(0)

        @pl.when(step == 0)
        def _():
            dsp[...] = jnp.zeros(dsp.shape, F32)

        a1[...] = jnp.zeros(a1.shape, F32)
        a2[...] = jnp.zeros(a2.shape, F32)

        def one(at, carry):
            d_hidden = dot_nt(db_ref[at], w2_ref[...])
            d_expand = (slope_ref[at].astype(F32) * d_hidden).astype(BF16)
            a2[...] += dot_tn(act_ref[at], db_ref[at])
            a1[...] += dot_nn(xt_ref[at], d_expand)
            dsp[at] += dot_nt(d_expand, w1_ref[...])
            return carry

        lax.fori_loop(0, n[0], one, 0)
        g1_ref[...] = a1[...].astype(BF16)
        g2_ref[...] = a2[...].astype(BF16)

        @pl.when(step == steps - 1)
        def _():
            out = pltpu.make_async_copy(dsp, dsp_ref, sem)
            out.start()
            out.wait()

    by_col = pl.BlockSpec((channels, block), lambda j, n: (0, j))
    by_row = pl.BlockSpec((block, channels), lambda j, n: (j, 0))
    by_hidden = pl.BlockSpec((slots, cells, block), lambda j, n: (0, 0, j))
    wide = (slots, cells, channels)
    return run(
        "conv_mlp_back",
        body,
        (steps,),
        live,
        (spatial_flip, act, slope, d_branch, w_pw1, w_pw2),
        [whole(*spatial_flip.shape), by_hidden, by_hidden, whole(*wide), by_col, by_row],
        [
            (w_pw1.shape, BF16, by_col),
            (w_pw2.shape, BF16, by_row),
            (wide, F32, pl.BlockSpec(memory_space=pl.ANY)),
        ],
        [
            pltpu.VMEM((channels, block), F32),
            pltpu.VMEM((block, channels), F32),
            pltpu.VMEM(wide, F32),
            pltpu.SemaphoreType.DMA,
        ],
        flops=8 * slots * cells * channels * hidden,
    )


def conv_norm_back(live, d_spatial, unit_values, inverse, gains):
    slots, cells, channels = d_spatial.shape

    def body(n, e_ref, u_ref, inv_ref, g_ref, out_ref, sums_ref):
        at = pl.program_id(0)

        @pl.when(at == 0)
        def _():
            sums_ref[...] = jnp.zeros(sums_ref.shape, F32)

        @pl.when(at < n[0])
        def _():
            def part(rows):
                e = e_ref[0, rows, :]
                value = u_ref[0, rows, :].astype(F32)
                sums_ref[0:1, :] += col_sum(e * value)
                sums_ref[1:2, :] += col_sum(e)
                grad = unit_back(value, inv_ref[0, rows, :], e * g_ref[0:1, :])
                sums_ref[2:3, :] += col_sum(grad)
                out_ref[0, rows, :] = grad.astype(BF16)

            over_rows(cells, part)

    one = slot(cells, channels)
    return run(
        "conv_norm_back",
        body,
        (slots,),
        live,
        (d_spatial, unit_values, inverse, gains),
        [one, one, slot(cells, 1), whole(*gains.shape)],
        [(d_spatial.shape, BF16, one), ((8, channels), F32, result(8, channels))],
    )


def conv_back(live, top, high, bottom, d_top, d_mid, d_bottom, d_post, kernel):
    slots, rows, cols, channels = high.shape

    def body(
        n, top_ref, mid_ref, bottom_ref, dt_ref, dm_ref, db_ref, dpost_ref, k_ref,
        out_ref, gk_ref, frame, d_frame,
    ):
        at = pl.program_id(0)

        @pl.when(at == 0)
        def _():
            gk_ref[...] = jnp.zeros(gk_ref.shape, F32)

        @pl.when(at < n[0])
        def _():
            frame[...] = jnp.zeros(frame.shape, F32)
            d_frame[...] = jnp.zeros(d_frame.shape, F32)

            def tile(tile_at, carry):
                lanes = lane_tile(tile_at)
                stage_rows(frame, top_ref, mid_ref, bottom_ref, lanes)
                stage_rows(d_frame, dt_ref, dm_ref, db_ref, lanes)

                def emit(y, total):
                    grad = total + dpost_ref[0, y, :, lanes].astype(F32)
                    out_ref[0, y, :, lanes] = grad.astype(BF16)

                depthwise_rows(d_frame, rows, cols, lambda t: k_ref[t : t + 1, lanes], True, emit)
                for left in range(KS):
                    totals = [None] * KS
                    grads = {}
                    for y in range(rows + 2 * REACH):
                        begin = EDGE - REACH + left
                        shifted = frame[y, begin : begin + cols, :].reshape(cols // 8, 8, LANES)
                        if y < rows:
                            grads[y] = d_frame[y + REACH, EDGE : EDGE + cols, :].reshape(
                                cols // 8, 8, LANES
                            )
                        for tap_row in range(KS):
                            row = y - tap_row
                            if 0 <= row < rows:
                                term = jnp.sum(shifted * grads[row], axis=0)
                                old = totals[tap_row]
                                totals[tap_row] = term if old is None else old + term
                        grads.pop(y - KS + 1, None)
                    for tap_row in range(KS):
                        tap = tap_row * KS + left
                        gk_ref[tap : tap + 1, lanes] += col_sum(totals[tap_row])
                return carry

            lax.fori_loop(0, channels // LANES, tile, 0)

        @pl.when(at >= n[0])
        def _():
            out_ref[...] = jnp.zeros(out_ref.shape, BF16)

    halo = slot(REACH, cols, channels)
    one = slot(rows, cols, channels)
    frame_shape = (rows + 2 * REACH, cols + 2 * EDGE, LANES)
    return run(
        "conv_back",
        body,
        (slots,),
        live,
        (top, high, bottom, d_top, d_mid, d_bottom, d_post, kernel),
        [halo, one, halo, halo, one, halo, one, whole(*kernel.shape)],
        [
            (high.shape, BF16, every_slot(rows, cols, channels)),
            ((64, channels), F32, result(64, channels)),
        ],
        [pltpu.VMEM(frame_shape, F32), pltpu.VMEM(frame_shape, F32)],
        flops=4 * slots * rows * cols * channels * KS * KS * 40,
    )


def from_both_sides(head, tail):
    count = lax.axis_size("strip")
    before = lax.ppermute(tail, "strip", [(i, i + 1) for i in range(count - 1)])
    after = lax.ppermute(head, "strip", [(i + 1, i) for i in range(count - 1)])
    return before, after


def bin_weights(edges, cell_count):
    cells = jnp.arange(cell_count, dtype=jnp.int32)
    inside = (cells[None, :] >= edges[:-1, None]) & (cells[None, :] < edges[1:, None])
    widths = (edges[1:] - edges[:-1]).astype(F32)
    return inside.astype(F32) / widths[:, None]


def strip_bins(edges, first_bin, bin_count, first_cell, cell_count):
    padded = jnp.concatenate([edges[:1], edges, edges[-1:]])
    window = lax.dynamic_slice_in_dim(padded, first_bin + 1, bin_count + 1)
    cells = first_cell + jnp.arange(cell_count, dtype=jnp.int32)
    inside = (cells[None, :] >= window[:-1, None]) & (cells[None, :] < window[1:, None])
    widths = jnp.maximum(window[1:] - window[:-1], 1).astype(F32)
    return inside.astype(F32) / widths[:, None]


def bit_of(axis, bit):
    return (lax.axis_index(axis) >> bit) & 1


def swap_halves(cells, axis, bit, own):
    size = lax.axis_size(axis)
    keep = lax.dynamic_index_in_dim(cells, own, 1, keepdims=False)
    send = lax.dynamic_index_in_dim(cells, 1 - own, 1, keepdims=False)
    got = lax.ppermute(send, axis, [(i, i ^ (1 << bit)) for i in range(size)])
    return (keep.astype(F32) + got.astype(F32)).astype(BF16)


def bits(axis):
    return int(math.log2(lax.axis_size(axis)))


def halve_dp(cells, base, bit):
    if cells.shape[0] % 2:
        cells = jnp.pad(cells, [(0, 1)] + [(0, 0)] * (cells.ndim - 1))
    own = (bit_of("dp", bit) - base) & 1
    cells = cells.reshape((cells.shape[0] // 2, 2) + cells.shape[1:])
    return swap_halves(cells, "dp", bit, own), (base + own) >> 1


def halve_strip(cells):
    for bit in range(bits("strip")):
        m, count = cells.shape[:2]
        cells = cells.reshape((m * count // 2, 2) + cells.shape[2:])
        cells = swap_halves(cells, "strip", bit, bit_of("strip", bit))
        cells = cells.reshape((m, count // 2) + cells.shape[1:])
    return cells


def shared_sum(matrix, offset, chunk, strip_first):
    strips = lax.axis_size("strip")
    rows, cols = matrix.shape
    chunk_rows = chunk // cols
    base = offset // (chunk * strips)
    front = (offset - base * chunk * strips) // cols
    groups = -(-(front + rows) // (chunk_rows * strips))
    back = groups * chunk_rows * strips - front - rows
    cells = jnp.pad(matrix, ((front, back), (0, 0))).reshape(groups, strips, chunk_rows, cols)
    cells, base = halve_dp(cells, base, 0)
    if strip_first:
        cells = halve_strip(cells)
        cells, base = halve_dp(cells, base, 1)
    else:
        cells, base = halve_dp(cells, base, 1)
        cells = halve_strip(cells)
    return cells.reshape(cells.shape[0], chunk), base


def owned_chunk(matrices, extras):
    data_count = lax.axis_size("dp")
    strips = lax.axis_size("strip")
    devices = data_count * strips
    total = sum(m.size for m in matrices)
    chunk = total // devices
    extra = extras.shape[0] // devices
    span = data_count // 4
    placed = None
    offset = 0
    for order, matrix in enumerate(matrices):
        part, base = shared_sum(matrix, offset, chunk, order % 2 == 0)
        canvas = jnp.zeros((span + part.shape[0], chunk), BF16)
        canvas = lax.dynamic_update_slice(canvas, part, (base, 0))[:span]
        placed = canvas if placed is None else placed + canvas
        offset += matrix.size
    for bit in range(2, bits("dp")):
        placed = placed.reshape(placed.shape[0] // 2, 2, chunk)
        placed = swap_halves(placed, "dp", bit, bit_of("dp", bit))
    mine = placed.reshape(chunk).astype(F32)
    index = lax.axis_index("dp") * strips + lax.axis_index("strip")
    pieces = [mine]
    left = extras.shape[0]
    padded = jnp.pad(extras, (0, chunk))
    for hop in range(1, -(-left // chunk) + 1):
        size = min(left, chunk)
        left -= size
        following = lax.ppermute(
            mine[:size].astype(BF16),
            ("dp", "strip"),
            [(i + hop, i) for i in range(devices - hop)],
        ).astype(F32)
        past = index + hop - devices
        own_extras = lax.dynamic_slice(padded, (jnp.maximum(past, 0) * chunk,), (size,))
        pieces.append(jnp.where(past >= 0, own_extras, following))
    return lax.dynamic_slice(jnp.concatenate(pieces), (index * extra,), (chunk + extra,))


def per_device(
    low_tokens,
    high_map,
    counts,
    row_edges,
    col_edges,
    w_qkv,
    w_attn_out,
    w_fc1,
    w_fc2,
    vit_gains,
    vit_shifts,
    w_pw1,
    w_pw2,
    w_pool,
    dw_kernel,
    conv_gains,
    conv_shifts,
    w_gate,
    d_merged,
    d_conv,
):
    slots, tok_rows, width = low_tokens.shape
    rows, cols, channels = high_map.shape[1:]
    cells = rows * cols
    strips = lax.axis_size("strip")
    strip = lax.axis_index("strip")
    live = counts[:1]

    col_bins = bin_weights(col_edges, cols)
    side = col_bins.shape[0]
    own_bins = tok_rows // side
    near_bins = strip_bins(row_edges, strip * own_bins - 1, own_bins + 2, strip * rows, rows)
    bins = (near_bins[:, None, :, None] * col_bins[None, :, None, :]).astype(BF16)
    bins = bins.reshape((own_bins + 2) * side, cells)

    def shifted(value, by):
        return lax.ppermute(value, "strip", [(i, (i + by) % strips) for i in range(strips)])

    tok_all = jnp.concatenate(
        [low_tokens] + [shifted(low_tokens, by) for by in range(1, strips)], axis=1
    )
    top, bottom = from_both_sides(high_map[:, :REACH], high_map[:, -REACH:])

    spatial, spatial_flip, conv_unit, conv_inverse = conv_front(
        live, top, high_map, bottom, dw_kernel, conv_gains, conv_shifts
    )
    act, slope, branch, high_out = conv_mlp(
        live, spatial, high_map.reshape(slots, cells, channels), w_pw1, w_pw2, conv_gains
    )
    own, before_part, after_part = pool(live, high_out, bins, side)
    first, last = from_both_sides(before_part, after_part)

    normed, q, kv, probs, mixed, residual, inner, inner_flip = vit_front(
        live, tok_all, w_qkv, w_attn_out, vit_gains, vit_shifts, tok_rows
    )
    low_out, d_inner, grad_fc1, grad_fc2 = vit_mlp(
        live, inner, inner_flip, d_merged, residual, w_fc1, w_fc2
    )
    merged, d_pooled, grad_pool, gate_sums = adapter(
        live, own, first, last, low_out, d_merged, w_pool, w_gate.reshape(1, channels)
    )
    near_before, near_after = from_both_sides(d_pooled[:, :side], d_pooled[:, -side:])
    d_post, d_branch, scale_sums = unpool(
        live,
        jnp.concatenate([near_before, d_pooled, near_after], axis=1),
        bins.T,
        d_conv.reshape(slots, cells, channels),
        branch,
        conv_gains,
    )
    grad_pw1, grad_pw2, d_spatial = conv_mlp_back(
        live, spatial_flip, act, slope, d_branch, w_pw1, w_pw2
    )
    d_conv_in, norm_sums = conv_norm_back(live, d_spatial, conv_unit, conv_inverse, conv_gains)
    d_conv_in = d_conv_in.reshape(high_map.shape)
    d_before, d_after = from_both_sides(d_conv_in[:, :REACH], d_conv_in[:, -REACH:])

    d_residual, d_mixed, grad_out, inner_sums = vit_back(
        live, residual, d_inner, d_merged, mixed, w_attn_out, vit_gains
    )
    d_q, d_k, d_v = attention_back(live, probs, q, kv, d_mixed)
    d_normed, grad_qkv = qkv_back(live, normed, d_q, d_k, d_v, w_qkv)
    arrived = jnp.zeros(low_tokens.shape, BF16)
    for by in range(1, strips):
        part = d_normed[:, by * tok_rows : (by + 1) * tok_rows].astype(BF16)
        arrived = arrived + shifted(part, -by) if by > 1 else shifted(part, -by)
    grad_tokens, token_sums = tokens_back(
        live, low_tokens, d_normed, arrived, d_residual, vit_gains
    )
    grad_map, kernel_sums = conv_back(
        live,
        top,
        high_map,
        bottom,
        d_before,
        d_conv_in,
        d_after,
        d_post.reshape(high_map.shape),
        dw_kernel,
    )

    vit_extras = jnp.concatenate([token_sums[0], inner_sums[0], token_sums[1], inner_sums[1]])
    conv_extras = jnp.concatenate(
        [
            kernel_sums[: KS * KS].reshape(-1),
            norm_sums[0],
            scale_sums[0],
            norm_sums[2],
            norm_sums[1],
            gate_sums[0],
        ]
    )
    extras = lax.psum(jnp.concatenate([vit_extras, conv_extras]), ("dp", "strip"))
    vit_grads = owned_chunk(
        [grad_qkv, grad_out, grad_fc1, grad_fc2], extras[: vit_extras.shape[0]]
    )
    conv_grads = owned_chunk([grad_pw1, grad_pw2, grad_pool], extras[vit_extras.shape[0] :])
    return (
        merged,
        high_out.reshape(high_map.shape),
        grad_tokens,
        grad_map,
        vit_grads,
        conv_grads,
    )


def solution(mesh):
    images = P("dp", "strip", None)
    maps = P("dp", "strip", None, None)
    flat = P(("dp", "strip"))
    in_specs = (images, maps, P("dp")) + (P(),) * 15 + (images, maps)
    out_specs = (images, maps, images, maps, flat, flat)
    return jax.shard_map(
        per_device, mesh=mesh, in_specs=in_specs, out_specs=out_specs, check_vma=False
    )
```

time: 3080 us -> 2050 us (0.67)
  other arithmetic: 1180 us -> 157 us
  matrix products: 734 us -> 0 us
  starting transfers between devices: 37.4 us -> 692 us
  waiting for transfers between devices: 748 us -> 323 us
  Pallas kernels: 0 us -> 299 us
  local copies, waits for them, and re-layouts: 354 us -> 544 us
    reduce_sum x15 -> x0, other arithmetic: 781 us -> none  [the longest x3 303 us: normed(): center = values - jnp.mean(values, axis=-1, keepdims=True)]
    all_to_all x2 -> x0, waiting for transfers between devices: 726 us -> none  [the longest x1 726 us: per_device(): lax.all_to_all(conv_blocks.astype(jnp.bfloat16), 'dp', split_axis=0, conc...]
    dot_general x30 -> x0, matrix products: 711 us -> none  [the longest x1 85.2 us: per_device(): jnp.einsum('iyxc,fc->iyxf', d_branch, w_pw2, preferred_element_type=jnp.f...]
    ppermute x8 -> x37, starting transfers between devices: 21 us -> 692 us  [the longest x25 660 us: swap_halves(): got = lax.ppermute(send, axis, [(i, i ^ 1 << bit) for i in range(size)])]
    dynamic_update_slice x0 -> x7, local copies, waits for them, and re-layouts: none -> 314 us  [owned_chunk(): canvas = lax.dynamic_update_slice(canvas, part, (base, 0))[:span]]
    ppermute x8 -> x37, waiting for transfers between devices: 22.3 us -> 323 us  [the longest x25 304 us: swap_halves(): got = lax.ppermute(send, axis, [(i, i ^ 1 << bit) for i in range(size)])]
    pallas_call x0 -> x14, Pallas kernels: none -> 299 us  [run(): pl.pallas_call(body, grid_spec=pltpu.PrefetchScalarGridSpec(num_scalar_pr...]
    convert_element_type x7 -> x17, other arithmetic: 334 us -> 86.8 us  [the longest x14 76 us: swap_halves(): return (keep.astype(F32) + got.astype(F32)).astype(BF16)]
  transfers between devices with their start and end apart: 13 -> 38, of which waited for: 7 -> 11; matrix products, arithmetic and copies ran while one was open for 57% -> 33% of each run, Pallas kernels for 0% -> 15%
where the time goes in v1:
time: 2050 us; the launch traced here: 2030 us
  starting transfers between devices  692 us (34%)
  local copies, waits for them, and re-layouts  544 us (27%)
  waiting for transfers between devices  323 us (16%)
  Pallas kernels  299 us (15%)
  other arithmetic  157 us (8%)
    ppermute x25, starting transfers between devices, swap_halves(): got = lax.ppermute(send, axis, [(i, i ^ 1 << bit) for i in range(size)])  660 us
    dynamic_update_slice x7, local copies, waits for them, and re-layouts, owned_chunk(): canvas = lax.dynamic_update_slice(canvas, part, (base, 0))[:span]  314 us
    ppermute x25, waiting for transfers between devices, swap_halves(): got = lax.ppermute(send, axis, [(i, i ^ 1 << bit) for i in range(size)])  304 us
    pallas_call x14, Pallas kernels, run(): pl.pallas_call(body, grid_spec=pltpu.PrefetchScalarGridSpec(num_scalar_pr...  299 us
    convert_element_type x14, other arithmetic, swap_halves(): return (keep.astype(F32) + got.astype(F32)).astype(BF16)  76 us
    squeeze x21, local copies, waits for them, and re-layouts, swap_halves(): send = lax.dynamic_index_in_dim(cells, 1 - own, 1, keepdims=False)  55.4 us
    pad x6, local copies, waits for them, and re-layouts, shared_sum(): jnp.pad(matrix, ((front, back), (0, 0)))  52.2 us
    unnamed x102, local copies, waits for them, and re-layouts  44.7 us
  transfers between devices with their start and end apart: 38, of which 11 were waited for; matrix products, arithmetic and copies ran while one was open for 33% of the time, Pallas kernels for 15%

profile of v1, /device:TPU:13, one launch (start us, length us, event | category | flops | bytes accessed | tf_op | source)
XLA Modules:
  0.0 2031.5 jit_solution(10168331184975247456)
XLA Ops:
  27.8 10.9 collective-permute-done.top_ref
  43.6 17.1 conv_front.1
  60.7 43.5 %conv_mlp.1 = (bf16[4,512,6144]{2,1,0:T(8,128)(2,1)}, bf16[4,512,6144]{2,1,0:T(8,128)(2,1)}, bf16[4,512,1536]{2,1,0:T(8,128)(2,1)}, bf16[4,512,1536]{2,1,0:T(8,128)(2,1)}) custom-call(s32[1]{0:T(128)S(6)} %copy.91.n, bf16[4,512,1536]{2,1,0:T(8,128)(2,1)} %get-tuple-element.54.x_ref, bf16[4,512,1536]{2,1,0:T(8,128)(2,1)} %bitcast.212, ...), custom_call_target="tpu_custom_call" | custom-call | flops 77309411328 | bytes 113258496 | tf_op jit(solution)/shard_map/conv_mlp/pallas_call | solution.py:114
  114.7 27.5 %vit_front.1 = (bf16[4,576,1024]{2,1,0:T(8,128)(2,1)}, bf16[4,288,1024]{2,1,0:T(8,128)(2,1)}, bf16[4,576,2048]{2,1,0:T(8,128)(2,1)}, bf16[4,16,576,288]{3,2,1,0:...) custom-call(s32[1]{0:T(128)S(6)} %copy.91.n, ...), custom_call_target="tpu_custom_call" | custom-call | flops 19931332608 | bytes 62668800 | tf_op jit(solution)/shard_map/vit_front/pallas_call | solution.py:114
  142.3 36.4 %vit_mlp.1 = (f32[4,288,1024]{2,1,0:T(8,128)}, f32[4,288,1024]{2,1,0:T(8,128)}, bf16[1024,4096]{1,0:T(8,128)(2,1)}, bf16[4096,1024]{1,0:T(8,128)(2,1)}) custom-call(s32[1]{0:T(128)S(6)} %copy.91.n, bf16[4,288,1024]{2,1,0:T(8,128)(2,1)} %get-tuple-element.59.x_ref, bf16[4,1024,288]{2,1,0:T(8,128)(2,1)} %get-tuple-element.60.xt_ref, ...), custom_call_target="tpu_custom_call" | custom-call | flops 57982058496 | bytes 54788096 | tf_op jit(solution)/shard_map/vit_mlp/pallas_call | solution.py:114
  178.6 8.4 vit_back.1
  187.0 18.7 attention_back.1
  205.8 16.9 qkv_back.1
  229.6 11.0 adapter.1
  247.1 8.2 pad.50
  269.8 8.2 pad.52
  294.1 5.9 unpool.1
  300.1 71.5 %conv_mlp_back.1 = (bf16[1536,6144]{1,0:T(8,128)(2,1)}, bf16[6144,1536]{1,0:T(8,128)(2,1)}, f32[4,512,1536]{2,1,0:T(8,128)}) custom-call(s32[1]{0:T(128)S(6)} %copy.91.n, bf16[4,1536,512]{2,1,0:T(8,128)(2,1)} %get-tuple-element.77.xt_ref, bf16[4,512,6144]{2,1,0:T(8,128)(2,1)} %get-tuple-element.78.act_ref, ...), custom_call_target="tpu_custom_call" | custom-call | flops 154618822656 | bytes 150994944 | tf_op jit(solution)/shard_map/conv_mlp_back/pallas_call | solution.py:114
  382.8 17.8 pad.55
  400.7 9.0 dynamic-slice_bitcast_fusion.1
  409.7 16.9 pad.56
  428.5 8.4 dynamic-slice_bitcast_fusion
  437.4 27.9 %conv_back.1 = (bf16[4,16,32,1536]{3,2,1,0:T(8,128)(2,1)}, f32[64,1536]{1,0:T(8,128)}) custom-call(s32[1]{0:T(128)S(6)} %copy.91.n, bf16[4,3,32,1536]{3,2,1,0:T(8,128)(2,1)} %collective-permute-done.top_ref, bf16[4,16,32,1536]{3,2,1,0:T(8,128)(2,1)} %mid_ref.3, bf16[4,3,32,1536]{3,2,1,0:T(8,128)(2,1)} %collective-permute-done.1.bottom_ref, ...), custom_call_target="tpu_custom_call" | custom-call | flops 24662507520 | bytes 30578688 | tf_op jit(solution)/shard_map/conv_back/pallas_call | solution.py:114
  471.0 368.7 %collective-permute-start.14 = (bf16[1,2,384,1024]{3,2,1,0:T(8,128)(2,1)}, bf16[1,2,384,1024]{3,2,1,0:T(8,128)(2,1)}, u32[]{:S(2)}, u32[]{:S(2)}) collective-permute-start(bf16[1,2,384,1024]{3,2,1,0:T(8,128)(2,1)} %pad_dynamic-slice_fusion), channel_id=1, source_target_pairs={{0,4},{2,6},{4,0},{6,2},{8,12},{10,14},{12,8},{14,10},{16,20},{18,... | collective-permute-start | bytes 4718600 | tf_op jit(solution)/shard_map/ppermute | solution.py:952
  852.1 22.6 %collective-permute-done.14 = bf16[1,2,384,1024]{3,2,1,0:T(8,128)(2,1)} collective-permute-done((bf16[1,2,384,1024]{3,2,1,0:T(8,128)(2,1)}, bf16[1,2,384,1024]{3,2,1,0:T(8,128)(2,1)}, u32[]{:S(2)}, u32[]{:S(2)}) %collective-permute-start.14) | collective-permute-done | bytes 1572896 | tf_op jit(solution)/shard_map/ppermute | solution.py:952
  889.1 6.4 fusion.5
  898.9 7.4 collective-permute-done.32
  930.8 28.9 %dynamic_update_slice.22 = bf16[5,393216]{1,0:T(8,128)(2,1)} dynamic-update-slice(bf16[5,393216]{1,0:T(8,128)(2,1)} %broadcast.119.clone, bf16[1,393216]{1,0:T(2,128)(2,1)} %bitcast.201, s32[]{:T(128)S(6)} %select_n.198, s32[]{:T(128)} %constant.212.clone.1) | dynamic-update-slice | bytes 1572868 | tf_op jit(solution)/shard_map/dynamic_update_slice | solution.py:1009
  962.8 44.6 %collective-permute-done.17 = bf16[3,96,4096]{2,1,0:T(8,128)(2,1)} collective-permute-done((bf16[3,96,4096]{2,1,0:T(8,128)(2,1)}, bf16[3,96,4096]{2,1,0:T(8,128)(2,1)}, u32[]{:S(2)}, u32[]{:S(2)}) %collective-permute-start.17) | collective-permute-done | bytes 2359328 | tf_op jit(solution)/shard_map/ppermute | solution.py:952
  1013.4 5.9 collective-permute-done.33
  1029.1 46.1 %dynamic_update_slice.27 = bf16[5,638976]{1,0:T(8,128)(2,1)} dynamic-update-slice(bf16[5,638976]{1,0:T(8,128)(2,1)} %broadcast_in_dim.2, bf16[1,638976]{1,0:T(2,128)(2,1)} %bitcast.200, s32[]{:T(128)S(6)} %select_n.227, s32[]{:T(128)} %constant.212.clone.1) | dynamic-update-slice | bytes 2555908 | tf_op jit(solution)/shard_map/dynamic_update_slice | solution.py:1009
  1089.0 29.2 %dynamic_update_slice.21 = bf16[5,393216]{1,0:T(8,128)(2,1)} dynamic-update-slice(bf16[5,393216]{1,0:T(8,128)(2,1)} %broadcast.119.clone.1, bf16[1,393216]{1,0:T(2,128)(2,1)} %bitcast.202, s32[]{:T(128)S(6)} %select_n.193, s32[]{:T(128)} %constant.212.clone.1) | dynamic-update-slice | bytes 1572868 | tf_op jit(solution)/shard_map/dynamic_update_slice | solution.py:1009
  1125.8 50.9 %dynamic_update_slice.23 = bf16[6,393216]{1,0:T(8,128)(2,1)} dynamic-update-slice(bf16[6,393216]{1,0:T(8,128)(2,1)} %broadcast.120.clone.1, bf16[2,393216]{1,0:T(2,128)(2,1)} %bitcast.203, s32[]{:T(128)S(6)} %select_n.203, s32[]{:T(128)} %constant.212.clone.1) | dynamic-update-slice | bytes 3145732 | tf_op jit(solution)/shard_map/dynamic_update_slice | solution.py:1009
  1183.3 37.6 %dynamic_update_slice.24 = bf16[6,393216]{1,0:T(8,128)(2,1)} dynamic-update-slice(bf16[6,393216]{1,0:T(8,128)(2,1)} %broadcast.120.clone, bf16[2,393216]{1,0:T(2,128)(2,1)S(1)} %bitcast.204, s32[]{:T(128)S(6)} %select_n.208, s32[]{:T(128)} %constant.212.clone.1) | dynamic-update-slice | bytes 3145732 | tf_op jit(solution)/shard_map/dynamic_update_slice | solution.py:1009
  1220.9 10.7 slice_add_fusion.2
  1235.0 12.5 fusion
  1247.5 8.5 constant_dynamic-slice_fusion.3
  1259.0 8.6 fusion.1
  1270.6 6.7 constant_dynamic-slice_fusion.5
  1283.1 82.2 %collective-permute-done.29 = bf16[2,2,416,1536]{3,2,0,1:T(8,128)(2,1)} collective-permute-done((bf16[2,2,416,1536]{3,2,0,1:T(8,128)(2,1)S(1)}, bf16[2,2,416,1536]{3,2,0,1:T(8,128)(2,1)}, u32[]{:S(2)}, u32[]{:S(2)}) %collective-permute-start.29) | collective-permute-done | bytes 5111840 | tf_op jit(solution)/shard_map/ppermute | solution.py:952
  1383.1 7.1 fusion.13
  1390.2 41.5 %collective-permute-done.30 = bf16[2,416,1536]{2,1,0:T(8,128)(2,1)} collective-permute-done((bf16[2,416,1536]{2,1,0:T(8,128)(2,1)}, bf16[2,416,1536]{2,1,0:T(8,128)(2,1)}, u32[]{:S(2)}, u32[]{:S(2)}) %collective-permute-start.30) | collective-permute-done | bytes 2555936 | tf_op jit(solution)/shard_map/ppermute | solution.py:952
  1447.5 60.6 %dynamic_update_slice.26 = bf16[6,638976]{1,0:T(8,128)(2,1)} dynamic-update-slice(bf16[6,638976]{1,0:T(8,128)(2,1)} %broadcast.121.clone, bf16[2,638976]{1,0:T(2,128)(2,1)S(1)} %bitcast.198, s32[]{:T(128)S(6)} %select_n.222, s32[]{:T(128)} %constant.212.clone.1) | dynamic-update-slice | bytes 5111812 | tf_op jit(solution)/shard_map/dynamic_update_slice | solution.py:1009
  1512.5 60.5 %dynamic_update_slice.25 = bf16[6,638976]{1,0:T(8,128)(2,1)} dynamic-update-slice(bf16[6,638976]{1,0:T(8,128)(2,1)} %broadcast.121.clone.1, bf16[2,638976]{1,0:T(2,128)(2,1)S(1)} %bitcast.199, s32[]{:T(128)S(6)} %select_n.217, s32[]{:T(128)} %constant.212.clone.1) | dynamic-update-slice | bytes 5111812 | tf_op jit(solution)/shard_map/dynamic_update_slice | solution.py:1009
  1573.1 12.9 slice_add_fusion
  1586.0 7.2 reshape.379
  1593.2 11.2 constant_dynamic-slice_fusion.1
  1604.4 8.8 copy.64
  1615.0 187.0 %collective-permute-start.23 = (bf16[1,393216]{1,0:T(2,128)(2,1)S(1)}, bf16[1,393216]{1,0:T(2,128)(2,1)S(1)}, u32[]{:S(2)}, u32[]{:S(2)}) collective-permute-start(bf16[1,393216]{1,0:T(2,128)(2,1)S(1)} %constant_dynamic-slice_fusion.4), channel_id=1, source_target_pairs={{0,16},{2,18},{4,20},{6,22},{8,24},{10,26},{12,28},{14,30},{16,0},... | collective-permute-start | bytes 2359304 | tf_op jit(solution)/shard_map/ppermute | solution.py:952
  1802.1 8.0 fusion.8
  1814.0 83.5 %collective-permute-start.35 = (bf16[1,638976]{1,0:T(2,128)(2,1)}, bf16[1,638976]{1,0:T(2,128)(2,1)}, u32[]{:S(2)}, u32[]{:S(2)}) collective-permute-start(bf16[1,638976]{1,0:T(2,128)(2,1)} %constant_dynamic-slice_fusion), channel_id=1, source_target_pairs={{0,16},{2,18},{4,20},{6,22},{8,24},{10,26},{12,28},{14,30},{16,0},... | collective-permute-start | bytes 3833864 | tf_op jit(solution)/shard_map/ppermute | solution.py:952
  1901.2 7.7 collective-permute-start.24
  1909.7 97.1 %collective-permute-done.35 = bf16[1,638976]{1,0:T(2,128)(2,1)} collective-permute-done((bf16[1,638976]{1,0:T(2,128)(2,1)}, bf16[1,638976]{1,0:T(2,128)(2,1)}, u32[]{:S(2)}, u32[]{:S(2)}) %collective-permute-start.35) | collective-permute-done | bytes 1277984 | tf_op jit(solution)/shard_map/ppermute | solution.py:952
  (260 shorter events, 280.6 us)
Async XLA Ops:
  7.2 1901.7 %all-reduce.14.cloned.1.call-start = ((), (), s32[]{:S(2)}) async-start(), calls=%async_computation | async-start | bytes 696320 | tf_op jit(solution)/shard_map/psum | solution.py:1147
  10.7 28.0 %collective-permute-start = (bf16[4,3,32,1536]{3,2,1,0:T(8,128)(2,1)}, bf16[4,3,32,1536]{3,2,1,0:T(8,128)(2,1)}, u32[]{:S(2)}, u32[]{:S(2)}) collective-permute-start(bf16[4,3,32,1536]{3,2,1,0:T(8,128)(2,1)} %get-tuple-element.116), channel_id=1, source_target_pairs={{0,1},{2,3},{4,5},{6,7},{8,9},{10,11},{12,13},{14,15},{16,17},{18,... | collective-permute-start | bytes 3538952 | tf_op jit(solution)/shard_map/ppermute | solution.py:923
  14.8 28.7 %collective-permute-start.1 = (bf16[4,3,32,1536]{3,2,1,0:T(8,128)(2,1)}, bf16[4,3,32,1536]{3,2,1,0:T(8,128)(2,1)}, u32[]{:S(2)}, u32[]{:S(2)}) collective-permute-start(bf16[4,3,32,1536]{3,2,1,0:T(8,128)(2,1)} %get-tuple-element.115), channel_id=1, source_target_pairs={{1,0},{3,2},{5,4},{7,6},{9,8},{11,10},{13,12},{15,14},{17,16},{19,... | collective-permute-start | bytes 3538952 | tf_op jit(solution)/shard_map/ppermute | solution.py:924
  16.1 94.2 %collective-permute-start.4 = (bf16[4,288,1024]{2,1,0:T(8,128)(2,1)S(1)}, bf16[4,288,1024]{2,1,0:T(8,128)(2,1)}, u32[]{:S(2)}, u32[]{:S(2)}) collective-permute-start(bf16[4,288,1024]{2,1,0:T(8,128)(2,1)S(1)} %copy-done.17), channel_id=1, source_target_pairs={{0,1},{1,0},{2,3},{3,2},{4,5},{5,4},{6,7},{7,6},{8,9},{9,8},{10,11... | collective-permute-start | bytes 7077896 | tf_op jit(solution)/shard_map/ppermute | solution.py:1071
  26.2 34.5 %copy-start.26 = (bf16[336,512]{1,0:T(8,128)(2,1)}, bf16[336,512]{1,0:T(8,128)(2,1)S(1)}, u32[]{:S(2)}) copy-start(bf16[336,512]{1,0:T(8,128)(2,1)S(1)} %convert_element_type.435.p_ref) | copy-start | bytes 1032196
  107.7 121.1 %collective-permute-start.2 = (bf16[4,24,1536]{2,1,0:T(8,128)(2,1)}, bf16[4,24,1536]{2,1,0:T(8,128)(2,1)S(1)}, u32[]{:S(2)}, u32[]{:S(2)}) collective-permute-start(bf16[4,24,1536]{2,1,0:T(8,128)(2,1)} %get-tuple-element.57), channel_id=1, source_target_pairs={{0,1},{2,3},{4,5},{6,7},{8,9},{10,11},{12,13},{14,15},{16,17},{18,... | collective-permute-start | bytes 884744 | tf_op jit(solution)/shard_map/ppermute | solution.py:923
  109.1 119.8 %collective-permute-start.3 = (bf16[4,24,1536]{2,1,0:T(8,128)(2,1)}, bf16[4,24,1536]{2,1,0:T(8,128)(2,1)S(1)}, u32[]{:S(2)}, u32[]{:S(2)}) collective-permute-start(bf16[4,24,1536]{2,1,0:T(8,128)(2,1)} %get-tuple-element.58), channel_id=1, source_target_pairs={{1,0},{3,2},{5,4},{7,6},{9,8},{11,10},{13,12},{15,14},{17,16},{19,... | collective-permute-start | bytes 884744 | tf_op jit(solution)/shard_map/ppermute | solution.py:924
  226.7 244.3 %collective-permute-start.5 = (bf16[4,288,1024]{2,1,0:T(8,128)(2,1)}, bf16[4,288,1024]{2,1,0:T(8,128)(2,1)}, u32[]{:S(2)}, u32[]{:S(2)}) collective-permute-start(bf16[4,288,1024]{2,1,0:T(8,128)(2,1)} %slice.184), channel_id=1, source_target_pairs={{0,1},{1,0},{2,3},{3,2},{4,5},{5,4},{6,7},{7,6},{8,9},{9,8},{10,11... | collective-permute-start | bytes 7077896 | tf_op jit(solution)/shard_map/ppermute | solution.py:1071
  241.8 49.3 %collective-permute-start.7 = (bf16[4,24,1536]{2,1,0:T(8,128)(2,1)S(1)}, bf16[4,24,1536]{2,1,0:T(8,128)(2,1)S(1)}, u32[]{:S(2)}, u32[]{:S(2)}) collective-permute-start(bf16[4,24,1536]{2,1,0:T(8,128)(2,1)S(1)} %get-tuple-element.120), channel_id=1, source_target_pairs={{1,0},{3,2},{5,4},{7,6},{9,8},{11,10},{13,12},{15,14},{17,16},{19,... | collective-permute-start | bytes 884744 | tf_op jit(solution)/shard_map/ppermute | solution.py:924
  243.1 48.0 %collective-permute-start.6 = (bf16[4,24,1536]{2,1,0:T(8,128)(2,1)S(1)}, bf16[4,24,1536]{2,1,0:T(8,128)(2,1)S(1)}, u32[]{:S(2)}, u32[]{:S(2)}) collective-permute-start(bf16[4,24,1536]{2,1,0:T(8,128)(2,1)S(1)} %get-tuple-element.119), channel_id=1, source_target_pairs={{0,1},{2,3},{4,5},{6,7},{8,9},{10,11},{12,13},{14,15},{16,17},{18,... | collective-permute-start | bytes 884744 | tf_op jit(solution)/shard_map/ppermute | solution.py:923
  260.5 626.3 %collective-permute-start.16 = (bf16[3,2,96,4096]{3,2,1,0:T(8,128)(2,1)}, bf16[3,2,96,4096]{3,2,1,0:T(8,128)(2,1)}, u32[]{:S(2)}, u32[]{:S(2)}) collective-permute-start(bf16[3,2,96,4096]{3,2,1,0:T(8,128)(2,1)} %dynamic-slice_bitcast_fusion.4), channel_id=1, source_target_pairs={{0,2},{2,0},{4,6},{6,4},{8,10},{10,8},{12,14},{14,12},{16,18},{18,... | collective-permute-start | bytes 14155784 | tf_op jit(solution)/shard_map/ppermute | solution.py:952
  268.4 198.0 %collective-permute-start.13 = (bf16[1,2,384,1024]{3,2,1,0:T(8,128)(2,1)}, bf16[1,2,384,1024]{3,2,1,0:T(8,128)(2,1)}, u32[]{:S(2)}, u32[]{:S(2)}) collective-permute-start(bf16[1,2,384,1024]{3,2,1,0:T(8,128)(2,1)} %dynamic-slice_bitcast_fusion.12), channel_id=1, source_target_pairs={{0,2},{2,0},{4,6},{6,4},{8,10},{10,8},{12,14},{14,12},{16,18},{18,... | collective-permute-start | bytes 4718600 | tf_op jit(solution)/shard_map/ppermute | solution.py:952
  379.2 57.6 %collective-permute-start.8 = (bf16[4,3,32,1536]{3,2,1,0:T(8,128)(2,1)S(1)}, bf16[4,3,32,1536]{3,2,1,0:T(8,128)(2,1)}, u32[]{:S(2)}, u32[]{:S(2)}) collective-permute-start(bf16[4,3,32,1536]{3,2,1,0:T(8,128)(2,1)S(1)} %get-tuple-element.114), channel_id=1, source_target_pairs={{0,1},{2,3},{4,5},{6,7},{8,9},{10,11},{12,13},{14,15},{16,17},{18,... | collective-permute-start | bytes 3538952 | tf_op jit(solution)/shard_map/ppermute | solution.py:923
  381.6 55.8 %collective-permute-start.9 = (bf16[4,3,32,1536]{3,2,1,0:T(8,128)(2,1)S(1)}, bf16[4,3,32,1536]{3,2,1,0:T(8,128)(2,1)}, u32[]{:S(2)}, u32[]{:S(2)}) collective-permute-start(bf16[4,3,32,1536]{3,2,1,0:T(8,128)(2,1)S(1)} %get-tuple-element.113), channel_id=1, source_target_pairs={{1,0},{3,2},{5,4},{7,6},{9,8},{11,10},{13,12},{15,14},{17,16},{19,... | collective-permute-start | bytes 3538952 | tf_op jit(solution)/shard_map/ppermute | solution.py:924
  436.8 443.5 %collective-permute-start.10 = (bf16[2,2,128,3072]{3,2,1,0:T(8,128)(2,1)}, bf16[2,2,128,3072]{3,2,1,0:T(8,128)(2,1)}, u32[]{:S(2)}, u32[]{:S(2)}) collective-permute-start(bf16[2,2,128,3072]{3,2,1,0:T(8,128)(2,1)} %dynamic-slice_bitcast_fusion.5), channel_id=1, source_target_pairs={{0,2},{2,0},{4,6},{6,4},{8,10},{10,8},{12,14},{14,12},{16,18},{18,... | collective-permute-start | bytes 9437192 | tf_op jit(solution)/shard_map/ppermute | solution.py:952
  437.3 409.3 %collective-permute-start.31 = (bf16[1,2,624,1024]{3,2,1,0:T(8,128)(2,1)}, bf16[1,2,624,1024]{3,2,1,0:T(8,128)(2,1)}, u32[]{:S(2)}, u32[]{:S(2)}) collective-permute-start(bf16[1,2,624,1024]{3,2,1,0:T(8,128)(2,1)} %dynamic-slice_bitcast_fusion.6), channel_id=1, source_target_pairs={{0,2},{2,0},{4,6},{6,4},{8,10},{10,8},{12,14},{14,12},{16,18},{18,... | collective-permute-start | bytes 7667720 | tf_op jit(solution)/shard_map/ppermute | solution.py:952
  466.3 444.4 %collective-permute-start.19 = (bf16[3,2,384,1024]{3,2,1,0:T(8,128)(2,1)}, bf16[3,2,384,1024]{3,2,1,0:T(8,128)(2,1)}, u32[]{:S(2)}, u32[]{:S(2)}) collective-permute-start(bf16[3,2,384,1024]{3,2,1,0:T(8,128)(2,1)} %dynamic-slice_bitcast_fusion.3), channel_id=1, source_target_pairs={{0,2},{2,0},{4,6},{6,4},{8,10},{10,8},{12,14},{14,12},{16,18},{18,... | collective-permute-start | bytes 14155784 | tf_op jit(solution)/shard_map/ppermute | solution.py:952
  471.0 403.7 %collective-permute-start.14 = (bf16[1,2,384,1024]{3,2,1,0:T(8,128)(2,1)}, bf16[1,2,384,1024]{3,2,1,0:T(8,128)(2,1)}, u32[]{:S(2)}, u32[]{:S(2)}) collective-permute-start(bf16[1,2,384,1024]{3,2,1,0:T(8,128)(2,1)} %pad_dynamic-slice_fusion), channel_id=1, source_target_pairs={{0,4},{2,6},{4,0},{6,2},{8,12},{10,14},{12,8},{14,10},{16,20},{18,... | collective-permute-start | bytes 4718600 | tf_op jit(solution)/shard_map/ppermute | solution.py:952
  846.6 388.4 %collective-permute-start.28 = (bf16[4,2,416,1536]{3,2,1,0:T(8,128)(2,1)}, bf16[4,2,416,1536]{3,2,1,0:T(8,128)(2,1)}, u32[]{:S(2)}, u32[]{:S(2)}) collective-permute-start(bf16[4,2,416,1536]{3,2,1,0:T(8,128)(2,1)} %dynamic-slice_bitcast_fusion), channel_id=1, source_target_pairs={{0,2},{2,0},{4,6},{6,4},{8,10},{10,8},{12,14},{14,12},{16,18},{18,... | collective-permute-start | bytes 30670856 | tf_op jit(solution)/shard_map/ppermute | solution.py:952
  847.0 42.0 %slice-start.3 = ((s8[9437184]{0:T(1024)(128)(4,1)}), s8[4194304]{0:T(1024)(128)(4,1)S(1)}, s32[]{:S(2)}) async-start(s8[9437184]{0:T(1024)(128)(4,1)} %bitcast.185), calls=%async_computation.4 | async-start | bytes 8388608
  850.9 29.4 %copy-start.15 = (bf16[1,2,624,1024]{3,2,1,0:T(8,128)(2,1)}, bf16[1,2,624,1024]{3,2,1,0:T(8,128)(2,1)S(1)}, u32[]{:S(2)}) copy-start(bf16[1,2,624,1024]{3,2,1,0:T(8,128)(2,1)S(1)} %fusion.9) | copy-start | bytes 7667716
  850.9 38.2 %slice-start.4 = ((s8[9437184]{0:T(1024)(128)(4,1)}), s8[4194304]{0:T(1024)(128)(4,1)S(1)}, s32[]{:S(2)}) async-start(s8[9437184]{0:T(1024)(128)(4,1)} %bitcast.185), calls=%async_computation.5 | async-start | bytes 8388608
  874.7 31.6 %collective-permute-start.32 = (bf16[1,624,1024]{2,1,0:T(8,128)(2,1)}, bf16[1,624,1024]{2,1,0:T(8,128)(2,1)}, u32[]{:S(2)}, u32[]{:S(2)}) collective-permute-start(bf16[1,624,1024]{2,1,0:T(8,128)(2,1)} %dynamic-slice_bitcast_fusion.14), channel_id=1, source_target_pairs={{0,1},{1,0},{2,3},{3,2},{4,5},{5,4},{6,7},{7,6},{8,9},{9,8},{10,11... | collective-permute-start | bytes 3833864 | tf_op jit(solution)/shard_map/ppermute | solution.py:952
  881.4 42.1 %collective-permute-start.15 = (bf16[1,384,1024]{2,1,0:T(8,128)(2,1)S(1)}, bf16[1,384,1024]{2,1,0:T(8,128)(2,1)S(1)}, u32[]{:S(2)}, u32[]{:S(2)}) collective-permute-start(bf16[1,384,1024]{2,1,0:T(8,128)(2,1)S(1)} %dynamic-slice_bitcast_fusion.15), channel_id=1, source_target_pairs={{0,1},{1,0},{2,3},{3,2},{4,5},{5,4},{6,7},{7,6},{8,9},{9,8},{10,11... | collective-permute-start | bytes 2359304 | tf_op jit(solution)/shard_map/ppermute | solution.py:952
  887.6 72.2 %collective-permute-start.11 = (bf16[2,128,3072]{2,1,0:T(8,128)(2,1)}, bf16[2,128,3072]{2,1,0:T(8,128)(2,1)}, u32[]{:S(2)}, u32[]{:S(2)}) collective-permute-start(bf16[2,128,3072]{2,1,0:T(8,128)(2,1)} %dynamic-slice_bitcast_fusion.13), channel_id=1, source_target_pairs={{0,1},{1,0},{2,3},{3,2},{4,5},{5,4},{6,7},{7,6},{8,9},{9,8},{10,11... | collective-permute-start | bytes 4718600 | tf_op jit(solution)/shard_map/ppermute | solution.py:952
  889.0 24.5 %slice-start = ((s8[9437184]{0:T(1024)(128)(4,1)}), s8[4194304]{0:T(1024)(128)(4,1)S(1)}, s32[]{:S(2)}) async-start(s8[9437184]{0:T(1024)(128)(4,1)} %bitcast.181), calls=%async_computation.1 | async-start | bytes 8388608
  906.3 101.1 %collective-permute-start.17 = (bf16[3,96,4096]{2,1,0:T(8,128)(2,1)}, bf16[3,96,4096]{2,1,0:T(8,128)(2,1)}, u32[]{:S(2)}, u32[]{:S(2)}) collective-permute-start(bf16[3,96,4096]{2,1,0:T(8,128)(2,1)} %dynamic-slice_bitcast_fusion.9), channel_id=1, source_target_pairs={{0,1},{1,0},{2,3},{3,2},{4,5},{5,4},{6,7},{7,6},{8,9},{9,8},{10,11... | collective-permute-start | bytes 7077896 | tf_op jit(solution)/shard_map/ppermute | solution.py:952
  910.7 348.3 %collective-permute-start.25 = (bf16[4,2,104,6144]{3,2,1,0:T(8,128)(2,1)}, bf16[4,2,104,6144]{3,2,1,0:T(8,128)(2,1)}, u32[]{:S(2)}, u32[]{:S(2)}) collective-permute-start(bf16[4,2,104,6144]{3,2,1,0:T(8,128)(2,1)} %dynamic-slice_bitcast_fusion.1), channel_id=1, source_target_pairs={{0,2},{2,0},{4,6},{6,4},{8,10},{10,8},{12,14},{14,12},{16,18},{18,... | collective-permute-start | bytes 30670856 | tf_op jit(solution)/shard_map/ppermute | solution.py:952
  923.5 151.8 %collective-permute-start.20 = (bf16[2,2,384,1024]{3,2,0,1:T(8,128)(2,1)}, bf16[2,2,384,1024]{3,2,0,1:T(8,128)(2,1)}, u32[]{:S(2)}, u32[]{:S(2)}) collective-permute-start(bf16[2,2,384,1024]{3,2,0,1:T(8,128)(2,1)} %bitcast.172), channel_id=1, source_target_pairs={{0,4},{2,6},{4,0},{6,2},{8,12},{10,14},{12,8},{14,10},{16,20},{18,... | collective-permute-start | bytes 9437192 | tf_op jit(solution)/shard_map/ppermute | solution.py:952
  930.8 29.0 %copy-start.7 = (bf16[2,2,128,3072]{3,2,1,0:T(8,128)(2,1)S(1)}, bf16[2,2,128,3072]{3,2,1,0:T(8,128)(2,1)}, u32[]{:S(2)}) copy-start(bf16[2,2,128,3072]{3,2,1,0:T(8,128)(2,1)} %copy-done.6) | copy-start | bytes 9437188
  959.8 59.5 %collective-permute-start.33 = (bf16[1,1,624,1024]{3,2,1,0:T(8,128)(2,1)}, bf16[1,1,624,1024]{3,2,1,0:T(8,128)(2,1)S(1)}, u32[]{:S(2)}, u32[]{:S(2)}) collective-permute-start(bf16[1,1,624,1024]{3,2,1,0:T(8,128)(2,1)} %pad_dynamic-slice_fusion.2), channel_id=1, source_target_pairs={{0,4},{2,6},{4,0},{6,2},{8,12},{10,14},{12,8},{14,10},{16,20},{18,... | collective-permute-start | bytes 3833864 | tf_op jit(solution)/shard_map/ppermute | solution.py:952
  961.8 45.6 %copy-start.20 = (bf16[2,128,3072]{2,1,0:T(8,128)(2,1)}, bf16[2,128,3072]{2,1,0:T(8,128)(2,1)S(1)}, u32[]{:S(2)}) copy-start(bf16[2,128,3072]{2,1,0:T(8,128)(2,1)S(1)} %fusion.17) | copy-start | bytes 4718596
  1007.4 73.5 %collective-permute-start.12 = (bf16[1,1,128,3072]{3,2,1,0:T(8,128)(2,1)}, bf16[1,1,128,3072]{3,2,1,0:T(8,128)(2,1)}, u32[]{:S(2)}, u32[]{:S(2)}) collective-permute-start(bf16[1,1,128,3072]{3,2,1,0:T(8,128)(2,1)} %dynamic-slice_bitcast_fusion.16), channel_id=1, source_target_pairs={{0,4},{2,6},{4,0},{6,2},{8,12},{10,14},{12,8},{14,10},{16,20},{18,... | collective-permute-start | bytes 2359304 | tf_op jit(solution)/shard_map/ppermute | solution.py:952
  1019.3 98.9 %collective-permute-start.18 = (bf16[2,1,96,4096]{3,2,0,1:T(8,128)(2,1)}, bf16[2,1,96,4096]{3,2,0,1:T(8,128)(2,1)}, u32[]{:S(2)}, u32[]{:S(2)}) collective-permute-start(bf16[2,1,96,4096]{3,2,0,1:T(8,128)(2,1)} %dynamic-slice_bitcast_fusion.11), channel_id=1, source_target_pairs={{0,4},{2,6},{4,0},{6,2},{8,12},{10,14},{12,8},{14,10},{16,20},{18,... | collective-permute-start | bytes 4718600 | tf_op jit(solution)/shard_map/ppermute | solution.py:952
  1081.0 95.8 %collective-permute-start.21 = (bf16[2,384,1024]{2,1,0:T(8,128)(2,1)}, bf16[2,384,1024]{2,1,0:T(8,128)(2,1)}, u32[]{:S(2)}, u32[]{:S(2)}) collective-permute-start(bf16[2,384,1024]{2,1,0:T(8,128)(2,1)} %dynamic-slice_bitcast_fusion.10), channel_id=1, source_target_pairs={{0,1},{1,0},{2,3},{3,2},{4,5},{5,4},{6,7},{7,6},{8,9},{9,8},{10,11... | collective-permute-start | bytes 4718600 | tf_op jit(solution)/shard_map/ppermute | solution.py:952
  1125.8 50.9 %copy-start.9 = (bf16[2,2,384,1024]{3,2,0,1:T(8,128)(2,1)S(1)}, bf16[2,2,384,1024]{3,2,0,1:T(8,128)(2,1)}, u32[]{:S(2)}) copy-start(bf16[2,2,384,1024]{3,2,0,1:T(8,128)(2,1)} %copy-done.8) | copy-start | bytes 9437188
  1258.9 106.5 %collective-permute-start.29 = (bf16[2,2,416,1536]{3,2,0,1:T(8,128)(2,1)S(1)}, bf16[2,2,416,1536]{3,2,0,1:T(8,128)(2,1)}, u32[]{:S(2)}, u32[]{:S(2)}) collective-permute-start(bf16[2,2,416,1536]{3,2,0,1:T(8,128)(2,1)S(1)} %bitcast.209), channel_id=1, source_target_pairs={{0,4},{2,6},{4,0},{6,2},{8,12},{10,14},{12,8},{14,10},{16,20},{18,... | collective-permute-start | bytes 15335432 | tf_op jit(solution)/shard_map/ppermute | solution.py:952
  1270.4 106.4 %collective-permute-start.26 = (bf16[4,104,6144]{2,1,0:T(8,128)(2,1)}, bf16[4,104,6144]{2,1,0:T(8,128)(2,1)}, u32[]{:S(2)}, u32[]{:S(2)}) collective-permute-start(bf16[4,104,6144]{2,1,0:T(8,128)(2,1)} %dynamic-slice_bitcast_fusion.2), channel_id=1, source_target_pairs={{0,1},{1,0},{2,3},{3,2},{4,5},{5,4},{6,7},{7,6},{8,9},{9,8},{10,11... | collective-permute-start | bytes 15335432 | tf_op jit(solution)/shard_map/ppermute | solution.py:952
  1283.1 99.7 %collective-permute-start.22 = (bf16[2,393216]{1,0:T(2,128)(2,1)}, bf16[2,393216]{1,0:T(2,128)(2,1)}, u32[]{:S(2)}, u32[]{:S(2)}) collective-permute-start(bf16[2,393216]{1,0:T(2,128)(2,1)} %bitcast.174), channel_id=1, source_target_pairs={{0,8},{2,10},{4,12},{6,14},{8,0},{10,2},{12,4},{14,6},{16,24},{18,... | collective-permute-start | bytes 4718600 | tf_op jit(solution)/shard_map/ppermute | solution.py:952
  1372.5 59.1 %collective-permute-start.30 = (bf16[2,416,1536]{2,1,0:T(8,128)(2,1)}, bf16[2,416,1536]{2,1,0:T(8,128)(2,1)}, u32[]{:S(2)}, u32[]{:S(2)}) collective-permute-start(bf16[2,416,1536]{2,1,0:T(8,128)(2,1)} %dynamic-slice_bitcast_fusion.7), channel_id=1, source_target_pairs={{0,1},{1,0},{2,3},{3,2},{4,5},{5,4},{6,7},{7,6},{8,9},{9,8},{10,11... | collective-permute-start | bytes 7667720 | tf_op jit(solution)/shard_map/ppermute | solution.py:952
  1381.4 56.8 %collective-permute-start.27 = (bf16[2,1,104,6144]{3,2,0,1:T(8,128)(2,1)S(1)}, bf16[2,1,104,6144]{3,2,0,1:T(8,128)(2,1)S(1)}, u32[]{:S(2)}, u32[]{:S(2)}) collective-permute-start(bf16[2,1,104,6144]{3,2,0,1:T(8,128)(2,1)S(1)} %dynamic-slice_bitcast_fusion.8), channel_id=1, source_target_pairs={{0,4},{2,6},{4,0},{6,2},{8,12},{10,14},{12,8},{14,10},{16,20},{18,... | collective-permute-start | bytes 7667720 | tf_op jit(solution)/shard_map/ppermute | solution.py:952
  1383.1 48.5 %copy-start.3 = (bf16[2,2,416,1536]{3,2,0,1:T(8,128)(2,1)S(1)}, bf16[2,2,416,1536]{3,2,0,1:T(8,128)(2,1)}, u32[]{:S(2)}) copy-start(bf16[2,2,416,1536]{3,2,0,1:T(8,128)(2,1)} %copy-done.2) | copy-start | bytes 15335428
  1613.2 188.8 %collective-permute-start.34 = (bf16[2,638976]{1,0:T(2,128)(2,1)S(1)}, bf16[2,638976]{1,0:T(2,128)(2,1)S(1)}, u32[]{:S(2)}, u32[]{:S(2)}) collective-permute-start(bf16[2,638976]{1,0:T(2,128)(2,1)S(1)} %bitcast.210), channel_id=1, source_target_pairs={{0,8},{2,10},{4,12},{6,14},{8,0},{10,2},{12,4},{14,6},{16,24},{18,... | collective-permute-start | bytes 7667720 | tf_op jit(solution)/shard_map/ppermute | solution.py:952
  1615.0 282.5 %collective-permute-start.23 = (bf16[1,393216]{1,0:T(2,128)(2,1)S(1)}, bf16[1,393216]{1,0:T(2,128)(2,1)S(1)}, u32[]{:S(2)}, u32[]{:S(2)}) collective-permute-start(bf16[1,393216]{1,0:T(2,128)(2,1)S(1)} %constant_dynamic-slice_fusion.4), channel_id=1, source_target_pairs={{0,16},{2,18},{4,20},{6,22},{8,24},{10,26},{12,28},{14,30},{16,0},... | collective-permute-start | bytes 2359304 | tf_op jit(solution)/shard_map/ppermute | solution.py:952
  1814.0 192.8 %collective-permute-start.35 = (bf16[1,638976]{1,0:T(2,128)(2,1)}, bf16[1,638976]{1,0:T(2,128)(2,1)}, u32[]{:S(2)}, u32[]{:S(2)}) collective-permute-start(bf16[1,638976]{1,0:T(2,128)(2,1)} %constant_dynamic-slice_fusion), channel_id=1, source_target_pairs={{0,16},{2,18},{4,20},{6,22},{8,24},{10,26},{12,28},{14,30},{16,0},... | collective-permute-start | bytes 3833864 | tf_op jit(solution)/shard_map/ppermute | solution.py:952
  1901.2 8.5 collective-permute-start.24
  1909.7 105.8 %copy-start.22 = (f32[1,393216]{1,0:T(1,128)S(1)}, f32[1,393216]{1,0:T(1,128)}, u32[]{:S(2)}) copy-start(f32[1,393216]{1,0:T(1,128)} %get-tuple-element.107) | copy-start | bytes 4718596
  2013.6 7.2 collective-permute-start.36
  (33 other events, 228.9 us)
Sparse Core Ops, SparseCore 0:
  846.7 321.8 all-reduce.13

commit v2 on v1

--- a/solution.py
+++ b/solution.py
@@ -13,6 +13,8 @@
 EPSILON = 1e-05
 LANES = 128
 EDGE = 8
+BLOCK = 256
+HALF_CHUNKS = 16
 F32 = jnp.float32
 BF16 = jnp.bfloat16
 VMEM_BYTES = 60 * 1024 * 1024
@@ -107,20 +109,26 @@
     return pl.BlockSpec(shape, lambda *g: (0,) * len(shape))
 
 
-def run(name, body, grid, live, args, in_specs, outs, scratch=(), flops=0):
+def run(name, body, grid, live, args, in_specs, outs, scratch=(), flops=0, after=(), alias=()):
     out_shape = [jax.ShapeDtypeStruct(shape, dtype) for shape, dtype, _ in outs]
     moved = sum(a.size * a.dtype.itemsize for a in args)
     moved += sum(math.prod(s) * jnp.dtype(d).itemsize for s, d, _ in outs)
+    count = 1 + len(args)
+
+    def without_order(*refs):
+        body(*refs[:count], *refs[count + len(after) :])
+
     return pl.pallas_call(
-        body,
+        without_order,
         grid_spec=pltpu.PrefetchScalarGridSpec(
             num_scalar_prefetch=1,
             grid=grid,
-            in_specs=in_specs,
+            in_specs=list(in_specs) + [pl.BlockSpec(memory_space=pl.ANY)] * len(after),
             out_specs=[spec for _, _, spec in outs],
             scratch_shapes=list(scratch),
         ),
         out_shape=out_shape,
+        input_output_aliases={1 + given: out for given, out in alias},
         compiler_params=pltpu.CompilerParams(
             dimension_semantics=("arbitrary",) * len(grid), vmem_limit_bytes=VMEM_BYTES
         ),
@@ -128,10 +136,81 @@
             flops=int(flops), bytes_accessed=int(moved), transcendentals=0
         ),
         name=name,
-    )(live, *args)
-
-
-def vit_front(live, tok_all, w_qkv, w_out, gains, shifts, tok_rows):
+    )(live, *args, *after)
+
+
+class Flat:
+    def __init__(self, shapes, devices):
+        self.shapes = shapes
+        self.chunk = sum(r * c for r, c in shapes) // devices
+        self.units = self.chunk // BLOCK
+        self.pieces = []
+        self.even = sum(r * c for r, c in shapes) % (devices * BLOCK * 3 * 16) == 0
+        offset = 0
+        for rows, cols in shapes:
+            self.even &= self.chunk % cols == 0 and offset % cols == 0 and cols % BLOCK == 0
+            found = []
+            if self.even:
+                height, begin = self.chunk // cols, offset // cols
+                for k in range(devices):
+                    low = max(k * height, begin)
+                    high = min((k + 1) * height, begin + rows)
+                    if low < high:
+                        start = (low - k * height) * (cols // BLOCK)
+                        found.append((k, low - begin, high - low, start))
+                        self.even &= (high - low) % 8 == 0 and start % 16 == 0
+            self.pieces.append(found)
+            offset += rows * cols
+
+    def within(self, matrix, first, count):
+        out = []
+        for k, row, height, start in self.pieces[matrix]:
+            low, high = max(row, first), min(row + height, first + count)
+            if low < high:
+                out.append((k, low, high - low, start + low - row, height))
+        return out
+
+
+def side_of(chunk):
+    z1, z0, y = (chunk >> 4) & 1, (chunk >> 3) & 1, (chunk >> 2) & 1
+    return (chunk >> 1) & 1, z1 * 8 + (z0 ^ z1) * 4 + y * 2 + (chunk & 1)
+
+
+def copy_out(own_core, keep_ref, send_ref, copies, sems, action):
+    for at, (chunk, source, place, rows) in enumerate(copies):
+        core, index = side_of(chunk)
+        for held_here, ref in ((True, keep_ref), (False, send_ref)):
+
+            @pl.when((own_core == core) == held_here)
+            def _(ref=ref, at=at, source=source, place=place, rows=rows, index=index):
+                target = ref.at[index, pl.ds(place, rows), :]
+                getattr(pltpu.make_async_copy(source, target, sems.at[at]), action)()
+
+
+def copy_all(own_core, keep_ref, send_ref, stage, flat, matrix, sems):
+    copies = []
+    for k, row, rows, start in flat.pieces[matrix]:
+        for c in range(stage.shape[1] // BLOCK):
+            copies.append((k, block_of(stage, row, rows, c), start + c * rows, rows))
+    copy_out(own_core, keep_ref, send_ref, copies, sems, "start")
+    copy_out(own_core, keep_ref, send_ref, copies, sems, "wait")
+
+
+def copy_semaphores(flat, matrix):
+    return pltpu.SemaphoreType.DMA((len(flat.pieces[matrix]) * flat.shapes[matrix][1] // BLOCK,))
+
+
+def halves(flat):
+    shape = (HALF_CHUNKS, flat.units, BLOCK)
+    spec = pl.BlockSpec(memory_space=pl.ANY)
+    return [(shape, BF16, spec), (shape, BF16, spec)]
+
+
+def block_of(ref, first, rows, block):
+    return ref.at[pl.ds(first, rows), pl.ds(block * BLOCK, BLOCK)]
+
+
+def vit_front(live, tok_all, w_qkv, w_out, gains, shifts, tok_rows, after):
     slots, key_rows, width = tok_all.shape
     head = width // HEADS
     pairs = width // LANES
@@ -204,21 +283,26 @@
             ((slots, width, tok_rows), BF16, slot(width, tok_rows)),
         ],
         flops=2 * macs,
-    )
-
-
-def vit_mlp(live, inner, inner_flip, d_mlp, residual, w_fc1, w_fc2):
+        after=after,
+    )
+
+
+def vit_mlp(live, inner, inner_flip, d_mlp, residual, lift, w_fc1, w_fc2, flat, after):
     slots, tok_rows, width = inner.shape
     hidden = w_fc1.shape[1]
     block = 512
     steps = hidden // block
+    blocks = width // BLOCK
 
     def body(
-        n, x_ref, xt_ref, dm_ref, res_ref, w1_ref, w2_ref, low_ref, din_ref, g1_ref, g2_ref, a1, a2
+        n, x_ref, xt_ref, dm_ref, res_ref, lift_ref, w1_ref, w2_ref,
+        merged_ref, din_ref, out1_ref, out2_ref, low, a1, a2, *rest,
     ):
-        @pl.when(pl.program_id(0) == 0)
-        def _():
-            low_ref[...] = res_ref[...]
+        step = pl.program_id(0)
+
+        @pl.when(step == 0)
+        def _():
+            low[...] = res_ref[...]
             din_ref[...] = jnp.zeros(din_ref.shape, F32)
 
         a1[...] = jnp.zeros(a1.shape, F32)
@@ -227,7 +311,7 @@
         def one(at, carry):
             act, slope = gelu_pair(dot_nn(x_ref[at], w1_ref[...]))
             act = act.astype(BF16)
-            low_ref[at] += dot_nn(act, w2_ref[...])
+            low[at] += dot_nn(act, w2_ref[...])
             d_fc = (slope * dot_nt(dm_ref[at], w2_ref[...])).astype(BF16)
             a1[...] += dot_nn(xt_ref[at], d_fc)
             a2[...] += dot_tn(act, dm_ref[at])
@@ -235,37 +319,103 @@
             return carry
 
         lax.fori_loop(0, n[0], one, 0)
-        g1_ref[...] = a1[...].astype(BF16)
-        g2_ref[...] = a2[...].astype(BF16)
+
+        @pl.when(step == steps - 1)
+        def _():
+            def close(at, carry):
+                merged_ref[at] = (low[at] + lift_ref[at]).astype(BF16)
+                return carry
+
+            def blank(at, carry):
+                merged_ref[at] = jnp.zeros(merged_ref.shape[1:], BF16)
+                return carry
+
+            lax.fori_loop(0, n[0], close, 0)
+            lax.fori_loop(n[0], slots, blank, 0)
+
+        if flat is None:
+            out1_ref[...] = a1[...].astype(BF16)
+            out2_ref[...] = a2[...].astype(BF16)
+            return
+        stage1, stage2, sems1, sems2 = rest
+
+        def first_copies(at):
+            out = []
+            for c in range(block // BLOCK):
+                for k, row, rows, start, height in flat.within(2, 0, width):
+                    place = start + (at * (block // BLOCK) + c) * height
+                    out.append((k, block_of(stage1, row, rows, c), pl.multiple_of(place, 16), rows))
+            return out
+
+        def second_copies(at):
+            out = []
+            for k, row, rows, start, height in flat.within(3, at * block, block):
+                for c in range(blocks):
+                    source = block_of(stage2, row - at * block, rows, c)
+                    out.append((k, source, start + c * height, rows))
+            return out
+
+        def each(at, now, action):
+            copy_out(n[1], out1_ref, out2_ref, first_copies(now), sems1, action)
+            for static in range(steps):
+
+                @pl.when(now == static)
+                def _(static=static):
+                    copy_out(n[1], out1_ref, out2_ref, second_copies(static), sems2, action)
+
+        @pl.when(step > 0)
+        def _():
+            each(step, step - 1, "wait")
+
+        stage1[...] = a1[...].astype(BF16)
+        stage2[...] = a2[...].astype(BF16)
+        each(step, step, "start")
+
+        @pl.when(step == steps - 1)
+        def _():
+            each(step, step, "wait")
 
     wide = (slots, tok_rows, width)
     by_col = pl.BlockSpec((width, block), lambda j, n: (0, j))
     by_row = pl.BlockSpec((block, width), lambda j, n: (j, 0))
+    scratch = [
+        pltpu.VMEM(wide, F32),
+        pltpu.VMEM((width, block), F32),
+        pltpu.VMEM((block, width), F32),
+    ]
+    if flat is None:
+        grads = [(w_fc1.shape, BF16, by_col), (w_fc2.shape, BF16, by_row)]
+    else:
+        grads = halves(flat)
+        most = max(len(flat.within(3, at * block, block)) for at in range(steps))
+        scratch += [
+            pltpu.VMEM((width, block), BF16),
+            pltpu.VMEM((block, width), BF16),
+            pltpu.SemaphoreType.DMA((block // BLOCK * len(flat.pieces[2]),)),
+            pltpu.SemaphoreType.DMA((most * blocks,)),
+        ]
     return run(
         "vit_mlp",
         body,
         (steps,),
         live,
-        (inner, inner_flip, d_mlp, residual, w_fc1, w_fc2),
-        [whole(*wide), whole(*inner_flip.shape), whole(*wide), whole(*wide), by_col, by_row],
-        [
-            (wide, F32, result(*wide)),
-            (wide, F32, result(*wide)),
-            (w_fc1.shape, BF16, by_col),
-            (w_fc2.shape, BF16, by_row),
-        ],
-        [pltpu.VMEM((width, block), F32), pltpu.VMEM((block, width), F32)],
+        (inner, inner_flip, d_mlp, residual, lift, w_fc1, w_fc2),
+        [whole(*wide), whole(*inner_flip.shape)] + [whole(*wide)] * 3 + [by_col, by_row],
+        [(wide, BF16, result(*wide)), (wide, F32, result(*wide))] + grads,
+        scratch,
         flops=12 * slots * tok_rows * width * hidden,
-    )
-
-
-def vit_back(live, residual, d_inner, d_merged, mixed, w_out, gains):
+        after=after,
+    )
+
+
+def vit_back(live, residual, d_inner, d_merged, mixed, w_out, gains, flat, kept, after):
     slots, tok_rows, width = residual.shape
 
-    def body(
-        n, res_ref, din_ref, dm_ref, mix_ref, wo_ref, g_ref,
-        dres_ref, dmix_ref, gout_ref, sums_ref, low, acc,
-    ):
+    def body(n, res_ref, din_ref, dm_ref, mix_ref, wo_ref, g_ref, *rest):
+        if flat is None:
+            dres_ref, dmix_ref, sums_ref, gout_ref, low, acc = rest
+        else:
+            _, _, dres_ref, dmix_ref, sums_ref, keep_ref, send_ref, low, acc, stage, sems = rest
         at = pl.program_id(0)
 
         @pl.when(at == 0)
@@ -290,25 +440,34 @@
 
         @pl.when(at == slots - 1)
         def _():
-            gout_ref[...] = acc[...].astype(BF16)
+            if flat is None:
+                gout_ref[...] = acc[...].astype(BF16)
+            else:
+                stage[...] = acc[...].astype(BF16)
+                copy_all(n[1], keep_ref, send_ref, stage, flat, 1, sems)
 
     wide = (slots, tok_rows, width)
     one = slot(tok_rows, width)
+    args = (residual, d_inner, d_merged, mixed, w_out, gains)
+    specs = [one, one, one, one, whole(*w_out.shape), whole(*gains.shape)]
+    scratch = [pltpu.VMEM((tok_rows, width), BF16), pltpu.VMEM(w_out.shape, F32)]
+    grads, alias = [(w_out.shape, BF16, result(*w_out.shape))], ()
+    if flat is not None:
+        args, specs, grads = args + kept, specs + [pl.BlockSpec(memory_space=pl.ANY)] * 2, halves(flat)
+        scratch += [pltpu.VMEM(w_out.shape, BF16), copy_semaphores(flat, 1)]
+        alias = ((6, 3), (7, 4))
     return run(
         "vit_back",
         body,
         (slots,),
         live,
-        (residual, d_inner, d_merged, mixed, w_out, gains),
-        [one, one, one, one, whole(*w_out.shape), whole(*gains.shape)],
-        [
-            (wide, F32, one),
-            (wide, BF16, one),
-            (w_out.shape, BF16, result(*w_out.shape)),
-            ((8, width), F32, result(8, width)),
-        ],
-        [pltpu.VMEM((tok_rows, width), BF16), pltpu.VMEM(w_out.shape, F32)],
+        args,
+        specs,
+        [(wide, F32, one), (wide, BF16, one), ((8, width), F32, result(8, width))] + grads,
+        scratch,
         flops=4 * slots * tok_rows * width * width,
+        after=after,
+        alias=alias,
     )
 
 
@@ -380,11 +539,15 @@
     )
 
 
-def qkv_back(live, normed, d_q, d_k, d_v, w_qkv):
+def qkv_back(live, normed, d_q, d_k, d_v, w_qkv, flat, kept):
     slots, key_rows, width = normed.shape
     tok_rows = d_q.shape[1]
 
-    def body(n, x_ref, dq_ref, dk_ref, dv_ref, w_ref, dn_ref, gw_ref, x_flip, acc):
+    def body(n, x_ref, dq_ref, dk_ref, dv_ref, w_ref, *rest):
+        if flat is None:
+            dn_ref, gw_ref, x_flip, acc = rest
+        else:
+            _, _, dn_ref, keep_ref, send_ref, x_flip, acc, stage, sems = rest
         at = pl.program_id(0)
 
         @pl.when(at == 0)
@@ -403,23 +566,36 @@
 
         @pl.when(at == slots - 1)
         def _():
-            gw_ref[...] = acc[...].astype(BF16)
+            if flat is None:
+                gw_ref[...] = acc[...].astype(BF16)
+            else:
+                stage[...] = acc[...].astype(BF16)
+                copy_all(n[1], keep_ref, send_ref, stage, flat, 0, sems)
 
     keys = slot(key_rows, width)
+    args = (normed, d_q, d_k, d_v, w_qkv)
+    specs = [keys, slot(tok_rows, width), keys, keys, whole(*w_qkv.shape)]
+    scratch = [pltpu.VMEM((width, key_rows), BF16), pltpu.VMEM(w_qkv.shape, F32)]
+    grads, alias = [(w_qkv.shape, BF16, result(*w_qkv.shape))], ()
+    if flat is not None:
+        args, specs, grads = args + kept, specs + [pl.BlockSpec(memory_space=pl.ANY)] * 2, halves(flat)
+        scratch += [pltpu.VMEM(w_qkv.shape, BF16), copy_semaphores(flat, 0)]
+        alias = ((5, 1), (6, 2))
     return run(
         "qkv_back",
         body,
         (slots,),
         live,
-        (normed, d_q, d_k, d_v, w_qkv),
-        [keys, slot(tok_rows, width), keys, keys, whole(*w_qkv.shape)],
-        [(normed.shape, F32, keys), (w_qkv.shape, BF16, result(*w_qkv.shape))],
-        [pltpu.VMEM((width, key_rows), BF16), pltpu.VMEM(w_qkv.shape, F32)],
+        args,
+        specs,
+        [(normed.shape, F32, keys)] + grads,
+        scratch,
         flops=4 * slots * width * width * (2 * key_rows + tok_rows),
-    )
-
-
-def tokens_back(live, tokens, d_norm, arrived, d_residual, gains):
+        alias=alias,
+    )
+
+
+def tokens_back(live, tokens, d_norm, arrived, d_residual, gains, after):
     slots, tok_rows, width = tokens.shape
 
     def body(n, x_ref, dn_ref, more_ref, dres_ref, g_ref, out_ref, sums_ref):
@@ -457,6 +633,7 @@
             (tokens.shape, BF16, every_slot(tok_rows, width)),
             ((8, width), F32, result(8, width)),
         ],
+        after=after,
     )
 
 
@@ -641,14 +818,14 @@
     )
 
 
-def adapter(live, own, first, last, low_out, d_merged, w_pool, w_gate):
+def adapter(live, own, first, last, d_merged, w_pool, w_gate, after):
     slots, tok_rows, channels = own.shape
     side = first.shape[1]
     width = w_pool.shape[1]
 
     def body(
-        n, own_ref, first_ref, last_ref, low_ref, dm_ref, w_ref, gate_ref,
-        merged_ref, dpool_ref, gw_ref, ggate_ref, acc,
+        n, own_ref, first_ref, last_ref, dm_ref, w_ref, gate_ref,
+        lift_ref, dpool_ref, gw_ref, ggate_ref, acc,
     ):
         at = pl.program_id(0)
 
@@ -671,7 +848,7 @@
             lifted = dot_nn(pooled_low, w_ref[...])
             logit = jnp.sum(pooled * gate_ref[...], axis=-1, keepdims=True)
             gate = 1.0 / (1.0 + jnp.exp(-logit))
-            merged_ref[0] = (low_ref[0] + gate * lifted).astype(BF16)
+            lift_ref[0] = gate * lifted
             d_top = dm_ref[0].astype(F32)
             d_logit = jnp.sum(d_top * lifted, axis=-1, keepdims=True) * gate * (1.0 - gate)
             d_lifted = (gate * d_top).astype(BF16)
@@ -679,10 +856,6 @@
             ggate_ref[0:1, :] += col_sum(d_logit * pooled)
             dpool_ref[0] = (dot_nt(d_lifted, w_ref[...]) + d_logit * gate_ref[...]).astype(BF16)
 
-        @pl.when(at >= n[0])
-        def _():
-            merged_ref[...] = jnp.zeros(merged_ref.shape, BF16)
-
         @pl.when(at == slots - 1)
         def _():
             gw_ref[...] = acc[...].astype(BF16)
@@ -693,17 +866,18 @@
         body,
         (slots,),
         live,
-        (own, first, last, low_out, d_merged, w_pool, w_gate),
-        [slot(tok_rows, channels), edge, edge, slot(tok_rows, width), slot(tok_rows, width)]
+        (own, first, last, d_merged, w_pool, w_gate),
+        [slot(tok_rows, channels), edge, edge, slot(tok_rows, width)]
         + [whole(*w_pool.shape), whole(*w_gate.shape)],
         [
-            ((slots, tok_rows, width), BF16, every_slot(tok_rows, width)),
+            ((slots, tok_rows, width), F32, slot(tok_rows, width)),
             (own.shape, BF16, slot(tok_rows, channels)),
             (w_pool.shape, BF16, result(*w_pool.shape)),
             ((8, channels), F32, result(8, channels)),
         ],
         [pltpu.VMEM(w_pool.shape, F32)],
         flops=6 * slots * tok_rows * channels * width,
+        after=after,
     )
 
 
@@ -745,36 +919,36 @@
     )
 
 
-def conv_mlp_back(live, spatial_flip, act, slope, d_branch, w_pw1, w_pw2):
+def conv_mlp_back(live, spatial_flip, act, slope, d_branch, w_pw1, w_pw2, grad_pool, flat):
     slots, channels, cells = spatial_flip.shape
     hidden = w_pw1.shape[1]
-    block = 256
+    block = BLOCK
     steps = hidden // block
+    blocks = channels // BLOCK
 
     def body(
-        n, xt_ref, act_ref, slope_ref, db_ref, w1_ref, w2_ref, g1_ref, g2_ref, dsp_ref,
-        a1, a2, dsp, sem,
+        n, xt_ref, act_ref, slope_ref, db_ref, w1_ref, w2_ref, pool_ref,
+        dsp_ref, out1_ref, out2_ref, a1, a2, dsp, sem, *rest,
     ):
         step = pl.program_id(0)
+        odd = lax.rem(step, 2)
 
         @pl.when(step == 0)
         def _():
             dsp[...] = jnp.zeros(dsp.shape, F32)
 
-        a1[...] = jnp.zeros(a1.shape, F32)
+        a1[odd] = jnp.zeros(a1.shape[1:], F32)
         a2[...] = jnp.zeros(a2.shape, F32)
 
         def one(at, carry):
             d_hidden = dot_nt(db_ref[at], w2_ref[...])
             d_expand = (slope_ref[at].astype(F32) * d_hidden).astype(BF16)
             a2[...] += dot_tn(act_ref[at], db_ref[at])
-            a1[...] += dot_nn(xt_ref[at], d_expand)
+            a1[odd] += dot_nn(xt_ref[at], d_expand)
             dsp[at] += dot_nt(d_expand, w1_ref[...])
             return carry
 
         lax.fori_loop(0, n[0], one, 0)
-        g1_ref[...] = a1[...].astype(BF16)
-        g2_ref[...] = a2[...].astype(BF16)
 
         @pl.when(step == steps - 1)
         def _():
@@ -782,28 +956,107 @@
             out.start()
             out.wait()
 
+        if flat is None:
+            out1_ref[...] = a1[odd].astype(BF16)
+            out2_ref[...] = a2[...].astype(BF16)
+            return
+        stage1, stage2, sems1, sems2, sems3 = rest
+
+        def first_copies(at):
+            out = []
+            for index, (k, _, rows, start) in enumerate(flat.pieces[0]):
+                place = pl.multiple_of(start + at * 2 * rows, 16)
+                out.append((k, stage1.at[index, pl.ds(0, 2 * rows), :], place, 2 * rows))
+            return out
+
+        def second_copies(at):
+            out = []
+            for k, row, rows, start, height in flat.within(1, at * block, block):
+                for c in range(blocks):
+                    source = block_of(stage2, row - at * block, rows, c)
+                    out.append((k, source, start + c * height, rows))
+            return out
+
+        def pool_copies():
+            out = []
+            for k, row, rows, start in flat.pieces[2]:
+                for c in range(flat.shapes[2][1] // BLOCK):
+                    out.append((k, block_of(pool_ref, row, rows, c), start + c * rows, rows))
+            return out
+
+        def firsts(now, action):
+            copy_out(n[1], out1_ref, out2_ref, first_copies(now), sems1, action)
+
+        def seconds(now, action):
+            for static in range(steps):
+
+                @pl.when(now == static)
+                def _(static=static):
+                    copy_out(n[1], out1_ref, out2_ref, second_copies(static), sems2, action)
+
+        @pl.when(step == 0)
+        def _():
+            copy_out(n[1], out1_ref, out2_ref, pool_copies(), sems3, "start")
+
+        @pl.when(step > 0)
+        def _():
+            seconds(step - 1, "wait")
+
+        stage2[...] = a2[...].astype(BF16)
+        seconds(step, "start")
+
+        @pl.when(odd == 1)
+        def _():
+            pair = step // 2
+
+            @pl.when(pair > 0)
+            def _():
+                firsts(pair - 1, "wait")
+
+            for index, (_, row, rows, _) in enumerate(flat.pieces[0]):
+                both = jnp.concatenate([a1[0, row : row + rows], a1[1, row : row + rows]], axis=0)
+                stage1[index, 0 : 2 * rows, :] = both.astype(BF16)
+            firsts(pair, "start")
+
+        @pl.when(step == steps - 1)
+        def _():
+            seconds(step, "wait")
+            firsts(step // 2, "wait")
+            copy_out(n[1], out1_ref, out2_ref, pool_copies(), sems3, "wait")
+
     by_col = pl.BlockSpec((channels, block), lambda j, n: (0, j))
     by_row = pl.BlockSpec((block, channels), lambda j, n: (j, 0))
     by_hidden = pl.BlockSpec((slots, cells, block), lambda j, n: (0, 0, j))
+    anywhere = pl.BlockSpec(memory_space=pl.ANY)
     wide = (slots, cells, channels)
+    scratch = [
+        pltpu.VMEM((2, channels, block), F32),
+        pltpu.VMEM((block, channels), F32),
+        pltpu.VMEM(wide, F32),
+        pltpu.SemaphoreType.DMA,
+    ]
+    if flat is None:
+        grads = [(w_pw1.shape, BF16, by_col), (w_pw2.shape, BF16, by_row)]
+    else:
+        grads = halves(flat)
+        most = max(len(flat.within(1, at * block, block)) for at in range(steps))
+        tall = max(rows for _, _, rows, _ in flat.pieces[0])
+        scratch += [
+            pltpu.VMEM((len(flat.pieces[0]), 2 * tall, BLOCK), BF16),
+            pltpu.VMEM((block, channels), BF16),
+            pltpu.SemaphoreType.DMA((len(flat.pieces[0]),)),
+            pltpu.SemaphoreType.DMA((most * blocks,)),
+            copy_semaphores(flat, 2),
+        ]
     return run(
         "conv_mlp_back",
         body,
         (steps,),
         live,
-        (spatial_flip, act, slope, d_branch, w_pw1, w_pw2),
-        [whole(*spatial_flip.shape), by_hidden, by_hidden, whole(*wide), by_col, by_row],
-        [
-            (w_pw1.shape, BF16, by_col),
-            (w_pw2.shape, BF16, by_row),
-            (wide, F32, pl.BlockSpec(memory_space=pl.ANY)),
-        ],
-        [
-            pltpu.VMEM((channels, block), F32),
-            pltpu.VMEM((block, channels), F32),
-            pltpu.VMEM(wide, F32),
-            pltpu.SemaphoreType.DMA,
-        ],
+        (spatial_flip, act, slope, d_branch, w_pw1, w_pw2, grad_pool),
+        [whole(*spatial_flip.shape), by_hidden, by_hidden, whole(*wide), by_col, by_row, anywhere],
+        [(wide, F32, anywhere)] + grads,
+        scratch,
         flops=8 * slots * cells * channels * hidden,
     )
 
@@ -843,7 +1096,7 @@
     )
 
 
-def conv_back(live, top, high, bottom, d_top, d_mid, d_bottom, d_post, kernel):
+def conv_back(live, top, high, bottom, d_top, d_mid, d_bottom, d_post, kernel, after):
     slots, rows, cols, channels = high.shape
 
     def body(
@@ -915,6 +1168,7 @@
         ],
         [pltpu.VMEM(frame_shape, F32), pltpu.VMEM(frame_shape, F32)],
         flops=4 * slots * rows * cols * channels * KS * KS * 40,
+        after=after,
     )
 
 
@@ -997,9 +1251,7 @@
     data_count = lax.axis_size("dp")
     strips = lax.axis_size("strip")
     devices = data_count * strips
-    total = sum(m.size for m in matrices)
-    chunk = total // devices
-    extra = extras.shape[0] // devices
+    chunk = sum(m.size for m in matrices) // devices
     span = data_count // 4
     placed = None
     offset = 0
@@ -1012,7 +1264,109 @@
     for bit in range(2, bits("dp")):
         placed = placed.reshape(placed.shape[0] // 2, 2, chunk)
         placed = swap_halves(placed, "dp", bit, bit_of("dp", bit))
-    mine = placed.reshape(chunk).astype(F32)
+    return share_of(placed.reshape(chunk).astype(F32), chunk, extras)
+
+
+STEPS = {
+    "core": ("dp", 1, lambda dp, strip: dp & 1),
+    "x": ("strip", 1, lambda dp, strip: strip & 1),
+    "y": ("dp", 2, lambda dp, strip: (dp >> 1) & 1),
+    "z": ("dp", 4, lambda dp, strip: ((dp >> 2) ^ (dp >> 3)) & 1),
+    "far": ("dp", 12, lambda dp, strip: (dp >> 3) & 1),
+}
+ORDERS = (("x", "y", "z", "far"), ("y", "z", "x", "far"), ("z", "x", "y", "far"))
+
+
+def across(step, value):
+    axis, flip_bits, _ = STEPS[step]
+    return lax.ppermute(value, axis, [(i, i ^ flip_bits) for i in range(lax.axis_size(axis))])
+
+
+def split_sum(flat, kept, arrived, level, after):
+    parts = len(ORDERS)
+    rows = flat.units // parts
+    count = HALF_CHUNKS >> (level + 1)
+    own = [STEPS[order[level]][2](lax.axis_index("dp"), lax.axis_index("strip")) for order in ORDERS]
+    bits = jnp.stack(own).astype(jnp.int32)
+    specs, args = [], []
+    for part, order in enumerate(ORDERS):
+        left = [name for name in ("far", "z", "y", "x") if name not in order[:level]]
+        low = len(left) - 1 - left.index(order[level])
+
+        for flipped in (0, 1):
+
+            def place(i, bit, part=part, low=low, flipped=flipped):
+                mine = bit[part] ^ flipped
+                index = ((i >> low) << (low + 1)) | (mine << low) | (i & ((1 << low) - 1))
+                return index, part if level == 0 else 0, 0
+
+            for source in (kept, arrived):
+                args.append(source[0 if level == 0 else part])
+                specs.append(pl.BlockSpec((1, rows, BLOCK), place))
+
+    def body(_, *refs):
+        ins, outs = refs[: 4 * parts], refs[4 * parts :]
+        for at in range(2 * parts):
+            total = ins[2 * at][...].astype(F32) + ins[2 * at + 1][...].astype(F32)
+            outs[at][...] = total.astype(BF16)
+
+    out = pl.BlockSpec((1, rows, BLOCK), lambda i, bit: (i, 0, 0))
+    done = run(
+        "split_sum",
+        body,
+        (count,),
+        bits,
+        tuple(args),
+        specs,
+        [((count, rows, BLOCK), BF16, out)] * (2 * parts),
+        after=after,
+    )
+    return done[0::2], done[1::2]
+
+
+def sent(sends, level):
+    return [across(order[level], value) for order, value in zip(ORDERS, sends)]
+
+
+def last_sum(kept, arrived):
+    parts = [(k.astype(F32) + a.astype(F32))[0] for k, a in zip(kept, arrived)]
+    return jnp.concatenate(parts, axis=0)
+
+
+def row_major(flat, units):
+    devices = lax.axis_size("dp") * lax.axis_size("strip")
+    index = lax.axis_index("dp") * lax.axis_size("strip") + lax.axis_index("strip")
+    kinds, kind_of = [], []
+    for k in range(devices):
+        kind = []
+        for matrix, pieces in enumerate(flat.pieces):
+            for chunk, _, rows, start in pieces:
+                if chunk == k:
+                    kind.append((start, rows, flat.shapes[matrix][1] // BLOCK))
+        kind = tuple(kind)
+        if kind not in kinds:
+            kinds.append(kind)
+        kind_of.append(kinds.index(kind))
+
+    def ordered(kind):
+        def branch(value):
+            out = []
+            for start, rows, blocks in kind:
+                piece = value[start : start + rows * blocks].reshape(blocks, rows, BLOCK)
+                out.append(piece.transpose(1, 0, 2).reshape(-1))
+            return jnp.concatenate(out)
+
+        return branch
+
+    which = jnp.asarray(kind_of, jnp.int32)[index]
+    return lax.switch(which, [ordered(kind) for kind in kinds], units)
+
+
+def share_of(mine, chunk, extras):
+    data_count = lax.axis_size("dp")
+    strips = lax.axis_size("strip")
+    devices = data_count * strips
+    extra = extras.shape[0] // devices
     index = lax.axis_index("dp") * strips + lax.axis_index("strip")
     pieces = [mine]
     left = extras.shape[0]
@@ -1058,7 +1412,7 @@
     cells = rows * cols
     strips = lax.axis_size("strip")
     strip = lax.axis_index("strip")
-    live = counts[:1]
+    live = jnp.stack([counts[0], lax.axis_index("dp") & 1]).astype(jnp.int32)
 
     col_bins = bin_weights(col_edges, cols)
     side = col_bins.shape[0]
@@ -1075,6 +1429,14 @@
     )
     top, bottom = from_both_sides(high_map[:, :REACH], high_map[:, -REACH:])
 
+    data_count = lax.axis_size("dp")
+    devices = data_count * strips
+    vit_flat = Flat([w.shape for w in (w_qkv, w_attn_out, w_fc1, w_fc2)], devices)
+    conv_flat = Flat([w.shape for w in (w_pw1, w_pw2, w_pool)], devices)
+    chunked = devices == 2 * HALF_CHUNKS and strips == 2 and vit_flat.even and conv_flat.even
+    if not chunked:
+        vit_flat = conv_flat = None
+
     spatial, spatial_flip, conv_unit, conv_inverse = conv_front(
         live, top, high_map, bottom, dw_kernel, conv_gains, conv_shifts
     )
@@ -1083,15 +1445,11 @@
     )
     own, before_part, after_part = pool(live, high_out, bins, side)
     first, last = from_both_sides(before_part, after_part)
-
     normed, q, kv, probs, mixed, residual, inner, inner_flip = vit_front(
-        live, tok_all, w_qkv, w_attn_out, vit_gains, vit_shifts, tok_rows
-    )
-    low_out, d_inner, grad_fc1, grad_fc2 = vit_mlp(
-        live, inner, inner_flip, d_merged, residual, w_fc1, w_fc2
-    )
-    merged, d_pooled, grad_pool, gate_sums = adapter(
-        live, own, first, last, low_out, d_merged, w_pool, w_gate.reshape(1, channels)
+        live, tok_all, w_qkv, w_attn_out, vit_gains, vit_shifts, tok_rows, (own,)
+    )
+    lift, d_pooled, grad_pool, gate_sums = adapter(
+        live, own, first, last, d_merged, w_pool, w_gate.reshape(1, channels), (inner,)
     )
     near_before, near_after = from_both_sides(d_pooled[:, :side], d_pooled[:, -side:])
     d_post, d_branch, scale_sums = unpool(
@@ -1102,25 +1460,41 @@
         branch,
         conv_gains,
     )
-    grad_pw1, grad_pw2, d_spatial = conv_mlp_back(
-        live, spatial_flip, act, slope, d_branch, w_pw1, w_pw2
+    d_spatial, *conv_grads = conv_mlp_back(
+        live, spatial_flip, act, slope, d_branch, w_pw1, w_pw2, grad_pool, conv_flat
     )
     d_conv_in, norm_sums = conv_norm_back(live, d_spatial, conv_unit, conv_inverse, conv_gains)
     d_conv_in = d_conv_in.reshape(high_map.shape)
     d_before, d_after = from_both_sides(d_conv_in[:, :REACH], d_conv_in[:, -REACH:])
 
-    d_residual, d_mixed, grad_out, inner_sums = vit_back(
-        live, residual, d_inner, d_merged, mixed, w_attn_out, vit_gains
+    merged, d_inner, *vit_grads = vit_mlp(
+        live, inner, inner_flip, d_merged, residual, lift, w_fc1, w_fc2, vit_flat, (d_conv_in,)
+    )
+    order = (d_inner,)
+    if chunked:
+        kept, sends = split_sum(
+            conv_flat, conv_grads[:1], [across("core", conv_grads[1])], 0, order
+        )
+        arrived = sent(sends, 0)
+        order = (sends[0],)
+    d_residual, d_mixed, inner_sums, *vit_grads_out = vit_back(
+        live, residual, d_inner, d_merged, mixed, w_attn_out, vit_gains, vit_flat,
+        tuple(vit_grads), order,
     )
     d_q, d_k, d_v = attention_back(live, probs, q, kv, d_mixed)
-    d_normed, grad_qkv = qkv_back(live, normed, d_q, d_k, d_v, w_qkv)
-    arrived = jnp.zeros(low_tokens.shape, BF16)
+    d_normed, *vit_grads_qkv = qkv_back(
+        live, normed, d_q, d_k, d_v, w_qkv, vit_flat, tuple(vit_grads_out)
+    )
+    d_other = jnp.zeros(low_tokens.shape, BF16)
     for by in range(1, strips):
         part = d_normed[:, by * tok_rows : (by + 1) * tok_rows].astype(BF16)
-        arrived = arrived + shifted(part, -by) if by > 1 else shifted(part, -by)
-    grad_tokens, token_sums = tokens_back(
-        live, low_tokens, d_normed, arrived, d_residual, vit_gains
-    )
+        d_other = d_other + shifted(part, -by) if by > 1 else shifted(part, -by)
+    order = (d_normed,)
+    if chunked:
+        kept, sends = split_sum(conv_flat, kept, arrived, 1, order)
+        arrived = sent(sends, 1)
+        vit_arrived = across("core", vit_grads_qkv[1])
+        order = (sends[0],)
     grad_map, kernel_sums = conv_back(
         live,
         top,
@@ -1131,6 +1505,17 @@
         d_after,
         d_post.reshape(high_map.shape),
         dw_kernel,
+        order,
+    )
+    order = (grad_map,)
+    if chunked:
+        kept, sends = split_sum(conv_flat, kept, arrived, 2, order)
+        arrived = sent(sends, 2)
+        vit_kept, vit_sends = split_sum(vit_flat, vit_grads_qkv[:1], [vit_arrived], 0, (sends[0],))
+        vit_arrived = sent(vit_sends, 0)
+        order = (vit_sends[0],)
+    grad_tokens, token_sums = tokens_back(
+        live, low_tokens, d_normed, d_other, d_residual, vit_gains, order
     )
 
     vit_extras = jnp.concatenate([token_sums[0], inner_sums[0], token_sums[1], inner_sums[1]])
@@ -1145,17 +1530,29 @@
         ]
     )
     extras = lax.psum(jnp.concatenate([vit_extras, conv_extras]), ("dp", "strip"))
-    vit_grads = owned_chunk(
-        [grad_qkv, grad_out, grad_fc1, grad_fc2], extras[: vit_extras.shape[0]]
-    )
-    conv_grads = owned_chunk([grad_pw1, grad_pw2, grad_pool], extras[vit_extras.shape[0] :])
+    vit_extras, conv_extras = extras[: vit_extras.shape[0]], extras[vit_extras.shape[0] :]
+    if chunked:
+        kept, sends = split_sum(conv_flat, kept, arrived, 3, (grad_tokens,))
+        arrived = sent(sends, 3)
+        vit_kept, vit_sends = split_sum(vit_flat, vit_kept, vit_arrived, 1, (sends[0],))
+        vit_arrived = sent(vit_sends, 1)
+        conv_mine = row_major(conv_flat, last_sum(kept, arrived))
+        conv_out = share_of(conv_mine, conv_flat.chunk, conv_extras)
+        for level in (2, 3):
+            vit_kept, vit_sends = split_sum(vit_flat, vit_kept, vit_arrived, level, ())
+            vit_arrived = sent(vit_sends, level)
+        vit_mine = row_major(vit_flat, last_sum(vit_kept, vit_arrived))
+        vit_out = share_of(vit_mine, vit_flat.chunk, vit_extras)
+    else:
+        vit_out = owned_chunk(vit_grads_qkv + vit_grads_out + vit_grads, vit_extras)
+        conv_out = owned_chunk(conv_grads + [grad_pool], conv_extras)
     return (
         merged,
         high_out.reshape(high_map.shape),
         grad_tokens,
         grad_map,
-        vit_grads,
-        conv_grads,
+        vit_out,
+        conv_out,
     )
 
 

time: 2050 us -> 1390 us (0.68)
  local copies, waits for them, and re-layouts: 544 us -> 40.7 us
  Pallas kernels: 299 us -> 786 us
  starting transfers between devices: 692 us -> 214 us
  other arithmetic: 157 us -> 35.1 us
  waiting for transfers between devices: 323 us -> 287 us
    pallas_call x14 -> x22, Pallas kernels: 299 us -> 786 us  [run(): pl.pallas_call(without_order, grid_spec=pltpu.PrefetchScalarGridSpec(num_...]
    ppermute x27 -> x28, starting transfers between devices: 669 us -> 191 us  [the longest x26 184 us: across(): lax.ppermute(value, axis, [(i, i ^ flip_bits) for i in range(lax.axis_siz...]
    dynamic_update_slice x7 -> x0, local copies, waits for them, and re-layouts: 314 us -> none  [owned_chunk(): canvas = lax.dynamic_update_slice(canvas, part, (base, 0))[:span]]
    ppermute x27 -> x28, waiting for transfers between devices: 308 us -> 186 us  [the longest x26 186 us: across(): lax.ppermute(value, axis, [(i, i ^ flip_bits) for i in range(lax.axis_siz...]
    convert_element_type x16 -> x0, other arithmetic: 85.4 us -> none  [the longest x14 76 us: swap_halves(): return (keep.astype(F32) + got.astype(F32)).astype(BF16)]
    psum x1, waiting for transfers between devices: 0.02 us -> 77.4 us  [per_device(): lax.psum(jnp.concatenate([vit_extras, conv_extras]), ('dp', 'strip'))]
    squeeze x21 -> x0, local copies, waits for them, and re-layouts: 55.4 us -> none  [swap_halves(): send = lax.dynamic_index_in_dim(cells, 1 - own, 1, keepdims=False)]
    pad x8 -> x0, local copies, waits for them, and re-layouts: 53.3 us -> none  [the longest x6 52.2 us: shared_sum(): jnp.pad(matrix, ((front, back), (0, 0)))]
  transfers between devices with their start and end apart: 38 -> 39, of which waited for: 11 -> 17; matrix products, arithmetic and copies ran while one was open for 33% -> 4% of each run, Pallas kernels for 15% -> 33%
where the time goes in v2:
time: 1390 us; the launch traced here: 1380 us
  Pallas kernels  786 us (57%)
  waiting for transfers between devices  287 us (21%)
  starting transfers between devices  214 us (15%)
  local copies, waits for them, and re-layouts  40.7 us (3%)
  other arithmetic  35.1 us (3%)
  between operations  16.8 us (1%)
    pallas_call x22, Pallas kernels, run(): pl.pallas_call(without_order, grid_spec=pltpu.PrefetchScalarGridSpec(num_...  786 us
    ppermute x26, waiting for transfers between devices, across(): lax.ppermute(value, axis, [(i, i ^ flip_bits) for i in range(lax.axis_siz...  186 us
    ppermute x26, starting transfers between devices, across(): lax.ppermute(value, axis, [(i, i ^ flip_bits) for i in range(lax.axis_siz...  184 us
    psum x1, waiting for transfers between devices, per_device(): lax.psum(jnp.concatenate([vit_extras, conv_extras]), ('dp', 'strip'))  77.4 us
  transfers between devices with their start and end apart: 39, of which 17 were waited for; matrix products, arithmetic and copies ran while one was open for 4% of the time, Pallas kernels for 33%

profile of v2, /device:TPU:13, one launch (start us, length us, event | category | flops | bytes accessed | tf_op | source)
XLA Modules:
  0.0 1380.0 jit_solution(1831877148395347471)
XLA Ops:
  11.5 6.0 collective-permute-start.1
  24.5 3.2 convert_element_type.81.refs_2_
  28.2 11.1 collective-permute-done.2.refs_3_
  40.8 44.0 %conv_front.1 = (bf16[4,512,1536]{2,1,0:T(8,128)(2,1)}, bf16[4,1536,512]{2,1,0:T(8,128)(2,1)}, bf16[4,512,1536]{2,1,0:T(8,128)(2,1)}, f32[4,512,1]{2,1,0:T(8,128)}) custom-call(s32[2]{0:T(128)} %pad_add_fusion.refs_0_, bf16[4,3,32,1536]{3,2,1,0:T(8,128)(2,1)} %collective-permute-done.1.refs_1_, bf16[4,16,32,1536]{3,2,1,0:T(8,128)(2,1)} %refs_2_.5, ...), custom_call_target="tpu_custom_call" | custom-call | flops 12331253760 | bytes 27858944 | tf_op jit(solution)/shard_map/conv_front/pallas_call | solution.py:121
  84.8 107.6 %conv_mlp.1 = (bf16[4,512,6144]{2,1,0:T(8,128)(2,1)}, bf16[4,512,6144]{2,1,0:T(8,128)(2,1)}, bf16[4,512,1536]{2,1,0:T(8,128)(2,1)}, bf16[4,512,1536]{2,1,0:T(8,128)(2,1)}) custom-call(s32[2]{0:T(128)} %pad_add_fusion.refs_0_, bf16[4,512,1536]{2,1,0:T(8,128)(2,1)} %get-tuple-element.141.refs_1_, bf16[4,512,1536]{2,1,0:T(8,128)(2,1)} %bitcast.136, ...), custom_call_target="tpu_custom_call" | custom-call | flops 77309411328 | bytes 113258496 | tf_op jit(solution)/shard_map/conv_mlp/pallas_call | solution.py:121
  192.5 7.6 pool.1
  200.0 4.2 collective-permute-start.3
  205.8 4.4 pad_maximum_fusion.4.refs_1_
  210.2 62.8 %vit_front.1 = (bf16[4,576,1024]{2,1,0:T(8,128)(2,1)}, bf16[4,288,1024]{2,1,0:T(8,128)(2,1)}, bf16[4,576,2048]{2,1,0:T(8,128)(2,1)}, bf16[4,16,576,288]{3,2,1,0:...) custom-call(s32[2]{0:T(128)} %pad_add_fusion.refs_0_, ...), custom_call_target="tpu_custom_call" | custom-call | flops 19931332608 | bytes 62668800 | tf_op jit(solution)/shard_map/vit_front/pallas_call | solution.py:121
  273.8 18.3 %adapter.1 = (f32[4,288,1024]{2,1,0:T(8,128)}, bf16[4,288,1536]{2,1,0:T(8,128)(2,1)}, bf16[1536,1024]{1,0:T(8,128)(2,1)}, f32[8,1536]{1,0:T(8,128)}) custom-call(s32[2]{0:T(128)} %pad_add_fusion.refs_0_, f32[4,288,1536]{2,1,0:T(8,128)} %get-tuple-element.143.refs_6_.refs_1_, bf16[4,24,1536]{2,1,0:T(8,128)(2,1)} %copy-done.21, ...), custom_call_target="tpu_custom_call" | custom-call | flops 10871635968 | bytes 24631296 | tf_op jit(solution)/shard_map/adapter/pallas_call | solution.py:121
  293.3 4.0 collective-permute-start.5
  300.9 3.8 collective-permute-done.6
  304.8 3.6 pad_maximum_fusion.5.refs_1_
  308.3 13.0 unpool.1
  321.3 183.3 %conv_mlp_back.1 = (f32[4,512,1536]{2,1,0:T(8,128)}, bf16[16,2496,256]{2,1,0:T(8,128)(2,1)}, bf16[16,2496,256]{2,1,0:T(8,128)(2,1)}) custom-call(s32[2]{0:T(128)} %pad_add_fusion.refs_0_, bf16[4,1536,512]{2,1,0:T(8,128)(2,1)} %get-tuple-element.150.refs_1_, bf16[4,512,6144]{2,1,0:T(8,128)(2,1)} %get-tuple-element.151.refs_2_, ...), custom_call_target="tpu_custom_call" | custom-call | flops 154618822656 | bytes 157286400 | tf_op jit(solution)/shard_map/conv_mlp_back/pallas_call | solution.py:121
  505.4 11.7 conv_norm_back.1
  517.1 85.5 %vit_mlp.1 = (bf16[4,288,1024]{2,1,0:T(8,128)(2,1)}, f32[4,288,1024]{2,1,0:T(8,128)}, bf16[16,1536,256]{2,1,0:T(8,128)(2,1)}, bf16[16,1536,256]{2,1,0:T(8,128)(2,1)}) custom-call(s32[2]{0:T(128)} %pad_add_fusion.refs_0_, bf16[4,288,1024]{2,1,0:T(8,128)(2,1)} %get-tuple-element.144.refs_7_.refs_1_, bf16[4,1024,288]{2,1,0:T(8,128)(2,1)} %get-tuple-element.145.refs_2_, ...), custom_call_target="tpu_custom_call" | custom-call | flops 57982058496 | bytes 65536000 | tf_op jit(solution)/shard_map/vit_mlp/pallas_call | solution.py:121
  602.6 21.4 %split_sum.8 = (bf16[8,832,256]{2,1,0:T(8,128)(2,1)}, bf16[8,832,256]{2,1,0:T(8,128)(2,1)}, bf16[8,832,256]{2,1,0:T(8,128)(2,1)}, bf16[8,832,256]{2,1,0:T(8,128)...) custom-call(s32[3]{0:T(128)} %pad_add_fusion.2.refs_0_, ...), custom_call_target="tpu_custom_call" | custom-call | bytes 265814016 | tf_op jit(solution)/shard_map/split_sum/pallas_call | solution.py:121
  623.9 16.4 %vit_back.1 = (f32[4,288,1024]{2,1,0:T(8,128)}, bf16[4,288,1024]{2,1,0:T(8,128)(2,1)}, f32[8,1024]{1,0:T(8,128)}, bf16[16,1536,256]{2,1,0:T(8,128)(2,1)}, bf16[16,1536,256]{2,1,0:T(8,128)(2,1)}) custom-call(s32[2]{0:T(128)} %pad_add_fusion.refs_0_, f32[4,288,1024]{2,1,0:T(8,128)} %get-tuple-element.146.refs_4_.refs_1_, ...), custom_call_target="tpu_custom_call", output_to_operand_aliasing={{3}: (7, {}), {4}: (8, {})} | custom-call | flops 4831838208 | bytes 73703424 | tf_op jit(solution)/shard_map/vit_back/pallas_call | solution.py:121
  640.3 43.5 %attention_back.1 = (bf16[4,288,1024]{2,1,0:T(8,128)(2,1)}, bf16[4,576,1024]{2,1,0:T(8,128)(2,1)}, bf16[4,576,1024]{2,1,0:T(8,128)(2,1)}) custom-call(s32[2]{0:T(128)} %pad_add_fusion.refs_0_, bf16[4,16,576,288]{3,2,1,0:T(8,128)(2,1)} %get-tuple-element.163.refs_1_, bf16[4,288,1024]{2,1,0:T(8,128)(2,1)} %get-tuple-element.164.refs_2_, ...), custom_call_target="tpu_custom_call" | custom-call | flops 10871635968 | bytes 56623104 | tf_op jit(solution)/shard_map/attention_back/pallas_call | solution.py:121
  683.8 34.4 %qkv_back.1 = (f32[4,576,1024]{2,1,0:T(8,128)}, bf16[16,1536,256]{2,1,0:T(8,128)(2,1)}, bf16[16,1536,256]{2,1,0:T(8,128)(2,1)}) custom-call(s32[2]{0:T(128)} %pad_add_fusion.refs_0_, bf16[4,576,1024]{2,1,0:T(8,128)(2,1)} %get-tuple-element.162.refs_1_, ...), custom_call_target="tpu_custom_call", output_to_operand_aliasing={{1}: (6, {}), {2}: (7, {})} | custom-call | flops 24159191040 | bytes 82575360 | tf_op jit(solution)/shard_map/qkv_back/pallas_call | solution.py:121
  718.3 161.3 %collective-permute-start.11 = (bf16[8,832,256]{2,1,0:T(8,128)(2,1)}, bf16[8,832,256]{2,1,0:T(8,128)(2,1)S(1)}, u32[]{:S(2)}, u32[]{:S(2)}) collective-permute-start(bf16[8,832,256]{2,1,0:T(8,128)(2,1)} %get-tuple-element.185), channel_id=1, source_target_pairs={{0,4},{2,6},{4,0},{6,2},{8,12},{10,14},{12,8},{14,10},{16,20},{18,... | collective-permute-start | bytes 10223624 | tf_op jit(solution)/shard_map/ppermute | solution.py:1282
  879.6 3.3 fusion.7
  884.1 69.5 %collective-permute-done.11.refs_6_.refs_8_ = bf16[8,832,256]{2,1,0:T(8,128)(2,1)S(1)} collective-permute-done((bf16[8,832,256]{2,1,0:T(8,128)(2,1)}, bf16[8,832,256]{2,1,0:T(8,128)(2,1)S(1)}, u32[]{:S(2)}, u32[]{:S(2)}) %collective-permute-start.11) | collective-permute-done | bytes 3407904 | tf_op jit(solution)/shard_map/ppermute | solution.py:1282
  957.3 4.1 slice.152
  961.4 12.0 split_sum.9
  973.5 6.2 collective-permute-done.17.refs_6_
  980.6 72.4 %conv_back.1 = (bf16[4,16,32,1536]{3,2,1,0:T(8,128)(2,1)}, f32[64,1536]{1,0:T(8,128)}) custom-call(s32[2]{0:T(128)} %pad_add_fusion.refs_0_, bf16[4,3,32,1536]{3,2,1,0:T(8,128)(2,1)} %collective-permute-done.1.refs_1_, bf16[4,16,32,1536]{3,2,1,0:T(8,128)(2,1)} %refs_2_.5, bf16[4,3,32,1536]{3,2,1,0:T(8,128)(2,1)} %collective-permute-done.2.refs_3_, ...), custom_call_target="tpu_custom_call" | custom-call | flops 24662507520 | bytes 30578688 | tf_op jit(solution)/shard_map/conv_back/pallas_call | solution.py:121
  1053.0 13.9 %collective-permute-done.15.refs_10_.refs_12_ = bf16[4,832,256]{2,1,0:T(8,128)(2,1)S(1)} collective-permute-done((bf16[4,832,256]{2,1,0:T(8,128)(2,1)}, bf16[4,832,256]{2,1,0:T(8,128)(2,1)S(1)}, u32[]{:S(2)}, u32[]{:S(2)}) %collective-permute-start.15) | collective-permute-done | bytes 1703968 | tf_op jit(solution)/shard_map/ppermute | solution.py:1282
  1068.1 6.8 split_sum.10
  1077.0 15.1 %split_sum.11 = (bf16[8,512,256]{2,1,0:T(8,128)(2,1)}, bf16[8,512,256]{2,1,0:T(8,128)(2,1)}, bf16[8,512,256]{2,1,0:T(8,128)(2,1)}, bf16[8,512,256]{2,1,0:T(8,128...) custom-call(s32[3]{0:T(128)} %pad_add_fusion.2.refs_0_, ...), custom_call_target="tpu_custom_call" | custom-call | bytes 163577856 | tf_op jit(solution)/shard_map/split_sum/pallas_call | solution.py:121
  1092.1 9.3 collective-permute-start.19
  1109.4 8.4 tokens_back.1
  1117.9 42.8 %collective-permute-done.23.refs_10_.refs_12_ = bf16[2,832,256]{2,1,0:T(8,128)(2,1)} collective-permute-done((bf16[2,832,256]{2,1,0:T(8,128)(2,1)}, bf16[2,832,256]{2,1,0:T(8,128)(2,1)}, u32[]{:S(2)}, u32[]{:S(2)}) %collective-permute-start.23) | collective-permute-done | bytes 852000 | tf_op jit(solution)/shard_map/ppermute | solution.py:1282
  1162.5 4.8 split_sum.12
  1171.3 8.5 split_sum.13
  1186.3 8.9 collective-permute-done.35
  1198.4 6.7 collective-permute-done.36
  1207.1 15.2 %collective-permute-done.34 = bf16[1,832,256]{2,1,0:T(8,128)(2,1)S(1)} collective-permute-done((bf16[1,832,256]{2,1,0:T(8,128)(2,1)}, bf16[1,832,256]{2,1,0:T(8,128)(2,1)S(1)}, u32[]{:S(2)}, u32[]{:S(2)}) %collective-permute-start.34) | collective-permute-done | bytes 426016 | tf_op jit(solution)/shard_map/ppermute | solution.py:1282
  1224.7 5.1 split_sum.14
  1232.3 6.0 conditional.3
  1242.2 77.4 %all-reduce.4.cloned.1.call-done = f32[87040]{0:T(1024)} async-done(((f32[87040]{0:T(1024)}), f32[87040]{0:T(1024)}) %all-reduce.4.cloned.1.call-update) | async-done | bytes 348176 | tf_op jit(solution)/shard_map/psum | solution.py:1532
  1319.6 3.8 split_sum.15
  1327.6 19.1 %collective-permute-done.31 = bf16[1,512,256]{2,1,0:T(8,128)(2,1)S(1)} collective-permute-done((bf16[1,512,256]{2,1,0:T(8,128)(2,1)}, bf16[1,512,256]{2,1,0:T(8,128)(2,1)S(1)}, u32[]{:S(2)}, u32[]{:S(2)}) %collective-permute-start.31) | collective-permute-done | bytes 262176 | tf_op jit(solution)/shard_map/ppermute | solution.py:1282
  1347.7 4.6 collective-permute-done.32
  1354.1 3.8 collective-permute-done.30
  1360.9 5.3 collective-permute-start.33
  1366.2 4.6 fusion
  (170 shorter events, 82.2 us)
Async XLA Ops:
  7.2 13.7 copy-start.19
  7.2 1312.4 %all-reduce.4.cloned.1.call-start = ((), (), s32[]{:S(2)}) async-start(), calls=%async_computation | async-start | bytes 696320 | tf_op jit(solution)/shard_map/psum | solution.py:1532
  10.3 29.0 %collective-permute-start.2 = (bf16[4,3,32,1536]{3,2,1,0:T(8,128)(2,1)}, bf16[4,3,32,1536]{3,2,1,0:T(8,128)(2,1)}, u32[]{:S(2)}, u32[]{:S(2)}) collective-permute-start(bf16[4,3,32,1536]{3,2,1,0:T(8,128)(2,1)} %get-tuple-element.244), channel_id=1, source_target_pairs={{1,0},{3,2},{5,4},{7,6},{9,8},{11,10},{13,12},{15,14},{17,16},{19,... | collective-permute-start | bytes 3538952 | tf_op jit(solution)/shard_map/ppermute | solution.py:1178
  11.5 29.3 %collective-permute-start.1 = (bf16[4,3,32,1536]{3,2,1,0:T(8,128)(2,1)S(1)}, bf16[4,3,32,1536]{3,2,1,0:T(8,128)(2,1)}, u32[]{:S(2)}, u32[]{:S(2)}) collective-permute-start(bf16[4,3,32,1536]{3,2,1,0:T(8,128)(2,1)S(1)} %get-tuple-element.245), channel_id=1, source_target_pairs={{0,1},{2,3},{4,5},{6,7},{8,9},{10,11},{12,13},{14,15},{16,17},{18,... | collective-permute-start | bytes 3538952 | tf_op jit(solution)/shard_map/ppermute | solution.py:1177
  17.6 188.2 %collective-permute-start = (bf16[4,288,1024]{2,1,0:T(8,128)(2,1)S(1)}, bf16[4,288,1024]{2,1,0:T(8,128)(2,1)}, u32[]{:S(2)}, u32[]{:S(2)}) collective-permute-start(bf16[4,288,1024]{2,1,0:T(8,128)(2,1)S(1)} %copy-done.3), channel_id=1, source_target_pairs={{0,1},{1,0},{2,3},{3,2},{4,5},{5,4},{6,7},{7,6},{8,9},{9,8},{10,11... | collective-permute-start | bytes 7077896 | tf_op jit(solution)/shard_map/ppermute | solution.py:1425
  200.0 72.9 %collective-permute-start.3 = (bf16[4,24,1536]{2,1,0:T(8,128)(2,1)}, bf16[4,24,1536]{2,1,0:T(8,128)(2,1)S(1)}, u32[]{:S(2)}, u32[]{:S(2)}) collective-permute-start(bf16[4,24,1536]{2,1,0:T(8,128)(2,1)} %get-tuple-element.147), channel_id=1, source_target_pairs={{0,1},{2,3},{4,5},{6,7},{8,9},{10,11},{12,13},{14,15},{16,17},{18,... | collective-permute-start | bytes 884744 | tf_op jit(solution)/shard_map/ppermute | solution.py:1177
  204.3 68.7 %collective-permute-start.4 = (bf16[4,24,1536]{2,1,0:T(8,128)(2,1)}, bf16[4,24,1536]{2,1,0:T(8,128)(2,1)S(1)}, u32[]{:S(2)}, u32[]{:S(2)}) collective-permute-start(bf16[4,24,1536]{2,1,0:T(8,128)(2,1)} %get-tuple-element.148), channel_id=1, source_target_pairs={{1,0},{3,2},{5,4},{7,6},{9,8},{11,10},{13,12},{15,14},{17,16},{19,... | collective-permute-start | bytes 884744 | tf_op jit(solution)/shard_map/ppermute | solution.py:1178
  273.8 25.2 %copy-start.11 = (bf16[336,512]{1,0:T(8,128)(2,1)S(1)}, bf16[336,512]{1,0:T(8,128)(2,1)}, u32[]{:S(2)}) copy-start(bf16[336,512]{1,0:T(8,128)(2,1)} %convert_element_type.81.refs_2_) | copy-start | bytes 1032196
  293.3 7.7 collective-permute-start.5
  297.3 7.5 collective-permute-start.6
  504.6 98.0 %collective-permute-start.7 = (bf16[16,2496,256]{2,1,0:T(8,128)(2,1)}, bf16[16,2496,256]{2,1,0:T(8,128)(2,1)}, u32[]{:S(2)}, u32[]{:S(2)}) collective-permute-start(bf16[16,2496,256]{2,1,0:T(8,128)(2,1)} %get-tuple-element.171), channel_id=1, source_target_pairs={{0,2},{2,0},{4,6},{6,4},{8,10},{10,8},{12,14},{14,12},{16,18},{18,... | collective-permute-start | bytes 61341704 | tf_op jit(solution)/shard_map/ppermute | solution.py:1282
  718.2 358.8 %collective-permute-start.9 = (bf16[16,1536,256]{2,1,0:T(8,128)(2,1)}, bf16[16,1536,256]{2,1,0:T(8,128)(2,1)}, u32[]{:S(2)}, u32[]{:S(2)}) collective-permute-start(bf16[16,1536,256]{2,1,0:T(8,128)(2,1)} %get-tuple-element.182), channel_id=1, source_target_pairs={{0,2},{2,0},{4,6},{6,4},{8,10},{10,8},{12,14},{14,12},{16,18},{18,... | collective-permute-start | bytes 37748744 | tf_op jit(solution)/shard_map/ppermute | solution.py:1282
  718.3 235.3 %collective-permute-start.11 = (bf16[8,832,256]{2,1,0:T(8,128)(2,1)}, bf16[8,832,256]{2,1,0:T(8,128)(2,1)S(1)}, u32[]{:S(2)}, u32[]{:S(2)}) collective-permute-start(bf16[8,832,256]{2,1,0:T(8,128)(2,1)} %get-tuple-element.185), channel_id=1, source_target_pairs={{0,4},{2,6},{4,0},{6,2},{8,12},{10,14},{12,8},{14,10},{16,20},{18,... | collective-permute-start | bytes 10223624 | tf_op jit(solution)/shard_map/ppermute | solution.py:1282
  879.6 81.8 %collective-permute-start.12 = (bf16[8,832,256]{2,1,0:T(8,128)(2,1)}, bf16[8,832,256]{2,1,0:T(8,128)(2,1)}, u32[]{:S(2)}, u32[]{:S(2)}) collective-permute-start(bf16[8,832,256]{2,1,0:T(8,128)(2,1)} %get-tuple-element.187), channel_id=1, source_target_pairs={{0,8},{2,10},{4,12},{6,14},{8,0},{10,2},{12,4},{14,6},{16,24},{18,... | collective-permute-start | bytes 10223624 | tf_op jit(solution)/shard_map/ppermute | solution.py:1282
  879.6 81.8 %collective-permute-start.10 = (bf16[8,832,256]{2,1,0:T(8,128)(2,1)}, bf16[8,832,256]{2,1,0:T(8,128)(2,1)}, u32[]{:S(2)}, u32[]{:S(2)}) collective-permute-start(bf16[8,832,256]{2,1,0:T(8,128)(2,1)} %get-tuple-element.172.refs_9_), channel_id=1, source_target_pairs={{0,1},{1,0},{2,3},{3,2},{4,5},{5,4},{6,7},{7,6},{8,9},{9,8},{10,11... | collective-permute-start | bytes 10223624 | tf_op jit(solution)/shard_map/ppermute | solution.py:1282
  882.9 96.9 %collective-permute-start.17 = (bf16[4,3,32,1536]{3,2,1,0:T(8,128)(2,1)}, bf16[4,3,32,1536]{3,2,1,0:T(8,128)(2,1)}, u32[]{:S(2)}, u32[]{:S(2)}) collective-permute-start(bf16[4,3,32,1536]{3,2,1,0:T(8,128)(2,1)} %get-tuple-element.242), channel_id=1, source_target_pairs={{1,0},{3,2},{5,4},{7,6},{9,8},{11,10},{13,12},{15,14},{17,16},{19,... | collective-permute-start | bytes 3538952 | tf_op jit(solution)/shard_map/ppermute | solution.py:1178
  953.6 26.2 %collective-permute-start.16 = (bf16[4,3,32,1536]{3,2,1,0:T(8,128)(2,1)}, bf16[4,3,32,1536]{3,2,1,0:T(8,128)(2,1)}, u32[]{:S(2)}, u32[]{:S(2)}) collective-permute-start(bf16[4,3,32,1536]{3,2,1,0:T(8,128)(2,1)} %get-tuple-element.243), channel_id=1, source_target_pairs={{0,1},{2,3},{4,5},{6,7},{8,9},{10,11},{12,13},{14,15},{16,17},{18,... | collective-permute-start | bytes 3538952 | tf_op jit(solution)/shard_map/ppermute | solution.py:1177
  961.4 140.0 %collective-permute-start.8 = (bf16[4,288,1024]{2,1,0:T(8,128)(2,1)}, bf16[4,288,1024]{2,1,0:T(8,128)(2,1)}, u32[]{:S(2)}, u32[]{:S(2)}) collective-permute-start(bf16[4,288,1024]{2,1,0:T(8,128)(2,1)} %slice.152), channel_id=1, source_target_pairs={{0,1},{1,0},{2,3},{3,2},{4,5},{5,4},{6,7},{7,6},{8,9},{9,8},{10,11... | collective-permute-start | bytes 7077896 | tf_op jit(solution)/shard_map/ppermute | solution.py:1425
  973.4 79.6 %collective-permute-start.14 = (bf16[4,832,256]{2,1,0:T(8,128)(2,1)}, bf16[4,832,256]{2,1,0:T(8,128)(2,1)S(1)}, u32[]{:S(2)}, u32[]{:S(2)}) collective-permute-start(bf16[4,832,256]{2,1,0:T(8,128)(2,1)} %get-tuple-element.191), channel_id=1, source_target_pairs={{0,8},{2,10},{4,12},{6,14},{8,0},{10,2},{12,4},{14,6},{16,24},{18,... | collective-permute-start | bytes 5111816 | tf_op jit(solution)/shard_map/ppermute | solution.py:1282
  979.7 87.2 %collective-permute-start.15 = (bf16[4,832,256]{2,1,0:T(8,128)(2,1)}, bf16[4,832,256]{2,1,0:T(8,128)(2,1)S(1)}, u32[]{:S(2)}, u32[]{:S(2)}) collective-permute-start(bf16[4,832,256]{2,1,0:T(8,128)(2,1)} %get-tuple-element.193), channel_id=1, source_target_pairs={{0,1},{1,0},{2,3},{3,2},{4,5},{5,4},{6,7},{7,6},{8,9},{9,8},{10,11... | collective-permute-start | bytes 5111816 | tf_op jit(solution)/shard_map/ppermute | solution.py:1282
  979.8 87.1 %collective-permute-start.13 = (bf16[4,832,256]{2,1,0:T(8,128)(2,1)}, bf16[4,832,256]{2,1,0:T(8,128)(2,1)}, u32[]{:S(2)}, u32[]{:S(2)}) collective-permute-start(bf16[4,832,256]{2,1,0:T(8,128)(2,1)} %get-tuple-element.189.refs_9_), channel_id=1, source_target_pairs={{0,4},{2,6},{4,0},{6,2},{8,12},{10,14},{12,8},{14,10},{16,20},{18,... | collective-permute-start | bytes 5111816 | tf_op jit(solution)/shard_map/ppermute | solution.py:1282
  1053.0 13.9 %copy-start.5 = (bf16[4,832,256]{2,1,0:T(8,128)(2,1)}, bf16[4,832,256]{2,1,0:T(8,128)(2,1)S(1)}, u32[]{:S(2)}) copy-start(bf16[4,832,256]{2,1,0:T(8,128)(2,1)S(1)} %collective-permute-done.14.refs_6_.refs_8_) | copy-start | bytes 5111812
  1074.9 26.8 %collective-permute-start.22 = (bf16[2,832,256]{2,1,0:T(8,128)(2,1)}, bf16[2,832,256]{2,1,0:T(8,128)(2,1)S(1)}, u32[]{:S(2)}, u32[]{:S(2)}) collective-permute-start(bf16[2,832,256]{2,1,0:T(8,128)(2,1)} %get-tuple-element.206), channel_id=1, source_target_pairs={{0,1},{1,0},{2,3},{3,2},{4,5},{5,4},{6,7},{7,6},{8,9},{9,8},{10,11... | collective-permute-start | bytes 2555912 | tf_op jit(solution)/shard_map/ppermute | solution.py:1282
  1077.0 25.9 %copy-start.24 = (s32[32]{0:T(128)S(1)}, s32[32]{0:T(128)}, u32[]{:S(2)}) copy-start(s32[32]{0:T(128)} %constant.57.clone) | copy-start | bytes 388
  1092.1 77.6 %collective-permute-start.19 = (bf16[8,512,256]{2,1,0:T(8,128)(2,1)}, bf16[8,512,256]{2,1,0:T(8,128)(2,1)S(1)}, u32[]{:S(2)}, u32[]{:S(2)}) collective-permute-start(bf16[8,512,256]{2,1,0:T(8,128)(2,1)} %get-tuple-element.201), channel_id=1, source_target_pairs={{0,4},{2,6},{4,0},{6,2},{8,12},{10,14},{12,8},{14,10},{16,20},{18,... | collective-permute-start | bytes 6291464 | tf_op jit(solution)/shard_map/ppermute | solution.py:1282
  1101.4 68.4 %collective-permute-start.20 = (bf16[8,512,256]{2,1,0:T(8,128)(2,1)}, bf16[8,512,256]{2,1,0:T(8,128)(2,1)}, u32[]{:S(2)}, u32[]{:S(2)}) collective-permute-start(bf16[8,512,256]{2,1,0:T(8,128)(2,1)} %get-tuple-element.203), channel_id=1, source_target_pairs={{0,8},{2,10},{4,12},{6,14},{8,0},{10,2},{12,4},{14,6},{16,24},{18,... | collective-permute-start | bytes 6291464 | tf_op jit(solution)/shard_map/ppermute | solution.py:1282
  1101.4 68.4 %collective-permute-start.18 = (bf16[8,512,256]{2,1,0:T(8,128)(2,1)}, bf16[8,512,256]{2,1,0:T(8,128)(2,1)}, u32[]{:S(2)}, u32[]{:S(2)}) collective-permute-start(bf16[8,512,256]{2,1,0:T(8,128)(2,1)} %get-tuple-element.197.refs_6_), channel_id=1, source_target_pairs={{0,1},{1,0},{2,3},{3,2},{4,5},{5,4},{6,7},{7,6},{8,9},{9,8},{10,11... | collective-permute-start | bytes 6291464 | tf_op jit(solution)/shard_map/ppermute | solution.py:1282
  1101.4 59.2 %collective-permute-start.23 = (bf16[2,832,256]{2,1,0:T(8,128)(2,1)}, bf16[2,832,256]{2,1,0:T(8,128)(2,1)}, u32[]{:S(2)}, u32[]{:S(2)}) collective-permute-start(bf16[2,832,256]{2,1,0:T(8,128)(2,1)} %get-tuple-element.208), channel_id=1, source_target_pairs={{0,4},{2,6},{4,0},{6,2},{8,12},{10,14},{12,8},{14,10},{16,20},{18,... | collective-permute-start | bytes 2555912 | tf_op jit(solution)/shard_map/ppermute | solution.py:1282
  1101.7 16.2 %copy-start.9 = (bf16[2,832,256]{2,1,0:T(8,128)(2,1)}, bf16[2,832,256]{2,1,0:T(8,128)(2,1)S(1)}, u32[]{:S(2)}) copy-start(bf16[2,832,256]{2,1,0:T(8,128)(2,1)S(1)} %collective-permute-done.22.refs_6_.refs_8_) | copy-start | bytes 2555908
  1101.7 60.4 %collective-permute-start.21 = (bf16[2,832,256]{2,1,0:T(8,128)(2,1)}, bf16[2,832,256]{2,1,0:T(8,128)(2,1)}, u32[]{:S(2)}, u32[]{:S(2)}) collective-permute-start(bf16[2,832,256]{2,1,0:T(8,128)(2,1)} %get-tuple-element.196.refs_13_), channel_id=1, source_target_pairs={{0,8},{2,10},{4,12},{6,14},{8,0},{10,2},{12,4},{14,6},{16,24},{18,... | collective-permute-start | bytes 2555912 | tf_op jit(solution)/shard_map/ppermute | solution.py:1282
  1167.3 27.9 %collective-permute-start.35 = (bf16[1,832,256]{2,1,0:T(8,128)(2,1)}, bf16[1,832,256]{2,1,0:T(8,128)(2,1)}, u32[]{:S(2)}, u32[]{:S(2)}) collective-permute-start(bf16[1,832,256]{2,1,0:T(8,128)(2,1)} %get-tuple-element.236), channel_id=1, source_target_pairs={{0,24},{2,26},{4,28},{6,30},{8,16},{10,18},{12,20},{14,22},{16,8},... | collective-permute-start | bytes 1277960 | tf_op jit(solution)/shard_map/ppermute | solution.py:1282
  1168.6 36.5 %collective-permute-start.36 = (bf16[1,832,256]{2,1,0:T(8,128)(2,1)}, bf16[1,832,256]{2,1,0:T(8,128)(2,1)S(1)}, u32[]{:S(2)}, u32[]{:S(2)}) collective-permute-start(bf16[1,832,256]{2,1,0:T(8,128)(2,1)} %get-tuple-element.238), channel_id=1, source_target_pairs={{0,24},{2,26},{4,28},{6,30},{8,16},{10,18},{12,20},{14,22},{16,8},... | collective-permute-start | bytes 1277960 | tf_op jit(solution)/shard_map/ppermute | solution.py:1282
  1171.3 25.1 %copy-start.15 = (bf16[1,832,256]{2,1,0:T(8,128)(2,1)S(1)}, bf16[1,832,256]{2,1,0:T(8,128)(2,1)}, u32[]{:S(2)}) copy-start(bf16[1,832,256]{2,1,0:T(8,128)(2,1)} %get-tuple-element.235) | copy-start | bytes 1277956
  1179.7 42.6 %copy-start.14 = (bf16[1,832,256]{2,1,0:T(8,128)(2,1)S(1)}, bf16[1,832,256]{2,1,0:T(8,128)(2,1)}, u32[]{:S(2)}) copy-start(bf16[1,832,256]{2,1,0:T(8,128)(2,1)} %get-tuple-element.234) | copy-start | bytes 1277956
  1179.7 43.6 %collective-permute-start.24 = (bf16[4,512,256]{2,1,0:T(8,128)(2,1)}, bf16[4,512,256]{2,1,0:T(8,128)(2,1)S(1)}, u32[]{:S(2)}, u32[]{:S(2)}) collective-permute-start(bf16[4,512,256]{2,1,0:T(8,128)(2,1)} %get-tuple-element.211), channel_id=1, source_target_pairs={{0,4},{2,6},{4,0},{6,2},{8,12},{10,14},{12,8},{14,10},{16,20},{18,... | collective-permute-start | bytes 3145736 | tf_op jit(solution)/shard_map/ppermute | solution.py:1282
  1180.1 43.2 %collective-permute-start.25 = (bf16[4,512,256]{2,1,0:T(8,128)(2,1)}, bf16[4,512,256]{2,1,0:T(8,128)(2,1)S(1)}, u32[]{:S(2)}, u32[]{:S(2)}) collective-permute-start(bf16[4,512,256]{2,1,0:T(8,128)(2,1)} %get-tuple-element.213), channel_id=1, source_target_pairs={{0,8},{2,10},{4,12},{6,14},{8,0},{10,2},{12,4},{14,6},{16,24},{18,... | collective-permute-start | bytes 3145736 | tf_op jit(solution)/shard_map/ppermute | solution.py:1282
  1181.7 41.7 %collective-permute-start.26 = (bf16[4,512,256]{2,1,0:T(8,128)(2,1)}, bf16[4,512,256]{2,1,0:T(8,128)(2,1)}, u32[]{:S(2)}, u32[]{:S(2)}) collective-permute-start(bf16[4,512,256]{2,1,0:T(8,128)(2,1)} %get-tuple-element.215), channel_id=1, source_target_pairs={{0,1},{1,0},{2,3},{3,2},{4,5},{5,4},{6,7},{7,6},{8,9},{9,8},{10,11... | collective-permute-start | bytes 3145736 | tf_op jit(solution)/shard_map/ppermute | solution.py:1282
  1195.2 27.2 %collective-permute-start.34 = (bf16[1,832,256]{2,1,0:T(8,128)(2,1)}, bf16[1,832,256]{2,1,0:T(8,128)(2,1)S(1)}, u32[]{:S(2)}, u32[]{:S(2)}) collective-permute-start(bf16[1,832,256]{2,1,0:T(8,128)(2,1)} %get-tuple-element.209.refs_13_), channel_id=1, source_target_pairs={{0,24},{2,26},{4,28},{6,30},{8,16},{10,18},{12,20},{14,22},{16,8},... | collective-permute-start | bytes 1277960 | tf_op jit(solution)/shard_map/ppermute | solution.py:1282
  1229.8 89.8 %collective-permute-start.27 = (bf16[2,512,256]{2,1,0:T(8,128)(2,1)}, bf16[2,512,256]{2,1,0:T(8,128)(2,1)}, u32[]{:S(2)}, u32[]{:S(2)}) collective-permute-start(bf16[2,512,256]{2,1,0:T(8,128)(2,1)} %get-tuple-element.217), channel_id=1, source_target_pairs={{0,8},{2,10},{4,12},{6,14},{8,0},{10,2},{12,4},{14,6},{16,24},{18,... | collective-permute-start | bytes 1572872 | tf_op jit(solution)/shard_map/ppermute | solution.py:1282
  1229.9 89.7 %collective-permute-start.28 = (bf16[2,512,256]{2,1,0:T(8,128)(2,1)}, bf16[2,512,256]{2,1,0:T(8,128)(2,1)}, u32[]{:S(2)}, u32[]{:S(2)}) collective-permute-start(bf16[2,512,256]{2,1,0:T(8,128)(2,1)} %get-tuple-element.219), channel_id=1, source_target_pairs={{0,1},{1,0},{2,3},{3,2},{4,5},{5,4},{6,7},{7,6},{8,9},{9,8},{10,11... | collective-permute-start | bytes 1572872 | tf_op jit(solution)/shard_map/ppermute | solution.py:1282
  1230.0 89.6 %collective-permute-start.29 = (bf16[2,512,256]{2,1,0:T(8,128)(2,1)}, bf16[2,512,256]{2,1,0:T(8,128)(2,1)}, u32[]{:S(2)}, u32[]{:S(2)}) collective-permute-start(bf16[2,512,256]{2,1,0:T(8,128)(2,1)} %get-tuple-element.221), channel_id=1, source_target_pairs={{0,4},{2,6},{4,0},{6,2},{8,12},{10,14},{12,8},{14,10},{16,20},{18,... | collective-permute-start | bytes 1572872 | tf_op jit(solution)/shard_map/ppermute | solution.py:1282
  1238.3 85.2 %copy-start.2 = (f32[638976]{0:T(1024)}, f32[638976]{0:T(1024)S(1)}, u32[]{:S(2)}) copy-start(f32[638976]{0:T(1024)S(1)} %get-tuple-element.265) | copy-start | bytes 7667716
  1239.0 86.0 %collective-permute-start.37 = (bf16[82944]{0:T(1024)(128)(2,1)}, bf16[82944]{0:T(1024)(128)(2,1)}, u32[]{:S(2)}, u32[]{:S(2)}) collective-permute-start(bf16[82944]{0:T(1024)(128)(2,1)} %slice.153), channel_id=1, source_target_pairs={{1,0},{2,1},{3,2},{4,3},{5,4},{6,5},{7,6},{8,7},{9,8},{10,9},{11,1... | collective-permute-start | bytes 497672 | tf_op jit(solution)/shard_map/ppermute | solution.py:1377
  1323.5 34.4 %copy-start.18 = (bf16[1,512,256]{2,1,0:T(8,128)(2,1)S(1)}, bf16[1,512,256]{2,1,0:T(8,128)(2,1)}, u32[]{:S(2)}) copy-start(bf16[1,512,256]{2,1,0:T(8,128)(2,1)} %get-tuple-element.222) | copy-start | bytes 786436
  1323.5 23.2 %collective-permute-start.31 = (bf16[1,512,256]{2,1,0:T(8,128)(2,1)}, bf16[1,512,256]{2,1,0:T(8,128)(2,1)S(1)}, u32[]{:S(2)}, u32[]{:S(2)}) collective-permute-start(bf16[1,512,256]{2,1,0:T(8,128)(2,1)} %get-tuple-element.225), channel_id=1, source_target_pairs={{0,24},{2,26},{4,28},{6,30},{8,16},{10,18},{12,20},{14,22},{16,8},... | collective-permute-start | bytes 786440 | tf_op jit(solution)/shard_map/ppermute | solution.py:1282
  1324.4 27.9 %collective-permute-start.32 = (bf16[1,512,256]{2,1,0:T(8,128)(2,1)}, bf16[1,512,256]{2,1,0:T(8,128)(2,1)S(1)}, u32[]{:S(2)}, u32[]{:S(2)}) collective-permute-start(bf16[1,512,256]{2,1,0:T(8,128)(2,1)} %get-tuple-element.227), channel_id=1, source_target_pairs={{0,24},{2,26},{4,28},{6,30},{8,16},{10,18},{12,20},{14,22},{16,8},... | collective-permute-start | bytes 786440 | tf_op jit(solution)/shard_map/ppermute | solution.py:1282
  1326.8 31.1 %collective-permute-start.30 = (bf16[1,512,256]{2,1,0:T(8,128)(2,1)}, bf16[1,512,256]{2,1,0:T(8,128)(2,1)S(1)}, u32[]{:S(2)}, u32[]{:S(2)}) collective-permute-start(bf16[1,512,256]{2,1,0:T(8,128)(2,1)} %get-tuple-element.223), channel_id=1, source_target_pairs={{0,24},{2,26},{4,28},{6,30},{8,16},{10,18},{12,20},{14,22},{16,8},... | collective-permute-start | bytes 786440 | tf_op jit(solution)/shard_map/ppermute | solution.py:1282
  1360.9 9.9 collective-permute-start.33
  (16 other events, 75.2 us)
Sparse Core Ops, SparseCore 0:
  1186.5 133.1 all-reduce.3

commit v3 on v2

--- a/solution.py
+++ b/solution.py
@@ -109,10 +109,8 @@
     return pl.BlockSpec(shape, lambda *g: (0,) * len(shape))
 
 
-def run(name, body, grid, live, args, in_specs, outs, scratch=(), flops=0, after=(), alias=()):
+def run(name, body, grid, live, args, in_specs, outs, scratch=(), after=(), alias=()):
     out_shape = [jax.ShapeDtypeStruct(shape, dtype) for shape, dtype, _ in outs]
-    moved = sum(a.size * a.dtype.itemsize for a in args)
-    moved += sum(math.prod(s) * jnp.dtype(d).itemsize for s, d, _ in outs)
     count = 1 + len(args)
 
     def without_order(*refs):
@@ -132,9 +130,7 @@
         compiler_params=pltpu.CompilerParams(
             dimension_semantics=("arbitrary",) * len(grid), vmem_limit_bytes=VMEM_BYTES
         ),
-        cost_estimate=pl.CostEstimate(
-            flops=int(flops), bytes_accessed=int(moved), transcendentals=0
-        ),
+        cost_estimate=pl.CostEstimate(flops=0, bytes_accessed=0, transcendentals=0),
         name=name,
     )(live, *args, *after)
 
@@ -262,8 +258,6 @@
             over_rows(tok_rows, second_norm)
             flip_ref[0] = flip(inner_ref[0])
 
-    macs = slots * (key_rows * width * 2 * width + tok_rows * width * 2 * width)
-    macs += slots * 2 * HEADS * tok_rows * key_rows * LANES
     return run(
         "vit_front",
         body,
@@ -282,7 +276,6 @@
             ((slots, tok_rows, width), BF16, slot(tok_rows, width)),
             ((slots, width, tok_rows), BF16, slot(width, tok_rows)),
         ],
-        flops=2 * macs,
         after=after,
     )
 
@@ -309,12 +302,14 @@
         a2[...] = jnp.zeros(a2.shape, F32)
 
         def one(at, carry):
-            act, slope = gelu_pair(dot_nn(x_ref[at], w1_ref[...]))
+            before = dot_nn(x_ref[at], w1_ref[...])
+            d_act = dot_nt(dm_ref[at], w2_ref[...])
+            act, slope = gelu_pair(before)
             act = act.astype(BF16)
+            d_fc = (slope * d_act).astype(BF16)
             low[at] += dot_nn(act, w2_ref[...])
-            d_fc = (slope * dot_nt(dm_ref[at], w2_ref[...])).astype(BF16)
+            a2[...] += dot_tn(act, dm_ref[at])
             a1[...] += dot_nn(xt_ref[at], d_fc)
-            a2[...] += dot_tn(act, dm_ref[at])
             din_ref[at] += dot_nt(d_fc, w1_ref[...])
             return carry
 
@@ -403,7 +398,6 @@
         [whole(*wide), whole(*inner_flip.shape)] + [whole(*wide)] * 3 + [by_col, by_row],
         [(wide, BF16, result(*wide)), (wide, F32, result(*wide))] + grads,
         scratch,
-        flops=12 * slots * tok_rows * width * hidden,
         after=after,
     )
 
@@ -465,7 +459,6 @@
         specs,
         [(wide, F32, one), (wide, BF16, one), ((8, width), F32, result(8, width))] + grads,
         scratch,
-        flops=4 * slots * tok_rows * width * width,
         after=after,
         alias=alias,
     )
@@ -535,11 +528,10 @@
             ((slots, key_rows, width), BF16, keys),
             ((slots, key_rows, width), BF16, keys),
         ],
-        flops=8 * slots * HEADS * tok_rows * key_rows * LANES,
-    )
-
-
-def qkv_back(live, normed, d_q, d_k, d_v, w_qkv, flat, kept):
+    )
+
+
+def qkv_back(live, normed, d_q, d_k, d_v, w_qkv, flat, kept, after):
     slots, key_rows, width = normed.shape
     tok_rows = d_q.shape[1]
 
@@ -590,7 +582,7 @@
         specs,
         [(normed.shape, F32, keys)] + grads,
         scratch,
-        flops=4 * slots * width * width * (2 * key_rows + tok_rows),
+        after=after,
         alias=alias,
     )
 
@@ -713,14 +705,13 @@
             pltpu.VMEM((rows + 2 * REACH, cols + 2 * EDGE, LANES), F32),
             pltpu.VMEM((cells, channels), F32),
         ],
-        flops=2 * slots * cells * channels * KS * KS * 40,
     )
 
 
 def conv_mlp(live, spatial, high, w_pw1, w_pw2, gains):
     slots, cells, channels = spatial.shape
     hidden = w_pw1.shape[1]
-    block = 512
+    block = 1024
     steps = hidden // block
 
     def body(
@@ -728,21 +719,20 @@
     ):
         at, step = pl.program_id(0), pl.program_id(1)
 
+        @pl.when((at < n[0]) & (step == 0))
+        def _():
+            acc[...] = jnp.zeros(acc.shape, F32)
+
         @pl.when(at < n[0])
         def _():
-            act, slope = gelu_pair(dot_nn(x_ref[0], w1_ref[...]))
-            act = act.astype(BF16)
-            act_ref[0] = act
-            slope_ref[0] = slope.astype(BF16)
-            part = dot_nn(act, w2_ref[...])
-
-            @pl.when(step == 0)
-            def _():
-                acc[...] = part
-
-            @pl.when(step > 0)
-            def _():
-                acc[...] += part
+            parts = [slice(0, cells // 2), slice(cells // 2, cells)]
+            hidden_parts = [dot_nn(x_ref[0, rows, :], w1_ref[...]) for rows in parts]
+            for rows, value in zip(parts, hidden_parts):
+                act, slope = gelu_pair(value)
+                act = act.astype(BF16)
+                act_ref[0, rows, :] = act
+                slope_ref[0, rows, :] = slope.astype(BF16)
+                acc[rows, :] += dot_nn(act, w2_ref[...])
 
             @pl.when(step == steps - 1)
             def _():
@@ -786,7 +776,6 @@
             (spatial.shape, BF16, every_slot(cells, channels)),
         ],
         [pltpu.VMEM((cells, channels), F32)],
-        flops=4 * slots * cells * channels * hidden,
     )
 
 
@@ -814,7 +803,6 @@
             ((slots, side, channels), BF16, slot(side, channels)),
             ((slots, side, channels), BF16, slot(side, channels)),
         ],
-        flops=2 * slots * cells * channels * bins.shape[0],
     )
 
 
@@ -876,7 +864,6 @@
             ((8, channels), F32, result(8, channels)),
         ],
         [pltpu.VMEM(w_pool.shape, F32)],
-        flops=6 * slots * tok_rows * channels * width,
         after=after,
     )
 
@@ -915,14 +902,13 @@
             (d_conv.shape, BF16, one),
             ((8, channels), F32, result(8, channels)),
         ],
-        flops=2 * slots * cells * channels * near_rows,
     )
 
 
 def conv_mlp_back(live, spatial_flip, act, slope, d_branch, w_pw1, w_pw2, grad_pool, flat):
     slots, channels, cells = spatial_flip.shape
     hidden = w_pw1.shape[1]
-    block = BLOCK
+    block = 2 * BLOCK
     steps = hidden // block
     blocks = channels // BLOCK
 
@@ -931,20 +917,19 @@
         dsp_ref, out1_ref, out2_ref, a1, a2, dsp, sem, *rest,
     ):
         step = pl.program_id(0)
-        odd = lax.rem(step, 2)
 
         @pl.when(step == 0)
         def _():
             dsp[...] = jnp.zeros(dsp.shape, F32)
 
-        a1[odd] = jnp.zeros(a1.shape[1:], F32)
+        a1[...] = jnp.zeros(a1.shape, F32)
         a2[...] = jnp.zeros(a2.shape, F32)
 
         def one(at, carry):
             d_hidden = dot_nt(db_ref[at], w2_ref[...])
             d_expand = (slope_ref[at].astype(F32) * d_hidden).astype(BF16)
             a2[...] += dot_tn(act_ref[at], db_ref[at])
-            a1[odd] += dot_nn(xt_ref[at], d_expand)
+            a1[...] += dot_nn(xt_ref[at], d_expand)
             dsp[at] += dot_nt(d_expand, w1_ref[...])
             return carry
 
@@ -957,7 +942,7 @@
             out.wait()
 
         if flat is None:
-            out1_ref[...] = a1[odd].astype(BF16)
+            out1_ref[...] = a1[...].astype(BF16)
             out2_ref[...] = a2[...].astype(BF16)
             return
         stage1, stage2, sems1, sems2, sems3 = rest
@@ -1001,27 +986,20 @@
         @pl.when(step > 0)
         def _():
             seconds(step - 1, "wait")
+            firsts(step - 1, "wait")
 
         stage2[...] = a2[...].astype(BF16)
         seconds(step, "start")
-
-        @pl.when(odd == 1)
-        def _():
-            pair = step // 2
-
-            @pl.when(pair > 0)
-            def _():
-                firsts(pair - 1, "wait")
-
-            for index, (_, row, rows, _) in enumerate(flat.pieces[0]):
-                both = jnp.concatenate([a1[0, row : row + rows], a1[1, row : row + rows]], axis=0)
-                stage1[index, 0 : 2 * rows, :] = both.astype(BF16)
-            firsts(pair, "start")
+        for index, (_, row, rows, _) in enumerate(flat.pieces[0]):
+            part = a1[row : row + rows, :]
+            both = jnp.concatenate([part[:, 0:BLOCK], part[:, BLOCK:]], axis=0)
+            stage1[index, 0 : 2 * rows, :] = both.astype(BF16)
+        firsts(step, "start")
 
         @pl.when(step == steps - 1)
         def _():
             seconds(step, "wait")
-            firsts(step // 2, "wait")
+            firsts(step, "wait")
             copy_out(n[1], out1_ref, out2_ref, pool_copies(), sems3, "wait")
 
     by_col = pl.BlockSpec((channels, block), lambda j, n: (0, j))
@@ -1030,7 +1008,7 @@
     anywhere = pl.BlockSpec(memory_space=pl.ANY)
     wide = (slots, cells, channels)
     scratch = [
-        pltpu.VMEM((2, channels, block), F32),
+        pltpu.VMEM((channels, block), F32),
         pltpu.VMEM((block, channels), F32),
         pltpu.VMEM(wide, F32),
         pltpu.SemaphoreType.DMA,
@@ -1057,7 +1035,6 @@
         [whole(*spatial_flip.shape), by_hidden, by_hidden, whole(*wide), by_col, by_row, anywhere],
         [(wide, F32, anywhere)] + grads,
         scratch,
-        flops=8 * slots * cells * channels * hidden,
     )
 
 
@@ -1167,7 +1144,6 @@
             ((64, channels), F32, result(64, channels)),
         ],
         [pltpu.VMEM(frame_shape, F32), pltpu.VMEM(frame_shape, F32)],
-        flops=4 * slots * rows * cols * channels * KS * KS * 40,
         after=after,
     )
 
@@ -1205,6 +1181,16 @@
     send = lax.dynamic_index_in_dim(cells, 1 - own, 1, keepdims=False)
     got = lax.ppermute(send, axis, [(i, i ^ (1 << bit)) for i in range(size)])
     return (keep.astype(F32) + got.astype(F32)).astype(BF16)
+
+
+def sum_everywhere(values):
+    for axis in ("dp", "strip"):
+        size = lax.axis_size(axis)
+        step = 1
+        while step < size:
+            values = values + lax.ppermute(values, axis, [(i, i ^ step) for i in range(size)])
+            step *= 2
+    return values
 
 
 def bits(axis):
@@ -1482,8 +1468,13 @@
         tuple(vit_grads), order,
     )
     d_q, d_k, d_v = attention_back(live, probs, q, kv, d_mixed)
+    order = (d_q,)
+    if chunked:
+        kept, sends = split_sum(conv_flat, kept, arrived, 1, order)
+        arrived = sent(sends, 1)
+        order = (sends[0],)
     d_normed, *vit_grads_qkv = qkv_back(
-        live, normed, d_q, d_k, d_v, w_qkv, vit_flat, tuple(vit_grads_out)
+        live, normed, d_q, d_k, d_v, w_qkv, vit_flat, tuple(vit_grads_out), order
     )
     d_other = jnp.zeros(low_tokens.shape, BF16)
     for by in range(1, strips):
@@ -1491,10 +1482,7 @@
         d_other = d_other + shifted(part, -by) if by > 1 else shifted(part, -by)
     order = (d_normed,)
     if chunked:
-        kept, sends = split_sum(conv_flat, kept, arrived, 1, order)
-        arrived = sent(sends, 1)
         vit_arrived = across("core", vit_grads_qkv[1])
-        order = (sends[0],)
     grad_map, kernel_sums = conv_back(
         live,
         top,
@@ -1529,7 +1517,7 @@
             gate_sums[0],
         ]
     )
-    extras = lax.psum(jnp.concatenate([vit_extras, conv_extras]), ("dp", "strip"))
+    extras = sum_everywhere(jnp.concatenate([vit_extras, conv_extras]))
     vit_extras, conv_extras = extras[: vit_extras.shape[0]], extras[vit_extras.shape[0] :]
     if chunked:
         kept, sends = split_sum(conv_flat, kept, arrived, 3, (grad_tokens,))

time: 1390 us -> 1260 us (0.906)
  Pallas kernels: 786 us -> 418 us
  starting transfers between devices: 214 us -> 532 us
  waiting for transfers between devices: 287 us -> 228 us
    pallas_call x22, Pallas kernels: 786 us -> 418 us  [run(): pl.pallas_call(without_order, grid_spec=pltpu.PrefetchScalarGridSpec(num_...]
    ppermute x26, starting transfers between devices: 184 us -> 455 us  [across(): lax.ppermute(value, axis, [(i, i ^ flip_bits) for i in range(lax.axis_siz...]
    psum x1 -> x0, waiting for transfers between devices: 77.4 us -> none  [per_device(): lax.psum(jnp.concatenate([vit_extras, conv_extras]), ('dp', 'strip'))]
    ppermute x26, waiting for transfers between devices: 186 us -> 122 us  [across(): lax.ppermute(value, axis, [(i, i ^ flip_bits) for i in range(lax.axis_siz...]
    ppermute x4, waiting for transfers between devices: 21.1 us -> 83.4 us  [from_both_sides(): after = lax.ppermute(head, 'strip', [(i + 1, i) for i in range(count - 1)])]
    ppermute x0 -> x5, starting transfers between devices: none -> 50.5 us  [sum_everywhere(): lax.ppermute(values, axis, [(i, i ^ step) for i in range(size)])]
    ppermute x0 -> x5, waiting for transfers between devices: none -> 21.7 us  [sum_everywhere(): lax.ppermute(values, axis, [(i, i ^ step) for i in range(size)])]
  transfers between devices with their start and end apart: 39 -> 43, of which waited for: 17 -> 15; matrix products, arithmetic and copies ran while one was open for 4% -> 5% of each run, Pallas kernels for 33% -> 19%
where the time goes in v3:
time: 1260 us
  starting transfers between devices  532 us (42%)
  Pallas kernels  418 us (33%)
  waiting for transfers between devices  228 us (18%)
  other arithmetic  37.6 us (3%)
  local copies, waits for them, and re-layouts  37.3 us (3%)
    ppermute x26, starting transfers between devices, across(): lax.ppermute(value, axis, [(i, i ^ flip_bits) for i in range(lax.axis_siz...  455 us
    pallas_call x22, Pallas kernels, run(): pl.pallas_call(without_order, grid_spec=pltpu.PrefetchScalarGridSpec(num_...  418 us
    ppermute x26, waiting for transfers between devices, across(): lax.ppermute(value, axis, [(i, i ^ flip_bits) for i in range(lax.axis_siz...  122 us
    ppermute x4, waiting for transfers between devices, from_both_sides(): after = lax.ppermute(head, 'strip', [(i + 1, i) for i in range(count - 1)])  83.4 us
    ppermute x5, starting transfers between devices, sum_everywhere(): lax.ppermute(values, axis, [(i, i ^ step) for i in range(size)])  50.5 us
  transfers between devices with their start and end apart: 43, of which 15 were waited for; matrix products, arithmetic and copies ran while one was open for 5% of the time, Pallas kernels for 19%

profile of v3, /device:TPU:13, one launch (start us, length us, event | category | flops | bytes accessed | tf_op | source)
XLA Modules:
  0.0 1257.2 jit_solution(15117204166506076184)
XLA Ops:
  6.5 5.1 collective-permute-start.1
  17.7 60.6 %collective-permute-done.2.refs_3_ = bf16[4,3,32,1536]{3,2,1,0:T(8,128)(2,1)S(1)} collective-permute-done((bf16[4,3,32,1536]{3,2,1,0:T(8,128)(2,1)}, bf16[4,3,32,1536]{3,2,1,0:T(8,128)(2,1)S(1)}, u32[]{:S(2)}, u32[]{:S(2)}) %collective-permute-start.2) | collective-permute-done | bytes 1179680 | tf_op jit(solution)/shard_map/ppermute | solution.py:1154
  79.3 17.8 %conv_front.1 = (bf16[4,512,1536]{2,1,0:T(8,128)(2,1)}, bf16[4,1536,512]{2,1,0:T(8,128)(2,1)}, bf16[4,512,1536]{2,1,0:T(8,128)(2,1)}, f32[4,512,1]{2,1,0:T(8,128)}) custom-call(s32[2]{0:T(128)} %pad_add_fusion.refs_0_, bf16[4,3,32,1536]{3,2,1,0:T(8,128)(2,1)} %collective-permute-done.1.refs_1_, bf16[4,16,32,1536]{3,2,1,0:T(8,128)(2,1)} %refs_2_.5, ...), custom_call_target="tpu_custom_call" | custom-call | tf_op jit(solution)/shard_map/conv_front/pallas_call | solution.py:119
  97.2 34.9 %conv_mlp.1 = (bf16[4,512,6144]{2,1,0:T(8,128)(2,1)}, bf16[4,512,6144]{2,1,0:T(8,128)(2,1)}, bf16[4,512,1536]{2,1,0:T(8,128)(2,1)}, bf16[4,512,1536]{2,1,0:T(8,128)(2,1)}) custom-call(s32[2]{0:T(128)} %pad_add_fusion.refs_0_, bf16[4,512,1536]{2,1,0:T(8,128)(2,1)} %get-tuple-element.141.refs_1_, bf16[4,512,1536]{2,1,0:T(8,128)(2,1)} %bitcast.100, ...), custom_call_target="tpu_custom_call" | custom-call | tf_op jit(solution)/shard_map/conv_mlp/pallas_call | solution.py:119
  132.1 4.5 pool.1
  140.9 4.4 pad_maximum_fusion.4.refs_1_
  145.3 27.7 %vit_front.1 = (bf16[4,576,1024]{2,1,0:T(8,128)(2,1)}, bf16[4,288,1024]{2,1,0:T(8,128)(2,1)}, bf16[4,576,2048]{2,1,0:T(8,128)(2,1)}, bf16[4,16,576,288]{3,2,1,0:...) custom-call(s32[2]{0:T(128)} %pad_add_fusion.refs_0_, ...), custom_call_target="tpu_custom_call" | custom-call | tf_op jit(solution)/shard_map/vit_front/pallas_call | solution.py:119
  173.9 10.7 adapter.1
  185.7 4.0 collective-permute-start.5
  193.3 3.8 collective-permute-done.6
  197.2 3.9 pad_maximum_fusion.5.refs_1_
  201.1 6.6 unpool.1
  207.7 109.6 %conv_mlp_back.1 = (f32[4,512,1536]{2,1,0:T(8,128)}, bf16[16,2496,256]{2,1,0:T(8,128)(2,1)}, bf16[16,2496,256]{2,1,0:T(8,128)(2,1)}) custom-call(s32[2]{0:T(128)} %pad_add_fusion.refs_0_, bf16[4,1536,512]{2,1,0:T(8,128)(2,1)} %get-tuple-element.150.refs_1_, bf16[4,512,6144]{2,1,0:T(8,128)(2,1)} %get-tuple-element.151.refs_2_, ...), custom_call_target="tpu_custom_call" | custom-call | tf_op jit(solution)/shard_map/conv_mlp_back/pallas_call | solution.py:119
  317.3 176.7 %collective-permute-start.7 = (bf16[16,2496,256]{2,1,0:T(8,128)(2,1)}, bf16[16,2496,256]{2,1,0:T(8,128)(2,1)}, u32[]{:S(2)}, u32[]{:S(2)}) collective-permute-start(bf16[16,2496,256]{2,1,0:T(8,128)(2,1)} %get-tuple-element.171), channel_id=1, source_target_pairs={{0,2},{2,0},{4,6},{6,4},{8,10},{10,8},{12,14},{14,12},{16,18},{18,... | collective-permute-start | bytes 61341704 | tf_op jit(solution)/shard_map/ppermute | solution.py:1268
  494.5 6.6 conv_norm_back.1
  501.1 39.8 %vit_mlp.1 = (bf16[4,288,1024]{2,1,0:T(8,128)(2,1)}, f32[4,288,1024]{2,1,0:T(8,128)}, bf16[16,1536,256]{2,1,0:T(8,128)(2,1)}, bf16[16,1536,256]{2,1,0:T(8,128)(2,1)}) custom-call(s32[2]{0:T(128)} %pad_add_fusion.refs_0_, bf16[4,288,1024]{2,1,0:T(8,128)(2,1)} %get-tuple-element.144.refs_7_.refs_1_, bf16[4,1024,288]{2,1,0:T(8,128)(2,1)} %get-tuple-element.145.refs_2_, ...), custom_call_target="tpu_custom_call" | custom-call | tf_op jit(solution)/shard_map/vit_mlp/pallas_call | solution.py:119
  540.9 21.3 %split_sum.8 = (bf16[8,832,256]{2,1,0:T(8,128)(2,1)}, bf16[8,832,256]{2,1,0:T(8,128)(2,1)}, bf16[8,832,256]{2,1,0:T(8,128)(2,1)}, bf16[8,832,256]{2,1,0:T(8,128)...) custom-call(s32[3]{0:T(128)} %pad_add_fusion.2.refs_0_, ...), custom_call_target="tpu_custom_call" | custom-call | tf_op jit(solution)/shard_map/split_sum/pallas_call | solution.py:119
  562.3 149.2 %collective-permute-start.10 = (bf16[8,832,256]{2,1,0:T(8,128)(2,1)}, bf16[8,832,256]{2,1,0:T(8,128)(2,1)}, u32[]{:S(2)}, u32[]{:S(2)}) collective-permute-start(bf16[8,832,256]{2,1,0:T(8,128)(2,1)} %get-tuple-element.183), channel_id=1, source_target_pairs={{0,8},{2,10},{4,12},{6,14},{8,0},{10,2},{12,4},{14,6},{16,24},{18,... | collective-permute-start | bytes 10223624 | tf_op jit(solution)/shard_map/ppermute | solution.py:1268
  712.1 10.0 vit_back.1
  722.1 19.4 %attention_back.1 = (bf16[4,288,1024]{2,1,0:T(8,128)(2,1)}, bf16[4,576,1024]{2,1,0:T(8,128)(2,1)}, bf16[4,576,1024]{2,1,0:T(8,128)(2,1)}) custom-call(s32[2]{0:T(128)} %pad_add_fusion.refs_0_, bf16[4,16,576,288]{3,2,1,0:T(8,128)(2,1)} %get-tuple-element.163.refs_1_, bf16[4,288,1024]{2,1,0:T(8,128)(2,1)} %get-tuple-element.164.refs_2_, ...), custom_call_target="tpu_custom_call" | custom-call | tf_op jit(solution)/shard_map/attention_back/pallas_call | solution.py:119
  741.5 20.9 %collective-permute-done.10.refs_10_.refs_12_ = bf16[8,832,256]{2,1,0:T(8,128)(2,1)} collective-permute-done((bf16[8,832,256]{2,1,0:T(8,128)(2,1)}, bf16[8,832,256]{2,1,0:T(8,128)(2,1)}, u32[]{:S(2)}, u32[]{:S(2)}) %collective-permute-start.10) | collective-permute-done | bytes 3407904 | tf_op jit(solution)/shard_map/ppermute | solution.py:1268
  763.3 11.6 split_sum.9
  774.9 19.0 %qkv_back.1 = (f32[4,576,1024]{2,1,0:T(8,128)}, bf16[16,1536,256]{2,1,0:T(8,128)(2,1)}, bf16[16,1536,256]{2,1,0:T(8,128)(2,1)}) custom-call(s32[2]{0:T(128)} %pad_add_fusion.refs_0_, bf16[4,576,1024]{2,1,0:T(8,128)(2,1)} %get-tuple-element.162.refs_1_, ...), custom_call_target="tpu_custom_call", output_to_operand_aliasing={{1}: (6, {}), {2}: (7, {})} | custom-call | tf_op jit(solution)/shard_map/qkv_back/pallas_call | solution.py:119
  793.9 49.5 %collective-permute-start.12 = (bf16[16,1536,256]{2,1,0:T(8,128)(2,1)}, bf16[16,1536,256]{2,1,0:T(8,128)(2,1)}, u32[]{:S(2)}, u32[]{:S(2)}) collective-permute-start(bf16[16,1536,256]{2,1,0:T(8,128)(2,1)} %get-tuple-element.188), channel_id=1, source_target_pairs={{0,2},{2,0},{4,6},{6,4},{8,10},{10,8},{12,14},{14,12},{16,18},{18,... | collective-permute-start | bytes 37748744 | tf_op jit(solution)/shard_map/ppermute | solution.py:1268
  846.6 5.1 collective-permute-start.16
  851.7 4.1 slice.152
  855.8 19.0 %collective-permute-done.17.refs_6_ = bf16[4,3,32,1536]{3,2,1,0:T(8,128)(2,1)S(1)} collective-permute-done((bf16[4,3,32,1536]{3,2,1,0:T(8,128)(2,1)S(1)}, bf16[4,3,32,1536]{3,2,1,0:T(8,128)(2,1)S(1)}, u32[]{:S(2)}, u32[]{:S(2)}) %collective-permute-start.17) | collective-permute-done | bytes 1179680 | tf_op jit(solution)/shard_map/ppermute | solution.py:1154
  875.8 4.8 collective-permute-start.13
  884.7 28.9 %conv_back.1 = (bf16[4,16,32,1536]{3,2,1,0:T(8,128)(2,1)}, f32[64,1536]{1,0:T(8,128)}) custom-call(s32[2]{0:T(128)} %pad_add_fusion.refs_0_, bf16[4,3,32,1536]{3,2,1,0:T(8,128)(2,1)} %collective-permute-done.1.refs_1_, bf16[4,16,32,1536]{3,2,1,0:T(8,128)(2,1)} %refs_2_.5, bf16[4,3,32,1536]{3,2,1,0:T(8,128)(2,1)} %copy-done.7, ...), custom_call_target="tpu_custom_call" | custom-call | tf_op jit(solution)/shard_map/conv_back/pallas_call | solution.py:119
  917.1 45.8 %collective-permute-done.15.refs_10_.refs_12_ = bf16[4,832,256]{2,1,0:T(8,128)(2,1)S(1)} collective-permute-done((bf16[4,832,256]{2,1,0:T(8,128)(2,1)}, bf16[4,832,256]{2,1,0:T(8,128)(2,1)S(1)}, u32[]{:S(2)}, u32[]{:S(2)}) %collective-permute-start.15) | collective-permute-done | bytes 1703968 | tf_op jit(solution)/shard_map/ppermute | solution.py:1268
  964.1 6.8 split_sum.10
  973.0 15.0 %split_sum.11 = (bf16[8,512,256]{2,1,0:T(8,128)(2,1)}, bf16[8,512,256]{2,1,0:T(8,128)(2,1)}, bf16[8,512,256]{2,1,0:T(8,128)(2,1)}, bf16[8,512,256]{2,1,0:T(8,128...) custom-call(s32[3]{0:T(128)} %pad_add_fusion.2.refs_0_, ...), custom_call_target="tpu_custom_call" | custom-call | tf_op jit(solution)/shard_map/split_sum/pallas_call | solution.py:119
  988.1 5.8 tokens_back.1
  994.9 25.1 %collective-permute-start.20 = (bf16[8,512,256]{2,1,0:T(8,128)(2,1)}, bf16[8,512,256]{2,1,0:T(8,128)(2,1)}, u32[]{:S(2)}, u32[]{:S(2)}) collective-permute-start(bf16[8,512,256]{2,1,0:T(8,128)(2,1)} %get-tuple-element.203), channel_id=1, source_target_pairs={{0,8},{2,10},{4,12},{6,14},{8,0},{10,2},{12,4},{14,6},{16,24},{18,... | collective-permute-start | bytes 6291464 | tf_op jit(solution)/shard_map/ppermute | solution.py:1268
  1020.1 19.5 %collective-permute-start.33 = (f32[87040]{0:T(1024)S(1)}, f32[87040]{0:T(1024)S(1)}, u32[]{:S(2)}, u32[]{:S(2)}) collective-permute-start(f32[87040]{0:T(1024)S(1)} %constant_dynamic-update-slice_fusion), channel_id=1, source_target_pairs={{0,2},{2,0},{4,6},{6,4},{8,10},{10,8},{12,14},{14,12},{16,18},{18,... | collective-permute-start | bytes 1044488 | tf_op jit(solution)/shard_map/ppermute | solution.py:1191
  1040.9 19.9 %collective-permute-done.23.refs_10_.refs_12_ = bf16[2,832,256]{2,1,0:T(8,128)(2,1)} collective-permute-done((bf16[2,832,256]{2,1,0:T(8,128)(2,1)}, bf16[2,832,256]{2,1,0:T(8,128)(2,1)}, u32[]{:S(2)}, u32[]{:S(2)}) %collective-permute-start.23) | collective-permute-done | bytes 852000 | tf_op jit(solution)/shard_map/ppermute | solution.py:1268
  1060.9 4.4 collective-permute-done.21.refs_2_.refs_4_
  1065.9 4.6 split_sum.12
  1070.5 31.0 %collective-permute-start.40 = (bf16[1,832,256]{2,1,0:T(8,128)(2,1)}, bf16[1,832,256]{2,1,0:T(8,128)(2,1)}, u32[]{:S(2)}, u32[]{:S(2)}) collective-permute-start(bf16[1,832,256]{2,1,0:T(8,128)(2,1)} %get-tuple-element.236), channel_id=1, source_target_pairs={{0,24},{2,26},{4,28},{6,30},{8,16},{10,18},{12,20},{14,22},{16,8},... | collective-permute-start | bytes 1277960 | tf_op jit(solution)/shard_map/ppermute | solution.py:1268
  1107.1 8.4 split_sum.13
  1127.0 26.5 %collective-permute-start.36 = (f32[87040]{0:T(1024)S(1)}, f32[87040]{0:T(1024)S(1)}, u32[]{:S(2)}, u32[]{:S(2)}) collective-permute-start(f32[87040]{0:T(1024)S(1)} %add.95), channel_id=1, source_target_pairs={{0,16},{2,18},{4,20},{6,22},{8,24},{10,26},{12,28},{14,30},{16,0},... | collective-permute-start | bytes 1044488 | tf_op jit(solution)/shard_map/ppermute | solution.py:1191
  1156.8 20.4 %collective-permute-done.36 = f32[87040]{0:T(1024)S(1)} collective-permute-done((f32[87040]{0:T(1024)S(1)}, f32[87040]{0:T(1024)S(1)}, u32[]{:S(2)}, u32[]{:S(2)}) %collective-permute-start.36) | collective-permute-done | bytes 348192 | tf_op jit(solution)/shard_map/ppermute | solution.py:1191
  1180.6 5.1 split_sum.14
  1191.4 6.0 conditional.3
  1206.2 5.3 collective-permute-start.31
  1214.7 20.0 %collective-permute-done.31 = bf16[1,512,256]{2,1,0:T(8,128)(2,1)S(1)} collective-permute-done((bf16[1,512,256]{2,1,0:T(8,128)(2,1)}, bf16[1,512,256]{2,1,0:T(8,128)(2,1)S(1)}, u32[]{:S(2)}, u32[]{:S(2)}) %collective-permute-start.31) | collective-permute-done | bytes 262176 | tf_op jit(solution)/shard_map/ppermute | solution.py:1268
  1235.7 4.6 collective-permute-done.32
  1250.4 4.6 fusion
  (180 shorter events, 103.0 us)
Async XLA Ops:
  0.7 140.3 %collective-permute-start = (bf16[4,288,1024]{2,1,0:T(8,128)(2,1)}, bf16[4,288,1024]{2,1,0:T(8,128)(2,1)}, u32[]{:S(2)}, u32[]{:S(2)}) collective-permute-start(bf16[4,288,1024]{2,1,0:T(8,128)(2,1)} %refs_1_.1), channel_id=1, source_target_pairs={{0,1},{1,0},{2,3},{3,2},{4,5},{5,4},{6,7},{7,6},{8,9},{9,8},{10,11... | collective-permute-start | bytes 7077896 | tf_op jit(solution)/shard_map/ppermute | solution.py:1411
  5.2 73.1 %collective-permute-start.2 = (bf16[4,3,32,1536]{3,2,1,0:T(8,128)(2,1)}, bf16[4,3,32,1536]{3,2,1,0:T(8,128)(2,1)S(1)}, u32[]{:S(2)}, u32[]{:S(2)}) collective-permute-start(bf16[4,3,32,1536]{3,2,1,0:T(8,128)(2,1)} %get-tuple-element.244), channel_id=1, source_target_pairs={{1,0},{3,2},{5,4},{7,6},{9,8},{11,10},{13,12},{15,14},{17,16},{19,... | collective-permute-start | bytes 3538952 | tf_op jit(solution)/shard_map/ppermute | solution.py:1154
  6.5 71.9 %collective-permute-start.1 = (bf16[4,3,32,1536]{3,2,1,0:T(8,128)(2,1)}, bf16[4,3,32,1536]{3,2,1,0:T(8,128)(2,1)}, u32[]{:S(2)}, u32[]{:S(2)}) collective-permute-start(bf16[4,3,32,1536]{3,2,1,0:T(8,128)(2,1)} %get-tuple-element.245), channel_id=1, source_target_pairs={{0,1},{2,3},{4,5},{6,7},{8,9},{10,11},{12,13},{14,15},{16,17},{18,... | collective-permute-start | bytes 3538952 | tf_op jit(solution)/shard_map/ppermute | solution.py:1153
  136.6 36.4 %collective-permute-start.3 = (bf16[4,24,1536]{2,1,0:T(8,128)(2,1)}, bf16[4,24,1536]{2,1,0:T(8,128)(2,1)S(1)}, u32[]{:S(2)}, u32[]{:S(2)}) collective-permute-start(bf16[4,24,1536]{2,1,0:T(8,128)(2,1)} %get-tuple-element.147), channel_id=1, source_target_pairs={{0,1},{2,3},{4,5},{6,7},{8,9},{10,11},{12,13},{14,15},{16,17},{18,... | collective-permute-start | bytes 884744 | tf_op jit(solution)/shard_map/ppermute | solution.py:1153
  138.8 34.2 %collective-permute-start.4 = (bf16[4,24,1536]{2,1,0:T(8,128)(2,1)}, bf16[4,24,1536]{2,1,0:T(8,128)(2,1)S(1)}, u32[]{:S(2)}, u32[]{:S(2)}) collective-permute-start(bf16[4,24,1536]{2,1,0:T(8,128)(2,1)} %get-tuple-element.148), channel_id=1, source_target_pairs={{1,0},{3,2},{5,4},{7,6},{9,8},{11,10},{13,12},{15,14},{17,16},{19,... | collective-permute-start | bytes 884744 | tf_op jit(solution)/shard_map/ppermute | solution.py:1154
  185.7 7.7 collective-permute-start.5
  189.7 7.5 collective-permute-start.6
  317.3 223.6 %collective-permute-start.7 = (bf16[16,2496,256]{2,1,0:T(8,128)(2,1)}, bf16[16,2496,256]{2,1,0:T(8,128)(2,1)}, u32[]{:S(2)}, u32[]{:S(2)}) collective-permute-start(bf16[16,2496,256]{2,1,0:T(8,128)(2,1)} %get-tuple-element.171), channel_id=1, source_target_pairs={{0,2},{2,0},{4,6},{6,4},{8,10},{10,8},{12,14},{14,12},{16,18},{18,... | collective-permute-start | bytes 61341704 | tf_op jit(solution)/shard_map/ppermute | solution.py:1268
  562.2 179.3 %collective-permute-start.9 = (bf16[8,832,256]{2,1,0:T(8,128)(2,1)}, bf16[8,832,256]{2,1,0:T(8,128)(2,1)S(1)}, u32[]{:S(2)}, u32[]{:S(2)}) collective-permute-start(bf16[8,832,256]{2,1,0:T(8,128)(2,1)} %get-tuple-element.181), channel_id=1, source_target_pairs={{0,4},{2,6},{4,0},{6,2},{8,12},{10,14},{12,8},{14,10},{16,20},{18,... | collective-permute-start | bytes 10223624 | tf_op jit(solution)/shard_map/ppermute | solution.py:1268
  562.3 200.1 %collective-permute-start.10 = (bf16[8,832,256]{2,1,0:T(8,128)(2,1)}, bf16[8,832,256]{2,1,0:T(8,128)(2,1)}, u32[]{:S(2)}, u32[]{:S(2)}) collective-permute-start(bf16[8,832,256]{2,1,0:T(8,128)(2,1)} %get-tuple-element.183), channel_id=1, source_target_pairs={{0,8},{2,10},{4,12},{6,14},{8,0},{10,2},{12,4},{14,6},{16,24},{18,... | collective-permute-start | bytes 10223624 | tf_op jit(solution)/shard_map/ppermute | solution.py:1268
  711.5 51.8 %collective-permute-start.8 = (bf16[8,832,256]{2,1,0:T(8,128)(2,1)}, bf16[8,832,256]{2,1,0:T(8,128)(2,1)}, u32[]{:S(2)}, u32[]{:S(2)}) collective-permute-start(bf16[8,832,256]{2,1,0:T(8,128)(2,1)} %get-tuple-element.172.refs_9_), channel_id=1, source_target_pairs={{0,1},{1,0},{2,3},{3,2},{4,5},{5,4},{6,7},{7,6},{8,9},{9,8},{10,11... | collective-permute-start | bytes 10223624 | tf_op jit(solution)/shard_map/ppermute | solution.py:1268
  793.9 179.1 %collective-permute-start.12 = (bf16[16,1536,256]{2,1,0:T(8,128)(2,1)}, bf16[16,1536,256]{2,1,0:T(8,128)(2,1)}, u32[]{:S(2)}, u32[]{:S(2)}) collective-permute-start(bf16[16,1536,256]{2,1,0:T(8,128)(2,1)} %get-tuple-element.188), channel_id=1, source_target_pairs={{0,2},{2,0},{4,6},{6,4},{8,10},{10,8},{12,14},{14,12},{16,18},{18,... | collective-permute-start | bytes 37748744 | tf_op jit(solution)/shard_map/ppermute | solution.py:1268
  845.3 29.5 %collective-permute-start.17 = (bf16[4,3,32,1536]{3,2,1,0:T(8,128)(2,1)S(1)}, bf16[4,3,32,1536]{3,2,1,0:T(8,128)(2,1)S(1)}, u32[]{:S(2)}, u32[]{:S(2)}) collective-permute-start(bf16[4,3,32,1536]{3,2,1,0:T(8,128)(2,1)S(1)} %get-tuple-element.242), channel_id=1, source_target_pairs={{1,0},{3,2},{5,4},{7,6},{9,8},{11,10},{13,12},{15,14},{17,16},{19,... | collective-permute-start | bytes 3538952 | tf_op jit(solution)/shard_map/ppermute | solution.py:1154
  846.6 29.2 %collective-permute-start.16 = (bf16[4,3,32,1536]{3,2,1,0:T(8,128)(2,1)S(1)}, bf16[4,3,32,1536]{3,2,1,0:T(8,128)(2,1)}, u32[]{:S(2)}, u32[]{:S(2)}) collective-permute-start(bf16[4,3,32,1536]{3,2,1,0:T(8,128)(2,1)S(1)} %get-tuple-element.243), channel_id=1, source_target_pairs={{0,1},{2,3},{4,5},{6,7},{8,9},{10,11},{12,13},{14,15},{16,17},{18,... | collective-permute-start | bytes 3538952 | tf_op jit(solution)/shard_map/ppermute | solution.py:1153
  855.8 132.4 %collective-permute-start.11 = (bf16[4,288,1024]{2,1,0:T(8,128)(2,1)}, bf16[4,288,1024]{2,1,0:T(8,128)(2,1)}, u32[]{:S(2)}, u32[]{:S(2)}) collective-permute-start(bf16[4,288,1024]{2,1,0:T(8,128)(2,1)} %slice.152), channel_id=1, source_target_pairs={{0,1},{1,0},{2,3},{3,2},{4,5},{5,4},{6,7},{7,6},{8,9},{9,8},{10,11... | collective-permute-start | bytes 7077896 | tf_op jit(solution)/shard_map/ppermute | solution.py:1411
  855.8 61.3 %collective-permute-start.14 = (bf16[4,832,256]{2,1,0:T(8,128)(2,1)}, bf16[4,832,256]{2,1,0:T(8,128)(2,1)S(1)}, u32[]{:S(2)}, u32[]{:S(2)}) collective-permute-start(bf16[4,832,256]{2,1,0:T(8,128)(2,1)} %get-tuple-element.191), channel_id=1, source_target_pairs={{0,8},{2,10},{4,12},{6,14},{8,0},{10,2},{12,4},{14,6},{16,24},{18,... | collective-permute-start | bytes 5111816 | tf_op jit(solution)/shard_map/ppermute | solution.py:1268
  875.8 87.1 %collective-permute-start.15 = (bf16[4,832,256]{2,1,0:T(8,128)(2,1)}, bf16[4,832,256]{2,1,0:T(8,128)(2,1)S(1)}, u32[]{:S(2)}, u32[]{:S(2)}) collective-permute-start(bf16[4,832,256]{2,1,0:T(8,128)(2,1)} %get-tuple-element.193), channel_id=1, source_target_pairs={{0,1},{1,0},{2,3},{3,2},{4,5},{5,4},{6,7},{7,6},{8,9},{9,8},{10,11... | collective-permute-start | bytes 5111816 | tf_op jit(solution)/shard_map/ppermute | solution.py:1268
  875.8 87.1 %collective-permute-start.13 = (bf16[4,832,256]{2,1,0:T(8,128)(2,1)}, bf16[4,832,256]{2,1,0:T(8,128)(2,1)}, u32[]{:S(2)}, u32[]{:S(2)}) collective-permute-start(bf16[4,832,256]{2,1,0:T(8,128)(2,1)} %get-tuple-element.184.refs_8_), channel_id=1, source_target_pairs={{0,4},{2,6},{4,0},{6,2},{8,12},{10,14},{12,8},{14,10},{16,20},{18,... | collective-permute-start | bytes 5111816 | tf_op jit(solution)/shard_map/ppermute | solution.py:1268
  917.1 45.8 %copy-start.5 = (bf16[4,832,256]{2,1,0:T(8,128)(2,1)}, bf16[4,832,256]{2,1,0:T(8,128)(2,1)S(1)}, u32[]{:S(2)}) copy-start(bf16[4,832,256]{2,1,0:T(8,128)(2,1)S(1)} %collective-permute-done.14.refs_6_.refs_8_) | copy-start | bytes 5111812
  970.9 68.7 %collective-permute-start.22 = (bf16[2,832,256]{2,1,0:T(8,128)(2,1)}, bf16[2,832,256]{2,1,0:T(8,128)(2,1)S(1)}, u32[]{:S(2)}, u32[]{:S(2)}) collective-permute-start(bf16[2,832,256]{2,1,0:T(8,128)(2,1)} %get-tuple-element.206), channel_id=1, source_target_pairs={{0,1},{1,0},{2,3},{3,2},{4,5},{5,4},{6,7},{7,6},{8,9},{9,8},{10,11... | collective-permute-start | bytes 2555912 | tf_op jit(solution)/shard_map/ppermute | solution.py:1268
  988.0 117.7 %collective-permute-start.18 = (bf16[8,512,256]{2,1,0:T(8,128)(2,1)}, bf16[8,512,256]{2,1,0:T(8,128)(2,1)S(1)}, u32[]{:S(2)}, u32[]{:S(2)}) collective-permute-start(bf16[8,512,256]{2,1,0:T(8,128)(2,1)} %get-tuple-element.197.refs_6_), channel_id=1, source_target_pairs={{0,1},{1,0},{2,3},{3,2},{4,5},{5,4},{6,7},{7,6},{8,9},{9,8},{10,11... | collective-permute-start | bytes 6291464 | tf_op jit(solution)/shard_map/ppermute | solution.py:1268
  988.1 31.8 %copy-start.13 = (f32[75264]{0:T(1024)S(1)}, f32[75264]{0:T(1024)}, u32[]{:S(2)}) copy-start(f32[75264]{0:T(1024)} %reshape.253) | copy-start | bytes 903172
  994.8 110.9 %collective-permute-start.19 = (bf16[8,512,256]{2,1,0:T(8,128)(2,1)}, bf16[8,512,256]{2,1,0:T(8,128)(2,1)}, u32[]{:S(2)}, u32[]{:S(2)}) collective-permute-start(bf16[8,512,256]{2,1,0:T(8,128)(2,1)} %get-tuple-element.201), channel_id=1, source_target_pairs={{0,4},{2,6},{4,0},{6,2},{8,12},{10,14},{12,8},{14,10},{16,20},{18,... | collective-permute-start | bytes 6291464 | tf_op jit(solution)/shard_map/ppermute | solution.py:1268
  994.9 110.9 %collective-permute-start.20 = (bf16[8,512,256]{2,1,0:T(8,128)(2,1)}, bf16[8,512,256]{2,1,0:T(8,128)(2,1)}, u32[]{:S(2)}, u32[]{:S(2)}) collective-permute-start(bf16[8,512,256]{2,1,0:T(8,128)(2,1)} %get-tuple-element.203), channel_id=1, source_target_pairs={{0,8},{2,10},{4,12},{6,14},{8,0},{10,2},{12,4},{14,6},{16,24},{18,... | collective-permute-start | bytes 6291464 | tf_op jit(solution)/shard_map/ppermute | solution.py:1268
  1020.1 20.8 %collective-permute-start.33 = (f32[87040]{0:T(1024)S(1)}, f32[87040]{0:T(1024)S(1)}, u32[]{:S(2)}, u32[]{:S(2)}) collective-permute-start(f32[87040]{0:T(1024)S(1)} %constant_dynamic-update-slice_fusion), channel_id=1, source_target_pairs={{0,2},{2,0},{4,6},{6,4},{8,10},{10,8},{12,14},{14,12},{16,18},{18,... | collective-permute-start | bytes 1044488 | tf_op jit(solution)/shard_map/ppermute | solution.py:1191
  1039.6 26.3 %copy-start.10 = (bf16[2,832,256]{2,1,0:T(8,128)(2,1)}, bf16[2,832,256]{2,1,0:T(8,128)(2,1)S(1)}, u32[]{:S(2)}) copy-start(bf16[2,832,256]{2,1,0:T(8,128)(2,1)S(1)} %collective-permute-done.22.refs_6_.refs_8_) | copy-start | bytes 2555908
  1039.6 21.2 %collective-permute-start.23 = (bf16[2,832,256]{2,1,0:T(8,128)(2,1)}, bf16[2,832,256]{2,1,0:T(8,128)(2,1)}, u32[]{:S(2)}, u32[]{:S(2)}) collective-permute-start(bf16[2,832,256]{2,1,0:T(8,128)(2,1)} %get-tuple-element.208), channel_id=1, source_target_pairs={{0,4},{2,6},{4,0},{6,2},{8,12},{10,14},{12,8},{14,10},{16,20},{18,... | collective-permute-start | bytes 2555912 | tf_op jit(solution)/shard_map/ppermute | solution.py:1268
  1040.8 24.5 %collective-permute-start.21 = (bf16[2,832,256]{2,1,0:T(8,128)(2,1)}, bf16[2,832,256]{2,1,0:T(8,128)(2,1)}, u32[]{:S(2)}, u32[]{:S(2)}) collective-permute-start(bf16[2,832,256]{2,1,0:T(8,128)(2,1)} %get-tuple-element.196.refs_13_), channel_id=1, source_target_pairs={{0,8},{2,10},{4,12},{6,14},{8,0},{10,2},{12,4},{14,6},{16,24},{18,... | collective-permute-start | bytes 2555912 | tf_op jit(solution)/shard_map/ppermute | solution.py:1268
  1060.8 40.8 %collective-permute-start.34 = (f32[87040]{0:T(1024)S(1)}, f32[87040]{0:T(1024)}, u32[]{:S(2)}, u32[]{:S(2)}) collective-permute-start(f32[87040]{0:T(1024)S(1)} %add.93), channel_id=1, source_target_pairs={{0,4},{2,6},{4,0},{6,2},{8,12},{10,14},{12,8},{14,10},{16,20},{18,... | collective-permute-start | bytes 1044488 | tf_op jit(solution)/shard_map/ppermute | solution.py:1191
  1070.5 48.9 %collective-permute-start.40 = (bf16[1,832,256]{2,1,0:T(8,128)(2,1)}, bf16[1,832,256]{2,1,0:T(8,128)(2,1)}, u32[]{:S(2)}, u32[]{:S(2)}) collective-permute-start(bf16[1,832,256]{2,1,0:T(8,128)(2,1)} %get-tuple-element.236), channel_id=1, source_target_pairs={{0,24},{2,26},{4,28},{6,30},{8,16},{10,18},{12,20},{14,22},{16,8},... | collective-permute-start | bytes 1277960 | tf_op jit(solution)/shard_map/ppermute | solution.py:1268
  1102.6 18.1 %collective-permute-start.35 = (f32[87040]{0:T(1024)S(1)}, f32[87040]{0:T(1024)}, u32[]{:S(2)}, u32[]{:S(2)}) collective-permute-start(f32[87040]{0:T(1024)S(1)} %add.94), channel_id=1, source_target_pairs={{0,8},{2,10},{4,12},{6,14},{8,0},{10,2},{12,4},{14,6},{16,24},{18,... | collective-permute-start | bytes 1044488 | tf_op jit(solution)/shard_map/ppermute | solution.py:1191
  1115.5 63.7 %collective-permute-start.24 = (bf16[4,512,256]{2,1,0:T(8,128)(2,1)}, bf16[4,512,256]{2,1,0:T(8,128)(2,1)S(1)}, u32[]{:S(2)}, u32[]{:S(2)}) collective-permute-start(bf16[4,512,256]{2,1,0:T(8,128)(2,1)} %get-tuple-element.211), channel_id=1, source_target_pairs={{0,4},{2,6},{4,0},{6,2},{8,12},{10,14},{12,8},{14,10},{16,20},{18,... | collective-permute-start | bytes 3145736 | tf_op jit(solution)/shard_map/ppermute | solution.py:1268
  1118.3 61.0 %collective-permute-start.25 = (bf16[4,512,256]{2,1,0:T(8,128)(2,1)}, bf16[4,512,256]{2,1,0:T(8,128)(2,1)S(1)}, u32[]{:S(2)}, u32[]{:S(2)}) collective-permute-start(bf16[4,512,256]{2,1,0:T(8,128)(2,1)} %get-tuple-element.213), channel_id=1, source_target_pairs={{0,8},{2,10},{4,12},{6,14},{8,0},{10,2},{12,4},{14,6},{16,24},{18,... | collective-permute-start | bytes 3145736 | tf_op jit(solution)/shard_map/ppermute | solution.py:1268
  1118.3 61.0 %collective-permute-start.26 = (bf16[4,512,256]{2,1,0:T(8,128)(2,1)}, bf16[4,512,256]{2,1,0:T(8,128)(2,1)}, u32[]{:S(2)}, u32[]{:S(2)}) collective-permute-start(bf16[4,512,256]{2,1,0:T(8,128)(2,1)} %get-tuple-element.215), channel_id=1, source_target_pairs={{0,1},{1,0},{2,3},{3,2},{4,5},{5,4},{6,7},{7,6},{8,9},{9,8},{10,11... | collective-permute-start | bytes 3145736 | tf_op jit(solution)/shard_map/ppermute | solution.py:1268
  1119.4 7.6 collective-permute-start.41
  1120.7 34.1 %collective-permute-start.39 = (bf16[1,832,256]{2,1,0:T(8,128)(2,1)}, bf16[1,832,256]{2,1,0:T(8,128)(2,1)S(1)}, u32[]{:S(2)}, u32[]{:S(2)}) collective-permute-start(bf16[1,832,256]{2,1,0:T(8,128)(2,1)} %get-tuple-element.209.refs_13_), channel_id=1, source_target_pairs={{0,24},{2,26},{4,28},{6,30},{8,16},{10,18},{12,20},{14,22},{16,8},... | collective-permute-start | bytes 1277960 | tf_op jit(solution)/shard_map/ppermute | solution.py:1268
  1127.0 26.5 %copy-start.16 = (bf16[1,832,256]{2,1,0:T(8,128)(2,1)}, bf16[1,832,256]{2,1,0:T(8,128)(2,1)S(1)}, u32[]{:S(2)}) copy-start(bf16[1,832,256]{2,1,0:T(8,128)(2,1)S(1)} %collective-permute-done.41) | copy-start | bytes 1277956
  1127.0 50.2 %collective-permute-start.36 = (f32[87040]{0:T(1024)S(1)}, f32[87040]{0:T(1024)S(1)}, u32[]{:S(2)}, u32[]{:S(2)}) collective-permute-start(f32[87040]{0:T(1024)S(1)} %add.95), channel_id=1, source_target_pairs={{0,16},{2,18},{4,20},{6,22},{8,24},{10,26},{12,28},{14,30},{16,0},... | collective-permute-start | bytes 1044488 | tf_op jit(solution)/shard_map/ppermute | solution.py:1191
  1178.1 23.2 %collective-permute-start.37 = (f32[87040]{0:T(1024)}, f32[87040]{0:T(1024)}, u32[]{:S(2)}, u32[]{:S(2)}) collective-permute-start(f32[87040]{0:T(1024)} %add.96), channel_id=1, source_target_pairs={{0,1},{1,0},{2,3},{3,2},{4,5},{5,4},{6,7},{7,6},{8,9},{9,8},{10,11... | collective-permute-start | bytes 1044488 | tf_op jit(solution)/shard_map/ppermute | solution.py:1191
  1185.7 16.8 %collective-permute-start.27 = (bf16[2,512,256]{2,1,0:T(8,128)(2,1)}, bf16[2,512,256]{2,1,0:T(8,128)(2,1)}, u32[]{:S(2)}, u32[]{:S(2)}) collective-permute-start(bf16[2,512,256]{2,1,0:T(8,128)(2,1)} %get-tuple-element.217), channel_id=1, source_target_pairs={{0,8},{2,10},{4,12},{6,14},{8,0},{10,2},{12,4},{14,6},{16,24},{18,... | collective-permute-start | bytes 1572872 | tf_op jit(solution)/shard_map/ppermute | solution.py:1268
  1186.7 15.7 %collective-permute-start.28 = (bf16[2,512,256]{2,1,0:T(8,128)(2,1)}, bf16[2,512,256]{2,1,0:T(8,128)(2,1)}, u32[]{:S(2)}, u32[]{:S(2)}) collective-permute-start(bf16[2,512,256]{2,1,0:T(8,128)(2,1)} %get-tuple-element.219), channel_id=1, source_target_pairs={{0,1},{1,0},{2,3},{3,2},{4,5},{5,4},{6,7},{7,6},{8,9},{9,8},{10,11... | collective-permute-start | bytes 1572872 | tf_op jit(solution)/shard_map/ppermute | solution.py:1268
  1187.0 15.4 %collective-permute-start.29 = (bf16[2,512,256]{2,1,0:T(8,128)(2,1)}, bf16[2,512,256]{2,1,0:T(8,128)(2,1)}, u32[]{:S(2)}, u32[]{:S(2)}) collective-permute-start(bf16[2,512,256]{2,1,0:T(8,128)(2,1)} %get-tuple-element.221), channel_id=1, source_target_pairs={{0,4},{2,6},{4,0},{6,2},{8,12},{10,14},{12,8},{14,10},{16,20},{18,... | collective-permute-start | bytes 1572872 | tf_op jit(solution)/shard_map/ppermute | solution.py:1268
  1198.1 13.5 %collective-permute-start.42 = (bf16[82944]{0:T(1024)(128)(2,1)}, bf16[82944]{0:T(1024)(128)(2,1)}, u32[]{:S(2)}, u32[]{:S(2)}) collective-permute-start(bf16[82944]{0:T(1024)(128)(2,1)} %slice.153), channel_id=1, source_target_pairs={{1,0},{2,1},{3,2},{4,3},{5,4},{6,5},{7,6},{8,7},{9,8},{10,9},{11,1... | collective-permute-start | bytes 497672 | tf_op jit(solution)/shard_map/ppermute | solution.py:1363
  1206.2 39.3 %copy-start.19 = (bf16[1,512,256]{2,1,0:T(8,128)(2,1)S(1)}, bf16[1,512,256]{2,1,0:T(8,128)(2,1)}, u32[]{:S(2)}) copy-start(bf16[1,512,256]{2,1,0:T(8,128)(2,1)} %get-tuple-element.222) | copy-start | bytes 786436
  1206.2 28.5 %collective-permute-start.31 = (bf16[1,512,256]{2,1,0:T(8,128)(2,1)}, bf16[1,512,256]{2,1,0:T(8,128)(2,1)S(1)}, u32[]{:S(2)}, u32[]{:S(2)}) collective-permute-start(bf16[1,512,256]{2,1,0:T(8,128)(2,1)} %get-tuple-element.225), channel_id=1, source_target_pairs={{0,24},{2,26},{4,28},{6,30},{8,16},{10,18},{12,20},{14,22},{16,8},... | collective-permute-start | bytes 786440 | tf_op jit(solution)/shard_map/ppermute | solution.py:1268
  1211.5 28.8 %collective-permute-start.32 = (bf16[1,512,256]{2,1,0:T(8,128)(2,1)}, bf16[1,512,256]{2,1,0:T(8,128)(2,1)S(1)}, u32[]{:S(2)}, u32[]{:S(2)}) collective-permute-start(bf16[1,512,256]{2,1,0:T(8,128)(2,1)} %get-tuple-element.227), channel_id=1, source_target_pairs={{0,24},{2,26},{4,28},{6,30},{8,16},{10,18},{12,20},{14,22},{16,8},... | collective-permute-start | bytes 786440 | tf_op jit(solution)/shard_map/ppermute | solution.py:1268
  1213.3 32.1 %collective-permute-start.30 = (bf16[1,512,256]{2,1,0:T(8,128)(2,1)}, bf16[1,512,256]{2,1,0:T(8,128)(2,1)S(1)}, u32[]{:S(2)}, u32[]{:S(2)}) collective-permute-start(bf16[1,512,256]{2,1,0:T(8,128)(2,1)} %get-tuple-element.223), channel_id=1, source_target_pairs={{0,24},{2,26},{4,28},{6,30},{8,16},{10,18},{12,20},{14,22},{16,8},... | collective-permute-start | bytes 786440 | tf_op jit(solution)/shard_map/ppermute | solution.py:1268
  1248.5 6.5 collective-permute-start.38
  (18 other events, 134.1 us)
